TPU v7x, 32 devices: a whole 2x2x4 slice. The times are simulated.
32 devices in a mesh: expert: 8 (over z, y), shard: 4 (over x, core).
Axes of the slice: x: 2, y: 2, z: 4, core: 2. Of those that a mesh axis runs over, the one named last changes fastest.
Arguments:
- tokens: bfloat16 [4096, 2048], P(('expert', 'shard')), may hold values from -6 to 6
- segments: int32 [4096], P('expert'), may hold values from 0 to 8, as said below
- routes: int32 [4096, 6], P(('expert', 'shard')), may hold values from 0 to 15, all different within a row; in each aligned block of 128 rows (0 to 127, 128 to 255, ...) at most 96 rows name the same one
- cotangent: bfloat16 [4096, 2048], P(('expert', 'shard')), may hold values from -6 to 6
- attn_gain: bfloat16 [2048], P('expert'), may hold values from 0.5 to 1.5
- w_query: bfloat16 [2048, 3072], P('expert', 'shard'), may hold values from -0.125 to 0.125
- w_latent: bfloat16 [2048, 576], P('expert'), may hold values from -0.125 to 0.125
- latent_gain: bfloat16 [512], P('expert'), may hold values from 0.5 to 1.5
- w_expand: bfloat16 [512, 4096], P('expert', 'shard'), may hold values from -0.25 to 0.25
- w_output: bfloat16 [2048, 2048], P('shard', 'expert'), may hold values from -0.5 to 0.5
- ffn_gain: bfloat16 [2048], P('expert'), may hold values from 0.5 to 1.5
- w_router: bfloat16 [2048, 16], P('expert'), may hold values from -0.0625 to 0.0625
- w_shared_gate: bfloat16 [2048, 2816], P('expert', 'shard'), may hold values from -0.125 to 0.125
- w_shared_up: bfloat16 [2048, 2816], P('expert', 'shard'), may hold values from -0.125 to 0.125
- w_shared_down: bfloat16 [2816, 2048], P('shard', 'expert'), may hold values from -0.21875 to 0.21875
- w_expert_gate: bfloat16 [16, 2048, 1408], P('expert', None, 'shard'), may hold values from -0.125 to 0.125
- w_expert_up: bfloat16 [16, 2048, 1408], P('expert', None, 'shard'), may hold values from -0.125 to 0.125
- w_expert_down: bfloat16 [16, 1408, 2048], P('expert', 'shard'), may hold values from -0.3125 to 0.3125
Outputs:
- block_out: bfloat16 [4096, 2048], P(('expert', 'shard'))
- tokens_grad: float32 [4096, 2048], P(('expert', 'shard'))
- grad_attn_gain: float32 [2048], P('expert')
- grad_w_query: float32 [2048, 3072], P('expert', 'shard')
- grad_w_latent: float32 [2048, 576], P('expert')
- grad_latent_gain: float32 [512], P('expert')
- grad_w_expand: float32 [512, 4096], P('expert', 'shard')
- grad_w_output: float32 [2048, 2048], P('shard', 'expert')
- grad_ffn_gain: float32 [2048], P('expert')
- grad_w_router: float32 [2048, 16], P('expert')
- grad_w_shared_gate: float32 [2048, 2816], P('expert', 'shard')
- grad_w_shared_up: float32 [2048, 2816], P('expert', 'shard')
- grad_w_shared_down: float32 [2816, 2048], P('shard', 'expert')
- grad_w_expert_gate: float32 [16, 2048, 1408], P('expert', None, 'shard')
- grad_w_expert_up: float32 [16, 2048, 1408], P('expert', None, 'shard')
- grad_w_expert_down: float32 [16, 1408, 2048], P('expert', 'shard')
Inputs may be any that keep to these rules, and one draw needn't show every extreme that they name: `routes`: each row names 6 different experts. Among the rows of one device (128 aligned rows) no expert is named more than 96 times, and in every draw some expert is named exactly 96 times. `segments`: in each aligned group of 512 tokens the ids are 0 over a leading prompt of 192 to 320 tokens, then rise by one at each new continuation up to 8 at the group's end; each continuation has one token or more.
All inputs are finite; a program needn't handle non-finite values.
Results may differ from a plain program's by a relative error of at most 0.024.
Values may be sent and summed in bfloat16 or wider, within the bound.
No kernel may reach another device: no remote copies, remote signals or barrier semaphores. Data moves between devices by JAX's collectives and lax.ppermute only.
A program may use at most 512 MiB of HBM per device.

v0:
```python
import jax
import jax.numpy as jnp
from jax import lax
from jax.sharding import PartitionSpec as P

NOPE = 128
ROPE = 64
V_HEAD = 128
KV_RANK = 512
TOP = 6


epsilon = 1e-06


def rotate(values, cosine, sine):
    half_width = values.shape[-1] // 2
    first_half = values[..., :half_width]
    second_half = values[..., half_width:]
    return jnp.concatenate(
        [first_half * cosine - second_half * sine, second_half * cosine + first_half * sine],
        axis=-1,
    )


def angles(places, width):
    half_width = width // 2
    spacing = 10000.0 ** (-2.0 * jnp.arange(half_width, dtype=jnp.float32) / width)
    turned = places.astype(jnp.float32)[:, None] * spacing[None, :]
    return (jnp.cos(turned), jnp.sin(turned))


def positions(segment):
    indices = jnp.arange(segment.shape[0], dtype=jnp.int32)
    prompt_len = jnp.sum((segment == 0).astype(jnp.int32))
    earlier = jnp.sum((segment[None, :] < segment[:, None]).astype(jnp.int32), axis=1)
    return jnp.where(segment == 0, indices, prompt_len + indices - earlier)


def inverse_rms(values):
    return lax.rsqrt(jnp.mean(values * values, axis=-1, keepdims=True) + epsilon)


def norm_back(values, scaling, gain, incoming):
    weighted = incoming * gain
    inner = jnp.mean(weighted * values, axis=-1, keepdims=True)
    return (
        scaling * weighted - values * scaling**3 * inner,
        jnp.sum(incoming * values * scaling, axis=0),
    )


def silu_slope(values):
    logistic = jax.nn.sigmoid(values)
    return logistic * (1.0 + values * (1.0 - logistic))


def send_experts(values):
    return lax.all_to_all(values, "expert", split_axis=0, concat_axis=0, tiled=True)


def send_tokens(values):
    return lax.all_to_all(values, "expert", split_axis=0, concat_axis=0, tiled=True)


def spread_expert_rows(values):
    return lax.all_gather(values[None], "shard", axis=0, tiled=True)


def expert_total(values):
    return lax.psum_scatter(
        values.astype(jnp.bfloat16), "shard", scatter_dimension=0, tiled=True
    ).astype(jnp.float32)[0]


def body(
    tokens,
    segments,
    routes,
    cotangent,
    attn_gain,
    w_query,
    w_latent,
    latent_gain,
    w_expand,
    w_output,
    ffn_gain,
    w_router,
    w_shared_gate,
    w_shared_up,
    w_shared_down,
    w_expert_gate,
    w_expert_up,
    w_expert_down,
):

    def fetch_mixer():
        parted = (
            lax.all_gather(attn_gain, "expert", axis=0, tiled=True),
            lax.all_gather(w_query, "expert", axis=0, tiled=True),
            lax.all_gather(w_latent, "expert", axis=0, tiled=True),
            lax.all_gather(latent_gain, "expert", axis=0, tiled=True),
            lax.all_gather(w_expand, "expert", axis=0, tiled=True),
            lax.all_gather(w_output, "expert", axis=1, tiled=True),
            lax.all_gather(ffn_gain, "expert", axis=0, tiled=True),
            lax.all_gather(w_router, "expert", axis=0, tiled=True),
            lax.all_gather(w_shared_gate, "expert", axis=0, tiled=True),
            lax.all_gather(w_shared_up, "expert", axis=0, tiled=True),
            lax.all_gather(w_shared_down, "expert", axis=1, tiled=True),
        )
        columns = (
            lax.all_gather(parted[1], "shard", axis=1, tiled=True),
            lax.all_gather(parted[4], "shard", axis=1, tiled=True),
            lax.all_gather(parted[5], "shard", axis=0, tiled=True),
            lax.all_gather(parted[8], "shard", axis=1, tiled=True),
            lax.all_gather(parted[9], "shard", axis=1, tiled=True),
            lax.all_gather(parted[10], "shard", axis=0, tiled=True),
        )
        parted = (
            parted[0],
            columns[0],
            parted[2],
            parted[3],
            columns[1],
            columns[2],
            parted[6],
            parted[7],
            columns[3],
            columns[4],
            columns[5],
        )
        return parted

    float_type = jnp.float32
    low_type = jnp.bfloat16
    own_rows = tokens.shape[0]
    offset = lax.axis_index("shard") * own_rows
    group_len = segments.shape[0]
    experts = w_router.shape[1]
    capacity = 2 * own_rows * TOP // experts
    local_experts = w_expert_gate.shape[0]
    peer_count = lax.axis_size("expert")
    score_scale = (NOPE + ROPE) ** (-0.5)
    gathered = fetch_mixer()
    (
        gain_attn,
        query_full,
        latent_full,
        gain_latent,
        expand_full,
        output_full,
        gain_ffn,
        router_full,
        gate_shared,
        up_shared,
        down_shared,
    ) = gathered
    heads_dev = query_full.shape[1] // (NOPE + ROPE)
    token_float = tokens.astype(float_type)
    scale_attn = inverse_rms(token_float)
    normed_in = (token_float * scale_attn * gain_attn.astype(float_type)).astype(low_type)
    places = positions(segments)
    cos_group, sin_group = angles(places, ROPE)
    cos_own = lax.dynamic_slice_in_dim(cos_group, offset, own_rows, 0)
    sin_own = lax.dynamic_slice_in_dim(sin_group, offset, own_rows, 0)
    segment_own = lax.dynamic_slice_in_dim(segments, offset, own_rows, 0)
    key_index = jnp.arange(group_len, dtype=jnp.int32)
    cos_query, sin_query = (cos_own, sin_own)
    query_index = offset + jnp.arange(own_rows, dtype=jnp.int32)
    latent_raw = jnp.dot(normed_in, latent_full, preferred_element_type=float_type)
    compressed = latent_raw[:, :KV_RANK]
    scale_latent = inverse_rms(compressed)
    latent_use = (compressed * scale_latent * gain_latent.astype(float_type)).astype(low_type)
    rope_key = rotate(latent_raw[:, KV_RANK:], cos_own, sin_own).astype(low_type)
    latent_group, rope_group = (
        lax.all_gather(latent_use, "shard", axis=0, tiled=True),
        lax.all_gather(rope_key, "shard", axis=0, tiled=True),
    )
    query_rows = normed_in.shape[0]
    query_raw = jnp.dot(normed_in, query_full, preferred_element_type=float_type).reshape(
        query_rows, heads_dev, NOPE + ROPE
    )
    query_use = jnp.concatenate(
        [
            query_raw[..., :NOPE],
            rotate(query_raw[..., NOPE:], cos_query[:, None, :], sin_query[:, None, :]),
        ],
        axis=-1,
    ).astype(low_type)
    expanded = (
        jnp.dot(latent_group, expand_full, preferred_element_type=float_type)
        .astype(low_type)
        .reshape(group_len, heads_dev, NOPE + V_HEAD)
    )
    key_nope = expanded[..., :NOPE]
    value_heads = expanded[..., NOPE:]
    allowed = (key_index[None, :] <= query_index[:, None]) & (
        (segments[None, :] == 0) | (segments[None, :] == segment_own[:, None])
    )

    def masked_scores():
        direct = jnp.einsum(
            "qhd,khd->hqk", query_use[..., :NOPE], key_nope, preferred_element_type=float_type
        )
        rotary = jnp.einsum(
            "qhd,kd->hqk", query_use[..., NOPE:], rope_group, preferred_element_type=float_type
        )
        return jnp.where(allowed[None], (direct + rotary) * score_scale, -1e30)

    scores = masked_scores()
    largest = jnp.max(scores, axis=-1, keepdims=True)
    log_total = largest + jnp.log(jnp.sum(jnp.exp(scores - largest), axis=-1, keepdims=True))
    soft_low = jnp.exp(scores - log_total).astype(low_type)
    attn_mixed = (
        jnp.einsum("hqk,khd->qhd", soft_low, value_heads, preferred_element_type=float_type)
        .astype(low_type)
        .reshape(query_rows, heads_dev * V_HEAD)
    )
    attn_term = jnp.dot(attn_mixed, output_full, preferred_element_type=float_type)
    hidden_one = token_float + attn_term
    scale_ffn = inverse_rms(hidden_one)
    normed_ffn = (hidden_one * scale_ffn * gain_ffn.astype(float_type)).astype(low_type)
    logits = jnp.dot(normed_ffn, router_full, preferred_element_type=float_type)
    picked = jnp.take_along_axis(logits, routes, axis=1)
    gates = jax.nn.softmax(picked, axis=-1)
    shared_gate = jnp.dot(normed_ffn, gate_shared, preferred_element_type=float_type)
    shared_upv = jnp.dot(normed_ffn, up_shared, preferred_element_type=float_type)
    shared_hidden = (jax.nn.silu(shared_gate) * shared_upv).astype(low_type)
    shared_out = jnp.dot(shared_hidden, down_shared, preferred_element_type=float_type)
    flat_routes = routes.reshape(-1)
    pair_count = flat_routes.shape[0]
    route_table = (flat_routes[:, None] == jnp.arange(experts, dtype=jnp.int32)[None, :]).astype(
        jnp.int32
    )
    route_rank = jnp.sum((jnp.cumsum(route_table, axis=0) - 1) * route_table, axis=1)
    slot_index = flat_routes * capacity + route_rank
    slot_owner = (
        jnp.full((experts * capacity,), pair_count, jnp.int32)
        .at[slot_index]
        .set(jnp.arange(pair_count, dtype=jnp.int32))
    )
    slot_filled = slot_owner < pair_count
    slot_pair = jnp.minimum(slot_owner, pair_count - 1)
    zero_low = jnp.zeros((), low_type)
    send_rows = jnp.where(slot_filled[:, None], normed_ffn[slot_pair // TOP], zero_low).reshape(
        peer_count, local_experts, capacity, -1
    )
    arrived = send_experts(send_rows)
    expert_rows = spread_expert_rows(arrived)
    expert_gate = jnp.einsum(
        "asjcd,jdf->asjcf", expert_rows, w_expert_gate, preferred_element_type=float_type
    )
    expert_upv = jnp.einsum(
        "asjcd,jdf->asjcf", expert_rows, w_expert_up, preferred_element_type=float_type
    )
    expert_hidden = (jax.nn.silu(expert_gate) * expert_upv).astype(low_type)
    partial_out = jnp.einsum(
        "asjcf,jfd->asjcd", expert_hidden, w_expert_down, preferred_element_type=float_type
    )
    expert_out = expert_total(partial_out).astype(low_type)
    returned = send_tokens(expert_out).reshape(experts * capacity, -1)
    pair_out = returned[slot_index].reshape(own_rows, TOP, -1).astype(float_type)
    routed = jnp.sum(gates[:, :, None] * pair_out, axis=1)
    block_out = (hidden_one + shared_out + routed).astype(low_type)
    backward_copy = fetch_mixer()
    (
        gain_attn,
        query_full,
        latent_full,
        gain_latent,
        expand_full,
        output_full,
        gain_ffn,
        router_full,
        gate_shared,
        up_shared,
        down_shared,
    ) = backward_copy
    grad_in = cotangent.astype(float_type)
    d_rows = (gates[:, :, None] * grad_in[:, None, :]).astype(low_type)
    d_gates = jnp.sum(grad_in[:, None, :] * pair_out, axis=-1)
    d_picked = gates * (d_gates - jnp.sum(gates * d_gates, axis=-1, keepdims=True))
    chosen_table = routes[:, :, None] == jnp.arange(experts, dtype=jnp.int32)[None, None, :]
    d_logits = jnp.sum(jnp.where(chosen_table, d_picked[:, :, None], 0.0), axis=1).astype(low_type)
    grad_router = jnp.einsum("td,te->de", normed_ffn, d_logits, preferred_element_type=float_type)
    d_normed_ffn = jnp.einsum("te,de->td", d_logits, router_full, preferred_element_type=float_type)
    d_send = jnp.where(
        slot_filled[:, None], d_rows.reshape(pair_count, -1)[slot_pair], zero_low
    ).reshape(peer_count, local_experts, capacity, -1)
    d_arrived = send_experts(d_send)
    d_gathered = spread_expert_rows(d_arrived)
    grad_expert_down = jnp.einsum(
        "asjcf,asjcd->jfd", expert_hidden, d_gathered, preferred_element_type=float_type
    )
    d_hidden = jnp.einsum(
        "asjcd,jfd->asjcf", d_gathered, w_expert_down, preferred_element_type=float_type
    )
    d_expert_gate = (d_hidden * expert_upv * silu_slope(expert_gate)).astype(low_type)
    d_expert_up = (d_hidden * jax.nn.silu(expert_gate)).astype(low_type)
    grad_expert_gate = jnp.einsum(
        "asjcd,asjcf->jdf", expert_rows, d_expert_gate, preferred_element_type=float_type
    )
    grad_expert_up = jnp.einsum(
        "asjcd,asjcf->jdf", expert_rows, d_expert_up, preferred_element_type=float_type
    )
    d_partial = jnp.einsum(
        "asjcf,jdf->asjcd", d_expert_gate, w_expert_gate, preferred_element_type=float_type
    ) + jnp.einsum("asjcf,jdf->asjcd", d_expert_up, w_expert_up, preferred_element_type=float_type)
    d_pair = expert_total(d_partial).astype(low_type)
    d_returned = send_tokens(d_pair).reshape(experts * capacity, -1)
    d_normed_ffn = d_normed_ffn + jnp.sum(
        d_returned[slot_index].reshape(own_rows, TOP, -1).astype(float_type), axis=1
    )
    d_shared = grad_in.astype(low_type)
    grad_shared_down = jnp.einsum(
        "tf,td->fd", shared_hidden, d_shared, preferred_element_type=float_type
    )
    d_shared_hidden = jnp.einsum(
        "td,fd->tf", d_shared, down_shared, preferred_element_type=float_type
    )
    d_shared_gate = (d_shared_hidden * shared_upv * silu_slope(shared_gate)).astype(low_type)
    d_shared_up = (d_shared_hidden * jax.nn.silu(shared_gate)).astype(low_type)
    grad_shared_gate = jnp.einsum(
        "td,tf->df", normed_ffn, d_shared_gate, preferred_element_type=float_type
    )
    grad_shared_up = jnp.einsum(
        "td,tf->df", normed_ffn, d_shared_up, preferred_element_type=float_type
    )
    shared_back = jnp.einsum(
        "tf,df->td", d_shared_gate, gate_shared, preferred_element_type=float_type
    ) + jnp.einsum("tf,df->td", d_shared_up, up_shared, preferred_element_type=float_type)
    d_normed_ffn = d_normed_ffn + shared_back
    d_hidden_norm, grad_gain_ffn = norm_back(
        hidden_one, scale_ffn, gain_ffn.astype(float_type), d_normed_ffn
    )
    d_hidden_one = grad_in + d_hidden_norm
    d_attn_out = d_hidden_one.astype(low_type)
    grad_output = jnp.einsum("tv,td->vd", attn_mixed, d_attn_out, preferred_element_type=float_type)
    d_mixed = (
        jnp.einsum("td,vd->tv", d_attn_out, output_full, preferred_element_type=float_type)
        .astype(low_type)
        .reshape(query_rows, heads_dev, V_HEAD)
    )
    soft_again = jnp.exp(masked_scores() - log_total)
    soft_again_low = soft_again.astype(low_type)
    d_soft = jnp.einsum("qhd,khd->hqk", d_mixed, value_heads, preferred_element_type=float_type)
    d_values = jnp.einsum(
        "hqk,qhd->khd", soft_again_low, d_mixed, preferred_element_type=float_type
    )
    d_scores = (
        soft_again * (d_soft - jnp.sum(soft_again * d_soft, axis=-1, keepdims=True))
    ).astype(low_type)
    d_query_nope = score_scale * jnp.einsum(
        "hqk,khd->qhd", d_scores, key_nope, preferred_element_type=float_type
    )
    d_query_rope = score_scale * jnp.einsum(
        "hqk,kd->qhd", d_scores, rope_group, preferred_element_type=float_type
    )
    d_key_nope = score_scale * jnp.einsum(
        "hqk,qhd->khd", d_scores, query_use[..., :NOPE], preferred_element_type=float_type
    )
    d_key_rope = score_scale * jnp.einsum(
        "hqk,qhd->kd", d_scores, query_use[..., NOPE:], preferred_element_type=float_type
    )
    d_expanded_all = jnp.concatenate([d_key_nope, d_values], axis=-1).reshape(
        group_len, heads_dev * (NOPE + V_HEAD)
    )
    d_expanded_own, d_rope_own = (
        lax.psum_scatter(
            d_expanded_all.astype(jnp.bfloat16), "shard", scatter_dimension=0, tiled=True
        ).astype(jnp.float32),
        lax.psum_scatter(
            d_key_rope.astype(jnp.bfloat16), "shard", scatter_dimension=0, tiled=True
        ).astype(jnp.float32),
    )
    d_expanded = d_expanded_own.astype(low_type)
    grad_expand = jnp.einsum("tr,tc->rc", latent_use, d_expanded, preferred_element_type=float_type)
    d_latent_use = jnp.einsum(
        "tc,rc->tr", d_expanded, expand_full, preferred_element_type=float_type
    )
    d_compressed, grad_gain_latent = norm_back(
        compressed, scale_latent, gain_latent.astype(float_type), d_latent_use
    )
    d_latent = jnp.concatenate(
        [d_compressed, rotate(d_rope_own, cos_own, -sin_own)], axis=-1
    ).astype(low_type)
    d_query_raw = (
        jnp.concatenate(
            [d_query_nope, rotate(d_query_rope, cos_query[:, None, :], -sin_query[:, None, :])],
            axis=-1,
        )
        .reshape(query_rows, heads_dev * (NOPE + ROPE))
        .astype(low_type)
    )
    grad_query = jnp.einsum("td,tq->dq", normed_in, d_query_raw, preferred_element_type=float_type)
    grad_latent = jnp.einsum("td,tl->dl", normed_in, d_latent, preferred_element_type=float_type)
    query_back = jnp.einsum("tq,dq->td", d_query_raw, query_full, preferred_element_type=float_type)
    d_normed_in = query_back + jnp.einsum(
        "tl,dl->td", d_latent, latent_full, preferred_element_type=float_type
    )
    d_token_norm, grad_gain_attn = norm_back(
        token_float, scale_attn, gain_attn.astype(float_type), d_normed_in
    )
    tokens_grad = d_hidden_one + d_token_norm
    grad_query, grad_expand, grad_output, grad_shared_gate, grad_shared_up, grad_shared_down = (
        lax.psum_scatter(
            grad_query.astype(jnp.bfloat16), "shard", scatter_dimension=1, tiled=True
        ).astype(jnp.float32),
        lax.psum_scatter(
            grad_expand.astype(jnp.bfloat16), "shard", scatter_dimension=1, tiled=True
        ).astype(jnp.float32),
        lax.psum_scatter(
            grad_output.astype(jnp.bfloat16), "shard", scatter_dimension=0, tiled=True
        ).astype(jnp.float32),
        lax.psum_scatter(
            grad_shared_gate.astype(jnp.bfloat16), "shard", scatter_dimension=1, tiled=True
        ).astype(jnp.float32),
        lax.psum_scatter(
            grad_shared_up.astype(jnp.bfloat16), "shard", scatter_dimension=1, tiled=True
        ).astype(jnp.float32),
        lax.psum_scatter(
            grad_shared_down.astype(jnp.bfloat16), "shard", scatter_dimension=0, tiled=True
        ).astype(jnp.float32),
    )
    small_sums = (
        lax.psum(grad_gain_attn.astype(jnp.bfloat16), "shard").astype(jnp.float32),
        lax.psum(grad_latent.astype(jnp.bfloat16), "shard").astype(jnp.float32),
        lax.psum(grad_gain_latent.astype(jnp.bfloat16), "shard").astype(jnp.float32),
        lax.psum(grad_gain_ffn.astype(jnp.bfloat16), "shard").astype(jnp.float32),
        lax.psum(grad_router.astype(jnp.bfloat16), "shard").astype(jnp.float32),
    )
    summed = (
        lax.psum_scatter(
            small_sums[0].astype(jnp.bfloat16), "expert", scatter_dimension=0, tiled=True
        ).astype(jnp.float32),
        lax.psum_scatter(
            grad_query.astype(jnp.bfloat16), "expert", scatter_dimension=0, tiled=True
        ).astype(jnp.float32),
        lax.psum_scatter(
            small_sums[1].astype(jnp.bfloat16), "expert", scatter_dimension=0, tiled=True
        ).astype(jnp.float32),
        lax.psum_scatter(
            small_sums[2].astype(jnp.bfloat16), "expert", scatter_dimension=0, tiled=True
        ).astype(jnp.float32),
        lax.psum_scatter(
            grad_expand.astype(jnp.bfloat16), "expert", scatter_dimension=0, tiled=True
        ).astype(jnp.float32),
        lax.psum_scatter(
            grad_output.astype(jnp.bfloat16), "expert", scatter_dimension=1, tiled=True
        ).astype(jnp.float32),
        lax.psum_scatter(
            small_sums[3].astype(jnp.bfloat16), "expert", scatter_dimension=0, tiled=True
        ).astype(jnp.float32),
        lax.psum_scatter(
            small_sums[4].astype(jnp.bfloat16), "expert", scatter_dimension=0, tiled=True
        ).astype(jnp.float32),
        lax.psum_scatter(
            grad_shared_gate.astype(jnp.bfloat16), "expert", scatter_dimension=0, tiled=True
        ).astype(jnp.float32),
        lax.psum_scatter(
            grad_shared_up.astype(jnp.bfloat16), "expert", scatter_dimension=0, tiled=True
        ).astype(jnp.float32),
        lax.psum_scatter(
            grad_shared_down.astype(jnp.bfloat16), "expert", scatter_dimension=1, tiled=True
        ).astype(jnp.float32),
    )
    return (
        block_out,
        tokens_grad,
        summed[0],
        summed[1],
        summed[2],
        summed[3],
        summed[4],
        summed[5],
        summed[6],
        summed[7],
        summed[8],
        summed[9],
        summed[10],
        grad_expert_gate,
        grad_expert_up,
        grad_expert_down,
    )


def solution(mesh):
    return jax.shard_map(
        body,
        mesh=mesh,
        in_specs=(
            P(("expert", "shard"), None),
            P("expert"),
            P(("expert", "shard"), None),
            P(("expert", "shard"), None),
            P("expert"),
            P("expert", "shard"),
            P("expert", None),
            P("expert"),
            P("expert", "shard"),
            P("shard", "expert"),
            P("expert"),
            P("expert", None),
            P("expert", "shard"),
            P("expert", "shard"),
            P("shard", "expert"),
            P("expert", None, "shard"),
            P("expert", None, "shard"),
            P("expert", "shard", None),
        ),
        out_specs=(
            P(("expert", "shard"), None),
            P(("expert", "shard"), None),
            P("expert"),
            P("expert", "shard"),
            P("expert", None),
            P("expert"),
            P("expert", "shard"),
            P("shard", "expert"),
            P("expert"),
            P("expert", None),
            P("expert", "shard"),
            P("expert", "shard"),
            P("shard", "expert"),
            P("expert", None, "shard"),
            P("expert", None, "shard"),
            P("expert", "shard", None),
        ),
        check_vma=False,
    )
```

profile of v0, /device:TPU:1, one launch (start us, length us, event | category | flops | bytes accessed | tf_op | source)
XLA Modules:
  0.0 3527.7 jit_solution(9176685329152130605)
XLA Ops:
  51.6 61.5 %all-gather.26.cloned.1.call-done = bf16[2048,768]{1,0:T(8,128)(2,1)} async-done(((bf16[256,768]{1,0:T(8,128)(2,1)}), bf16[2048,768]{1,0:T(8,128)(2,1)}) %all-gather.26.cloned.1.call-update) | async-done | bytes 3145744 | tf_op jit(solution)/shard_map/all_gather | solution.py:100
  113.1 51.9 %all-gather.30.cloned.1.call-done = bf16[512,2048]{1,0:T(8,128)(2,1)} async-done(((bf16[512,256]{1,0:T(8,128)(2,1)}), bf16[512,2048]{1,0:T(8,128)(2,1)}) %all-gather.30.cloned.1.call-update) | async-done | bytes 2097168 | tf_op jit(solution)/shard_map/all_gather | solution.py:104
  356.9 43.9 %all-gather.32.cloned.1.call-done = bf16[2048,2048]{1,0:T(8,128)(2,1)} async-done(((bf16[512,2048]{1,0:T(8,128)(2,1)}), bf16[2048,2048]{1,0:T(8,128)(2,1)}) %all-gather.32.cloned.1.call-update) | async-done | bytes 8388624 | tf_op jit(solution)/shard_map/all_gather | solution.py:114
  448.5 142.5 %all_to_all.20 = bf16[8,2,96,2048]{3,2,1,0:T(8,128)(2,1)} all-to-all(bf16[8,2,96,2048]{3,2,1,0:T(8,128)(2,1)S(1)} %get-tuple-element.56), channel_id=1, replica_groups=mesh['expert'=8,'shard'=4] {'expert'}, dimensions={0} | all-to-all | bytes 12582912 | tf_op jit(solution)/shard_map/all_to_all | solution.py:59
  591.1 142.6 %all_to_all.21 = bf16[8,2,96,2048]{3,2,1,0:T(8,128)(2,1)} all-to-all(bf16[8,2,96,2048]{3,2,1,0:T(8,128)(2,1)} %get-tuple-element.55), channel_id=1, replica_groups=mesh['expert'=8,'shard'=4] {'expert'}, dimensions={0} | all-to-all | bytes 12582912 | tf_op jit(solution)/shard_map/all_to_all | solution.py:59
  810.4 91.5 %all-gather.48.cloned.1.call-done = bf16[32,2,96,2048]{3,2,1,0:T(8,128)(2,1)} async-done(((bf16[8,2,96,2048]{3,2,1,0:T(8,128)(2,1)}), bf16[32,2,96,2048]{3,2,1,0:T(8,128)(2,1)}) %all-gather.48.cloned.1.call-update) | async-done | bytes 25165840 | tf_op jit(solution)/shard_map/all_gather | solution.py:67
  1026.6 828.2 %all-reduce.14.cloned.1.call-done = (bf16[4,8,2,96,2048]{4,3,1,0,2:T(8,128)(2,1)}, bf16[4,8,2,96,2048]{4,3,1,0,2:T(8,128)(2,1)}) async-done(((bf16[4,8,2,96,2048]{4,3,1,0,2:T(8,128)(2,1)}, bf16[4,8,2,96,2048]{4,3,1,0,2:T(8,128)(2,1)}), (bf16[4,8,2,96,2048]{4,3,1,0,2:T(8,128)(2,1)}, bf16[4,8,2,96,2048]{4,3,1,0,2:T(8,128)(2,1)})) %all-reduce.14.cloned.1.call-update) | async-done | bytes 50331664
  1867.2 151.5 %all-gather.42.cloned.1.call-done = bf16[704,2048]{1,0:T(8,128)(2,1)} async-done(((bf16[704,256]{1,0:T(8,128)(2,1)}), bf16[704,2048]{1,0:T(8,128)(2,1)}) %all-gather.42.cloned.1.call-update) | async-done | bytes 2883600 | tf_op jit(solution)/shard_map/all_gather | solution.py:109
  2044.4 49.9 %all-gather.40.cloned.1.call-done = bf16[2048,2816]{0,1:T(8,128)(2,1)} async-done(((bf16[2048,704]{0,1:T(8,128)(2,1)}), bf16[2048,2816]{0,1:T(8,128)(2,1)}) %all-gather.40.cloned.1.call-update) | async-done | bytes 11534352 | tf_op jit(solution)/shard_map/all_gather | solution.py:116
  2103.6 68.3 %all-gather.36.cloned.1.call-done = bf16[2048,2816]{0,1:T(8,128)(2,1)} async-done(((bf16[2048,704]{0,1:T(8,128)(2,1)}), bf16[2048,2816]{0,1:T(8,128)(2,1)}) %all-gather.36.cloned.1.call-update) | async-done | bytes 11534352 | tf_op jit(solution)/shard_map/all_gather | solution.py:115
  2181.3 68.2 %all-gather.44.cloned.1.call-done = bf16[2816,2048]{1,0:T(8,128)(2,1)} async-done(((bf16[704,2048]{1,0:T(8,128)(2,1)}), bf16[2816,2048]{1,0:T(8,128)(2,1)}) %all-gather.44.cloned.1.call-update) | async-done | bytes 11534352 | tf_op jit(solution)/shard_map/all_gather | solution.py:117
  2429.9 73.2 %reduce-scatter.43.cloned.1.call-done = bf16[2048,704]{0,1:T(8,128)(2,1)} async-done(((bf16[2048,2816]{0,1:T(8,128)(2,1)}), bf16[2048,704]{0,1:T(8,128)(2,1)}) %reduce-scatter.43.cloned.1.call-update) | async-done | bytes 2883600 | tf_op jit(solution)/shard_map/reduce_scatter | solution.py:418
  2503.1 94.6 %reduce-scatter.39.cloned.1.call-done = bf16[2048,704]{0,1:T(8,128)(2,1)} async-done(((bf16[2048,2816]{0,1:T(8,128)(2,1)}), bf16[2048,704]{0,1:T(8,128)(2,1)}) %reduce-scatter.39.cloned.1.call-update) | async-done | bytes 2883600 | tf_op jit(solution)/shard_map/reduce_scatter | solution.py:415
  2597.8 94.8 %reduce-scatter.47.cloned.1.call-done = bf16[704,2048]{1,0:T(8,128)(2,1)} async-done(((bf16[2816,2048]{1,0:T(8,128)(2,1)}), bf16[704,2048]{1,0:T(8,128)(2,1)}) %reduce-scatter.47.cloned.1.call-update) | async-done | bytes 2883600 | tf_op jit(solution)/shard_map/reduce_scatter | solution.py:421
  2705.4 59.1 %reduce-scatter.51.cloned.1.call-done = bf16[256,576]{0,1:T(8,128)(2,1)} async-done(((bf16[2048,576]{0,1:T(8,128)(2,1)}), bf16[256,576]{0,1:T(8,128)(2,1)}) %reduce-scatter.51.cloned.1.call-update) | async-done | bytes 294928 | tf_op jit(solution)/shard_map/reduce_scatter | solution.py:439
  2764.6 47.7 %reduce-scatter.31.cloned.1.call-done = bf16[512,1024]{1,0:T(8,128)(2,1)} async-done(((bf16[512,4096]{1,0:T(8,128)(2,1)}), bf16[512,1024]{1,0:T(8,128)(2,1)}) %reduce-scatter.31.cloned.1.call-update) | async-done | bytes 1048592 | tf_op jit(solution)/shard_map/reduce_scatter | solution.py:409
  2812.3 74.3 %reduce-scatter.35.cloned.1.call-done = bf16[512,2048]{1,0:T(8,128)(2,1)} async-done(((bf16[2048,2048]{1,0:T(8,128)(2,1)}), bf16[512,2048]{1,0:T(8,128)(2,1)}) %reduce-scatter.35.cloned.1.call-update) | async-done | bytes 2097168 | tf_op jit(solution)/shard_map/reduce_scatter | solution.py:412
  2887.9 73.9 %reduce-scatter.45.cloned.1.call-done = bf16[256,704]{0,1:T(8,128)(2,1)} async-done(((bf16[2048,704]{0,1:T(8,128)(2,1)}), bf16[256,704]{0,1:T(8,128)(2,1)}) %reduce-scatter.45.cloned.1.call-update) | async-done | bytes 360464 | tf_op jit(solution)/shard_map/reduce_scatter | solution.py:460
  2963.7 73.0 %reduce-scatter.41.cloned.1.call-done = bf16[256,704]{0,1:T(8,128)(2,1)} async-done(((bf16[2048,704]{0,1:T(8,128)(2,1)}), bf16[256,704]{0,1:T(8,128)(2,1)}) %reduce-scatter.41.cloned.1.call-update) | async-done | bytes 360464 | tf_op jit(solution)/shard_map/reduce_scatter | solution.py:457
  3038.5 73.0 %reduce-scatter.49.cloned.1.call-done = bf16[704,256]{1,0:T(8,128)(2,1)} async-done(((bf16[704,2048]{1,0:T(8,128)(2,1)}), bf16[704,256]{1,0:T(8,128)(2,1)}) %reduce-scatter.49.cloned.1.call-update) | async-done | bytes 360464 | tf_op jit(solution)/shard_map/reduce_scatter | solution.py:463
  3132.4 80.6 %reduce-scatter.27.cloned.1.call-done = bf16[2048,768]{1,0:T(8,128)(2,1)} async-done(((bf16[2048,3072]{1,0:T(8,128)(2,1)}), bf16[2048,768]{1,0:T(8,128)(2,1)}) %reduce-scatter.27.cloned.1.call-update) | async-done | bytes 3145744 | tf_op jit(solution)/shard_map/reduce_scatter | solution.py:406
  3304.1 65.1 %reduce-scatter.33.cloned.1.call-done = bf16[64,1024]{1,0:T(8,128)(2,1)} async-done(((bf16[512,1024]{1,0:T(8,128)(2,1)}), bf16[64,1024]{1,0:T(8,128)(2,1)}) %reduce-scatter.33.cloned.1.call-update) | async-done | bytes 131088 | tf_op jit(solution)/shard_map/reduce_scatter | solution.py:445
  3370.8 69.5 %reduce-scatter.37.cloned.1.call-done = bf16[512,256]{1,0:T(8,128)(2,1)} async-done(((bf16[512,2048]{1,0:T(8,128)(2,1)}), bf16[512,256]{1,0:T(8,128)(2,1)}) %reduce-scatter.37.cloned.1.call-update) | async-done | bytes 262160 | tf_op jit(solution)/shard_map/reduce_scatter | solution.py:448
  3442.0 76.5 %reduce-scatter.29.cloned.1.call-done = bf16[256,768]{1,0:T(8,128)(2,1)} async-done(((bf16[2048,768]{1,0:T(8,128)(2,1)}), bf16[256,768]{1,0:T(8,128)(2,1)}) %reduce-scatter.29.cloned.1.call-update) | async-done | bytes 393232 | tf_op jit(solution)/shard_map/reduce_scatter | solution.py:436
  (426 shorter events, 854.2 us)
Async XLA Ops:
  10.1 290.0 %all-gather.24.cloned.1.call-start = ((), (), s32[]{:S(2)}) async-start(), calls=%async_computation.22 | async-start | bytes 5242880 | tf_op jit(solution)/shard_map/all_gather | solution.py:113
  165.1 580.5 %all-gather.46.cloned.1.call-start = ((), (), s32[]{:S(2)}) async-start(), calls=%async_computation.45 | async-start | bytes 31457280 | tf_op jit(solution)/shard_map/all_gather | solution.py:67
  591.0 310.9 %all-gather.48.cloned.1.call-start = ((), (), s32[]{:S(2)}) async-start(), calls=%async_computation.46 | async-start | bytes 31457280 | tf_op jit(solution)/shard_map/all_gather | solution.py:67
  733.8 291.1 %all-gather.38.cloned.1.call-start = ((), (), s32[]{:S(2)}) async-start(), calls=%async_computation.29 | async-start | bytes 3244032 | tf_op jit(solution)/shard_map/all_gather | solution.py:108
  734.3 291.1 %all-gather.34.cloned.1.call-start = ((), (), s32[]{:S(2)}) async-start(), calls=%async_computation.27 | async-start | bytes 3244032 | tf_op jit(solution)/shard_map/all_gather | solution.py:107
  735.1 1119.7 %all-reduce.14.cloned.1.call-start = ((), (), s32[]{:S(2)}) async-start(), calls=%async_computation.52 | async-start | bytes 100663296
  1024.1 994.7 %all-gather.42.cloned.1.call-start = ((), (), s32[]{:S(2)}) async-start(), calls=%async_computation.31 | async-start | bytes 3244032 | tf_op jit(solution)/shard_map/all_gather | solution.py:109
  1024.8 1069.5 %all-gather.40.cloned.1.call-start = ((), (), s32[]{:S(2)}) async-start(), calls=%async_computation.30 | async-start | bytes 14417920 | tf_op jit(solution)/shard_map/all_gather | solution.py:116
  1025.4 1146.5 %all-gather.36.cloned.1.call-start = ((), (), s32[]{:S(2)}) async-start(), calls=%async_computation.28 | async-start | bytes 14417920 | tf_op jit(solution)/shard_map/all_gather | solution.py:115
  1867.2 382.3 %all-gather.44.cloned.1.call-start = ((), (), s32[]{:S(2)}) async-start(), calls=%async_computation.32 | async-start | bytes 14417920 | tf_op jit(solution)/shard_map/all_gather | solution.py:117
  2043.1 332.5 %reduce-scatter.57.cloned.1.call-start = ((), (), s32[]{:S(2)}) async-start(), calls=%async_computation.51 | async-start | bytes 163840
  2367.5 325.1 %reduce-scatter.47.cloned.1.call-start = ((), (), s32[]{:S(2)}) async-start(), calls=%async_computation.43 | async-start | bytes 14417920 | tf_op jit(solution)/shard_map/reduce_scatter | solution.py:421
  2375.5 389.0 %reduce-scatter.51.cloned.1.call-start = ((), (), s32[]{:S(2)}) async-start(), calls=%async_computation.47 | async-start | bytes 2654208 | tf_op jit(solution)/shard_map/reduce_scatter | solution.py:439
  2416.1 396.1 %reduce-scatter.31.cloned.1.call-start = ((), (), s32[]{:S(2)}) async-start(), calls=%async_computation.35 | async-start | bytes 5242880 | tf_op jit(solution)/shard_map/reduce_scatter | solution.py:409
  2421.6 465.0 %reduce-scatter.35.cloned.1.call-start = ((), (), s32[]{:S(2)}) async-start(), calls=%async_computation.37 | async-start | bytes 10485760 | tf_op jit(solution)/shard_map/reduce_scatter | solution.py:412
  2429.8 532.0 %reduce-scatter.45.cloned.1.call-start = ((), (), s32[]{:S(2)}) async-start(), calls=%async_computation.42 | async-start | bytes 3244032 | tf_op jit(solution)/shard_map/reduce_scatter | solution.py:460
  2503.1 533.6 %reduce-scatter.41.cloned.1.call-start = ((), (), s32[]{:S(2)}) async-start(), calls=%async_computation.40 | async-start | bytes 3244032 | tf_op jit(solution)/shard_map/reduce_scatter | solution.py:457
  2597.8 513.8 %reduce-scatter.49.cloned.1.call-start = ((), (), s32[]{:S(2)}) async-start(), calls=%async_computation.44 | async-start | bytes 3244032 | tf_op jit(solution)/shard_map/reduce_scatter | solution.py:463
  2692.6 520.4 %reduce-scatter.27.cloned.1.call-start = ((), (), s32[]{:S(2)}) async-start(), calls=%async_computation.33 | async-start | bytes 15728640 | tf_op jit(solution)/shard_map/reduce_scatter | solution.py:406
  2703.9 580.2 %reduce-scatter.53.cloned.1.call-start = ((), (), s32[]{:S(2)}) async-start(), calls=%async_computation.49 | async-start | bytes 73728 | tf_op jit(solution)/shard_map/reduce_scatter | solution.py:454
  2705.4 596.9 %all-reduce.12.cloned.1.call-start = ((), (), s32[]{:S(2)}) async-start(), calls=%async_computation.48 | async-start | bytes 589824 | tf_op jit(solution)/shard_map/psum | solution.py:427
  2764.5 604.6 %reduce-scatter.33.cloned.1.call-start = ((), (), s32[]{:S(2)}) async-start(), calls=%async_computation.36 | async-start | bytes 1179648 | tf_op jit(solution)/shard_map/reduce_scatter | solution.py:445
  2812.2 628.0 %reduce-scatter.37.cloned.1.call-start = ((), (), s32[]{:S(2)}) async-start(), calls=%async_computation.38 | async-start | bytes 2359296 | tf_op jit(solution)/shard_map/reduce_scatter | solution.py:448
  2886.6 631.9 %reduce-scatter.29.cloned.1.call-start = ((), (), s32[]{:S(2)}) async-start(), calls=%async_computation.34 | async-start | bytes 3538944 | tf_op jit(solution)/shard_map/reduce_scatter | solution.py:436
  (100 other events, 5566.1 us)
Sparse Core Ops, SparseCore 0:
  53.7 59.3 all-gather.25
  255.7 85.2 all-gather.27
  342.5 58.2 all-gather.31
  591.2 154.3 all-gather.45
  747.1 154.7 all-gather.47
  903.9 59.1 all-gather.37
  965.1 58.1 all-gather.33
  1025.9 828.8 all-reduce.13
  1856.8 161.9 all-gather.41
  2020.2 74.0 all-gather.39
  2095.7 76.1 all-gather.35
  2173.3 76.1 all-gather.43
  2410.8 92.1 reduce-scatter.42
  2505.5 92.1 reduce-scatter.38
  2600.3 92.1 reduce-scatter.46
  2696.1 68.3 reduce-scatter.50
  2814.8 71.6 reduce-scatter.34
  2890.1 71.6 reduce-scatter.44
  2965.2 71.3 reduce-scatter.40
  3040.0 71.4 reduce-scatter.48
  3114.2 98.7 reduce-scatter.26
  3305.7 63.4 reduce-scatter.32
  3373.1 67.1 reduce-scatter.36
  3444.1 74.3 reduce-scatter.28
  (9 shorter events, 367.9 us)
where the time goes:
time: 3540 us; the launch traced here: 3530 us
  waiting for transfers between devices  2500 us (71%)
  blocking collectives  414 us (12%)
  matrix products  348 us (10%)
  local copies, waits for them, and re-layouts  167 us (5%)
  other arithmetic  67.5 us (2%)
    unnamed x36, waiting for transfers between devices  866 us
    all_to_all x2, blocking collectives, send_experts(): lax.all_to_all(values, 'expert', split_axis=0, concat_axis=0, tiled=True)  285 us
    all_gather x1, waiting for transfers between devices, fetch_mixer(): lax.all_gather(w_shared_down, 'expert', axis=1, tiled=True)  152 us
    all_gather x2, waiting for transfers between devices, spread_expert_rows(): return lax.all_gather(values[None], 'shard', axis=0, tiled=True)  102 us
    reduce_scatter x1, waiting for transfers between devices, body(): lax.psum_scatter(grad_shared_down.astype(jnp.bfloat16), 'shard', scatter_...  94.8 us
    reduce_scatter x1, waiting for transfers between devices, body(): lax.psum_scatter(grad_shared_gate.astype(jnp.bfloat16), 'shard', scatter_...  94.6 us
    reduce_scatter x1, waiting for transfers between devices, body(): lax.psum_scatter(grad_query.astype(jnp.bfloat16), 'shard', scatter_dimens...  80.6 us
    reduce_scatter x1, waiting for transfers between devices, body(): lax.psum_scatter(grad_query.astype(jnp.bfloat16), 'expert', scatter_dimen...  76.5 us
  transfers between devices with their start and end apart: 35, of which 28 were waited for; matrix products, arithmetic and copies ran while one was open for 13% of the time, Pallas kernels for 0%

commit v1 on v0

v1 whole, which is shorter than its diff:
```python
import jax
import jax.numpy as jnp
from jax import lax
from jax.sharding import PartitionSpec as P

NOPE = 128
ROPE = 64
V_HEAD = 128
KV_RANK = 512
TOP = 6
LANES = 128

epsilon = 1e-06
F32 = jnp.float32
BF16 = jnp.bfloat16


def pad_to(n, m):
    return -(-n // m) * m


def angles(places, width):
    half_width = width // 2
    spacing = 10000.0 ** (-2.0 * jnp.arange(half_width, dtype=F32) / width)
    turned = places.astype(F32)[:, None] * spacing[None, :]
    return (jnp.cos(turned), jnp.sin(turned))


def positions(segment):
    indices = jnp.arange(segment.shape[0], dtype=jnp.int32)
    prompt_len = jnp.sum((segment == 0).astype(jnp.int32))
    earlier = jnp.sum((segment[None, :] < segment[:, None]).astype(jnp.int32), axis=1)
    return jnp.where(segment == 0, indices, prompt_len + indices - earlier)


def inverse_rms(values):
    return lax.rsqrt(jnp.mean(values * values, axis=-1, keepdims=True) + epsilon)


def norm_back(values, scaling, gain, incoming):
    weighted = incoming * gain
    inner = jnp.mean(weighted * values, axis=-1, keepdims=True)
    return (
        scaling * weighted - values * scaling**3 * inner,
        jnp.sum(incoming * values * scaling, axis=0),
    )


def dot(a, b, dims):
    return lax.dot_general(a, b, (dims, ((), ())), preferred_element_type=F32)


def mm(a, b):
    return dot(a, b, ((1,), (0,)))


def mm_t(a, b):
    return dot(a, b, ((1,), (1,)))


def t_mm(a, b):
    return dot(a, b, ((0,), (0,)))


BOTH = ("expert", "shard")


def gather(values, axes, dim=0):
    return lax.all_gather(values, axes, axis=dim, tiled=True)


def total(values, axes, dim=0):
    return lax.psum_scatter(values, axes, scatter_dimension=dim, tiled=True)


def padded(parts, widths, dim):
    out = []
    for part, width in zip(parts, widths):
        pads = [(0, 0)] * part.ndim
        pads[dim] = (0, width - part.shape[dim])
        out.append(jnp.pad(part, pads))
    return jnp.concatenate(out, axis=dim)


def ffn_block(rows, grads, routed, gate_up, gate_up_t, down, down_t, sizes, first):
    seg, shared, experts, local = sizes
    width = down.shape[0]
    both = mm(rows, gate_up)
    logits = both[:, local * seg + shared : local * seg + shared + experts]
    masked = jnp.where(routed > 0, logits, -1e30)
    raised = jnp.where(routed > 0, jnp.exp(masked - jnp.max(masked, axis=1, keepdims=True)), 0.0)
    gates = raised / jnp.sum(raised, axis=1, keepdims=True)
    expert_lane = jnp.arange(experts, dtype=jnp.int32)[None, :]
    cols = [
        jnp.sum(jnp.where(expert_lane == first + j, gates, 0.0), axis=1, keepdims=True)
        for j in range(local)
    ]
    lane = jnp.arange(width, dtype=jnp.int32)[None, :]
    weight = jnp.where(lane < local * seg + shared, 1.0, 0.0)
    for j in range(local):
        weight = jnp.where((lane >= j * seg) & (lane < (j + 1) * seg), cols[j], weight)
    gate, up = both[:, :width], both[:, width:]
    logistic = jax.nn.sigmoid(gate)
    silu = gate * logistic
    hidden = silu * up
    scaled = (hidden * weight).astype(BF16)
    d_hidden = mm(grads, down_t)
    product = hidden * d_hidden
    d_gates = jnp.zeros(gates.shape, F32)
    for j in range(local):
        d_gates = d_gates + jnp.where(
            expert_lane == first + j,
            jnp.sum(product[:, j * seg : (j + 1) * seg], axis=1, keepdims=True),
            0.0,
        )
    d_hidden = d_hidden * weight
    d_gate = d_hidden * up * (logistic * (1.0 + gate * (1.0 - logistic)))
    d_up = d_hidden * silu
    d_both = jnp.concatenate([d_gate, d_up], axis=1).astype(BF16)
    out = mm(scaled, down).astype(BF16)
    d_rows = mm(d_both, gate_up_t).astype(BF16)
    return out, d_rows, scaled, d_both, d_gates


def body(
    tokens,
    segments,
    routes,
    cotangent,
    attn_gain,
    w_query,
    w_latent,
    latent_gain,
    w_expand,
    w_output,
    ffn_gain,
    w_router,
    w_shared_gate,
    w_shared_up,
    w_shared_down,
    w_expert_gate,
    w_expert_up,
    w_expert_down,
):
    own_rows, width = tokens.shape
    peers = lax.axis_size("expert")
    group_len = segments.shape[0]
    experts = w_router.shape[1]
    local, _, ff = w_expert_gate.shape
    rows_dev = w_query.shape[0]
    heads = w_query.shape[1] // (NOPE + ROPE)
    half = ROPE // 2
    rank_dev = w_expand.shape[0]
    expand_cols = w_expand.shape[1]
    value_cols = heads * V_HEAD
    query_cols = heads * (NOPE + ROPE)
    me_e = lax.axis_index("expert")
    me_s = lax.axis_index("shard")
    offset = me_s * own_rows
    score_scale = (NOPE + ROPE) ** (-0.5)
    shared_dev = w_shared_gate.shape[1]
    shared = shared_dev // peers

    token_group = gather(tokens, "shard")
    q3 = w_query.reshape(rows_dev, heads, NOPE + ROPE)
    query_parts = jnp.concatenate(
        [
            q3[..., :NOPE].reshape(rows_dev, -1),
            q3[..., NOPE : NOPE + half].reshape(rows_dev, -1),
            q3[..., NOPE + half :].reshape(rows_dev, -1),
        ],
        axis=1,
    )
    folds = rows_dev // rank_dev
    fold_cols = expand_cols // folds
    gain_latent_col = jnp.pad(latent_gain, (0, rows_dev - rank_dev))
    few = pad_to(KV_RANK + ROPE + experts + 3, LANES)
    few_pack = jnp.concatenate(
        [
            w_latent,
            w_router,
            attn_gain[:, None],
            ffn_gain[:, None],
            gain_latent_col[:, None],
            jnp.zeros((rows_dev, few - KV_RANK - ROPE - experts - 3), BF16),
        ],
        axis=1,
    )
    pack = jnp.concatenate(
        [query_parts, w_output.T, w_expand.reshape(rows_dev, fold_cols), few_pack], axis=1
    )
    pack = gather(pack, "expert")
    at = [0, query_cols, query_cols + value_cols, query_cols + value_cols + fold_cols]
    query_w = pack[:, at[0] : at[1]]
    output_t = pack[:, at[1] : at[2]]
    expand_w = pack[:, at[2] : at[3]].reshape(KV_RANK, expand_cols)
    few_all = pack[:, at[3] :]
    base = KV_RANK + ROPE
    latent_w = few_all[:, :base]
    router_w = few_all[:, base : base + experts]
    gain_attn = few_all[:, base + experts].astype(F32)
    gain_ffn = few_all[:, base + experts + 1].astype(F32)
    gain_latent = few_all[:, base + experts + 2].reshape(peers, rows_dev)[:, :rank_dev].reshape(-1).astype(F32)

    shared_pack = jnp.concatenate(
        [
            w_shared_gate.reshape(rows_dev, peers, shared),
            w_shared_up.reshape(rows_dev, peers, shared),
            w_shared_down.T.reshape(rows_dev, peers, shared),
        ],
        axis=2,
    ).transpose(1, 0, 2)
    shared_all = lax.all_to_all(shared_pack, "expert", 0, 0, tiled=True).reshape(width, 3 * shared)

    lane_experts = jnp.arange(experts, dtype=jnp.int32)
    routed_own = jnp.any(routes[:, :, None] == lane_experts[None, None, :], axis=1)
    routed_own_low = routed_own.astype(BF16)
    routed_all = gather(routed_own_low, BOTH)

    token_float = token_group.astype(F32)
    normed_in = (token_float * inverse_rms(token_float) * gain_attn).astype(BF16)
    cos_group, sin_group = angles(positions(segments), ROPE)
    latent_raw = mm(normed_in, latent_w)
    compressed = latent_raw[:, :KV_RANK]
    scale_latent = inverse_rms(compressed)
    latent_use = (compressed * scale_latent * gain_latent).astype(BF16)
    key_a = latent_raw[:, KV_RANK : KV_RANK + half]
    key_b = latent_raw[:, KV_RANK + half :]
    rope_key = jnp.concatenate(
        [key_a * cos_group - key_b * sin_group, key_b * cos_group + key_a * sin_group], axis=1
    ).astype(BF16)
    query_raw = mm(normed_in, query_w)
    cos_heads = jnp.tile(cos_group, (1, heads))
    sin_heads = jnp.tile(sin_group, (1, heads))
    nope_cols = heads * NOPE
    rope_cols = heads * half
    query_a = query_raw[:, nope_cols : nope_cols + rope_cols]
    query_b = query_raw[:, nope_cols + rope_cols :]
    query_nope = query_raw[:, :nope_cols].astype(BF16).reshape(group_len, heads, NOPE)
    query_rope = jnp.concatenate(
        [
            (query_a * cos_heads - query_b * sin_heads).reshape(group_len, heads, half),
            (query_b * cos_heads + query_a * sin_heads).reshape(group_len, heads, half),
        ],
        axis=2,
    ).astype(BF16)
    expanded = mm(latent_use, expand_w).astype(BF16).reshape(group_len, heads, NOPE + V_HEAD)
    key_nope = expanded[..., :NOPE]
    value_heads = expanded[..., NOPE:]
    index = jnp.arange(group_len, dtype=jnp.int32)
    allowed = (index[None, :] <= index[:, None]) & (
        (segments[None, :] == 0) | (segments[None, :] == segments[:, None])
    )

    def es(spec, *values):
        return jnp.einsum(spec, *values, preferred_element_type=F32)

    scores = es("qhd,khd->hqk", query_nope, key_nope) + es("qhd,kd->hqk", query_rope, rope_key)
    scores = jnp.where(allowed[None], scores * score_scale, -1e30)
    raised = jnp.exp(scores - jnp.max(scores, axis=-1, keepdims=True))
    soft = raised / jnp.sum(raised, axis=-1, keepdims=True)
    soft_low = soft.astype(BF16)
    attn_mixed = es("hqk,khd->qhd", soft_low, value_heads).astype(BF16).reshape(group_len, value_cols)
    attn_part = mm_t(attn_mixed, output_t).astype(BF16)
    attn_term = total(attn_part, "shard").astype(F32)
    own_float = tokens.astype(F32)
    hidden_one = own_float + attn_term
    scale_ffn = inverse_rms(hidden_one)
    normed_ffn = (hidden_one * scale_ffn * gain_ffn).astype(BF16)
    logits = mm(normed_ffn, router_w)
    masked = jnp.where(routed_own, logits, -1e30)
    lifted = jnp.where(routed_own, jnp.exp(masked - jnp.max(masked, axis=1, keepdims=True)), 0.0)
    gates = lifted / jnp.sum(lifted, axis=1, keepdims=True)

    seg = pad_to(ff, LANES)
    last = pad_to(shared + experts, LANES)
    shared_gate_w = shared_all[:, :shared]
    shared_up_w = shared_all[:, shared : 2 * shared]
    shared_down_t = shared_all[:, 2 * shared :]
    segs = [seg] * local + [last]
    gate_side = padded(
        [*(w_expert_gate[j] for j in range(local)), jnp.concatenate([shared_gate_w, router_w], axis=1)], segs, 1
    )
    gate_side_zero = padded([*(w_expert_gate[j] for j in range(local)), shared_gate_w], segs, 1)
    up_side = padded([*(w_expert_up[j] for j in range(local)), shared_up_w], segs, 1)
    gate_up = jnp.concatenate([gate_side, up_side], axis=1)
    gate_up_t = jnp.concatenate([gate_side_zero, up_side], axis=1).T
    down = padded([*(w_expert_down[j] for j in range(local)), shared_down_t.T], segs, 0)
    down_t = down.T
    chunks = max(1, own_rows * lax.axis_size(BOTH) // 4096)
    per = own_rows // chunks
    outs, d_rows_own, d_gates_own = [], [], []
    grad_gate_up = grad_down = 0.0
    for c in range(chunks):
        pick = slice(c * per, (c + 1) * per)
        rows_c = gather(normed_ffn[pick], BOTH)
        grad_c = gather(cotangent[pick], BOTH)
        routed_c = routed_all.reshape(-1, own_rows, experts)[:, pick].reshape(-1, experts)
        out, d_rows, scaled, d_both, d_gates = ffn_block(
            rows_c, grad_c, routed_c, gate_up, gate_up_t, down, down_t,
            (seg, shared, experts, local), me_e * local,
        )
        outs.append(total(out, BOTH))
        d_rows_own.append(total(d_rows, BOTH))
        d_gates_own.append(total(d_gates, BOTH))
        grad_gate_up = grad_gate_up + t_mm(rows_c, d_both)
        grad_down = grad_down + t_mm(scaled, grad_c)
    ffn_out = jnp.concatenate(outs, axis=0).astype(F32)
    d_normed = jnp.concatenate(d_rows_own, axis=0).astype(F32)
    d_gates = jnp.concatenate(d_gates_own, axis=0)
    block_out = (hidden_one + ffn_out).astype(BF16)
    side = down.shape[0]
    grad_expert_gate = jnp.stack([grad_gate_up[:, j * seg : j * seg + ff] for j in range(local)])
    grad_expert_up = jnp.stack([grad_gate_up[:, side + j * seg : side + j * seg + ff] for j in range(local)])
    grad_expert_down = jnp.stack([grad_down[j * seg : j * seg + ff] for j in range(local)])
    tail = local * seg
    shared_back = jnp.concatenate(
        [
            grad_gate_up[:, tail : tail + shared].astype(BF16),
            grad_gate_up[:, side + tail : side + tail + shared].astype(BF16),
            grad_down[tail : tail + shared].T.astype(BF16),
        ],
        axis=1,
    ).reshape(peers, rows_dev, 3 * shared)
    shared_home = lax.all_to_all(shared_back, "expert", 0, 0, tiled=True).transpose(1, 0, 2).astype(F32)
    grad_shared_gate = shared_home[..., :shared].reshape(rows_dev, shared_dev)
    grad_shared_up = shared_home[..., shared : 2 * shared].reshape(rows_dev, shared_dev)
    grad_shared_down = shared_home[..., 2 * shared :].reshape(rows_dev, shared_dev).T

    grad_in = cotangent.astype(F32)
    d_logits = (gates * (d_gates - jnp.sum(gates * d_gates, axis=1, keepdims=True))).astype(BF16)
    d_normed = d_normed + mm_t(d_logits, router_w)
    grad_router = t_mm(normed_ffn, d_logits)
    d_norm, grad_gain_ffn = norm_back(hidden_one, scale_ffn, gain_ffn, d_normed)
    d_hidden_one = grad_in + d_norm
    d_attn_group = gather(d_hidden_one.astype(BF16), "shard")
    grad_output_t = t_mm(d_attn_group, attn_mixed)
    d_mixed = mm(d_attn_group, output_t).astype(BF16).reshape(group_len, heads, V_HEAD)
    d_soft = es("qhd,khd->hqk", d_mixed, value_heads)
    d_values = es("hqk,qhd->khd", soft_low, d_mixed)
    d_scores = (score_scale * soft * (d_soft - jnp.sum(soft * d_soft, axis=-1, keepdims=True))).astype(BF16)
    d_query_nope = es("hqk,khd->qhd", d_scores, key_nope).reshape(group_len, nope_cols)
    d_query_rope = es("hqk,kd->qhd", d_scores, rope_key)
    d_key_nope = es("hqk,qhd->khd", d_scores, query_nope)
    d_key_rope = es("hqk,qhd->kd", d_scores, query_rope)
    d_expanded = jnp.concatenate([d_key_nope, d_values], axis=-1).reshape(group_len, expand_cols).astype(BF16)
    grad_expand = t_mm(latent_use, d_expanded)
    d_latent_use = mm_t(d_expanded, expand_w)
    d_compressed, grad_gain_latent = norm_back(compressed, scale_latent, gain_latent, d_latent_use)
    d_key_a, d_key_b = d_key_rope[:, :half], d_key_rope[:, half:]
    d_latent = jnp.concatenate(
        [
            d_compressed,
            d_key_a * cos_group + d_key_b * sin_group,
            d_key_b * cos_group - d_key_a * sin_group,
        ],
        axis=1,
    ).astype(BF16)
    d_a = d_query_rope[..., :half].reshape(group_len, rope_cols)
    d_b = d_query_rope[..., half:].reshape(group_len, rope_cols)
    d_query = jnp.concatenate(
        [d_query_nope, d_a * cos_heads + d_b * sin_heads, d_b * cos_heads - d_a * sin_heads], axis=1
    ).astype(BF16)
    grad_query = t_mm(normed_in, d_query)
    grad_latent = t_mm(normed_in, d_latent)
    d_normed_in = total((mm_t(d_query, query_w) + mm_t(d_latent, latent_w)).astype(BF16), "shard").astype(F32)
    d_token, grad_gain_attn = norm_back(own_float, inverse_rms(own_float), gain_attn, d_normed_in)
    tokens_grad = d_hidden_one + d_token

    latent_cols = jnp.pad(grad_gain_latent.reshape(peers, rank_dev), ((0, 0), (0, rows_dev - rank_dev))).reshape(-1)
    few_back = jnp.concatenate(
        [
            grad_latent,
            grad_router,
            grad_gain_attn[:, None],
            grad_gain_ffn[:, None],
            latent_cols[:, None],
            jnp.zeros((width, few - base - experts - 3), F32),
        ],
        axis=1,
    ).astype(BF16)
    back = jnp.concatenate(
        [
            grad_query.astype(BF16),
            grad_output_t.astype(BF16),
            grad_expand.reshape(width, fold_cols).astype(BF16),
            few_back,
        ],
        axis=1,
    )
    home = total(back, "expert").astype(F32)
    few_home = lax.psum(home[:, at[3] :].astype(BF16), "shard").astype(F32)
    gq = home[:, : at[1]]
    grad_query_own = jnp.concatenate(
        [
            gq[:, :nope_cols].reshape(rows_dev, heads, NOPE),
            gq[:, nope_cols : nope_cols + rope_cols].reshape(rows_dev, heads, half),
            gq[:, nope_cols + rope_cols :].reshape(rows_dev, heads, half),
        ],
        axis=2,
    ).reshape(rows_dev, query_cols)
    return (
        block_out,
        tokens_grad,
        few_home[:, base + experts],
        grad_query_own,
        few_home[:, :base],
        few_home[:rank_dev, base + experts + 2],
        home[:, at[2] : at[3]].reshape(rank_dev, expand_cols),
        home[:, at[1] : at[2]].T,
        few_home[:, base + experts + 1],
        few_home[:, base : base + experts],
        grad_shared_gate,
        grad_shared_up,
        grad_shared_down,
        grad_expert_gate,
        grad_expert_up,
        grad_expert_down,
    )


def solution(mesh):
    rows = P(("expert", "shard"), None)
    return jax.shard_map(
        body,
        mesh=mesh,
        in_specs=(
            rows,
            P("expert"),
            rows,
            rows,
            P("expert"),
            P("expert", "shard"),
            P("expert", None),
            P("expert"),
            P("expert", "shard"),
            P("shard", "expert"),
            P("expert"),
            P("expert", None),
            P("expert", "shard"),
            P("expert", "shard"),
            P("shard", "expert"),
            P("expert", None, "shard"),
            P("expert", None, "shard"),
            P("expert", "shard", None),
        ),
        out_specs=(
            rows,
            rows,
            P("expert"),
            P("expert", "shard"),
            P("expert", None),
            P("expert"),
            P("expert", "shard"),
            P("shard", "expert"),
            P("expert"),
            P("expert", None),
            P("expert", "shard"),
            P("expert", "shard"),
            P("shard", "expert"),
            P("expert", None, "shard"),
            P("expert", None, "shard"),
            P("expert", "shard", None),
        ),
        check_vma=False,
    )
```

time: 3540 us -> 1350 us (0.38)
  waiting for transfers between devices: 2500 us -> 820 us
  blocking collectives: 414 us -> 54.2 us
  matrix products: 348 us -> 260 us
  local copies, waits for them, and re-layouts: 167 us -> 116 us
    unnamed x36 -> x12, waiting for transfers between devices: 866 us -> 1.38 us
    reduce_scatter x14 -> x6, waiting for transfers between devices: 955 us -> 497 us  [total(): return lax.psum_scatter(values, axes, scatter_dimension=dim, tiled=True)]
    all_gather x15 -> x5, waiting for transfers between devices: 666 us -> 285 us  [gather(): return lax.all_gather(values, axes, axis=dim, tiled=True)]
    all_to_all x2 -> x0, blocking collectives: 285 us -> none  [send_experts(): lax.all_to_all(values, 'expert', split_axis=0, concat_axis=0, tiled=True)]
    dot_general x42 -> x30, matrix products: 348 us -> 260 us  [the longest x21 242 us: dot(): return lax.dot_general(a, b, (dims, ((), ())), preferred_element_type=F32)]
    concatenate x0 -> x3, local copies, waits for them, and re-layouts: none -> 50.5 us  [the longest x1 39.3 us: body(): jnp.concatenate([grad_query.astype(BF16), grad_output_t.astype(BF16), gra...]
    gather x9 -> x0, local copies, waits for them, and re-layouts: 49.6 us -> none  [the longest x1 15.4 us: body(): d_rows.reshape(pair_count, -1)[slot_pair]]
    all_gather x2 -> x0, local copies, waits for them, and re-layouts: 44.4 us -> none  [spread_expert_rows(): return lax.all_gather(values[None], 'shard', axis=0, tiled=True)]
  transfers between devices with their start and end apart: 35 -> 14, of which waited for: 28 -> 12; matrix products, arithmetic and copies ran while one was open for 13% -> 23% of each run, Pallas kernels for 0% -> 0%
where the time goes in v1:
time: 1350 us; the launch traced here: 1330 us
  waiting for transfers between devices  820 us (61%)
  matrix products  260 us (19%)
  local copies, waits for them, and re-layouts  116 us (9%)
  blocking collectives  54.2 us (4%)
  other arithmetic  53.6 us (4%)
  between operations  15.8 us (1%)
    reduce_scatter x6, waiting for transfers between devices, total(): return lax.psum_scatter(values, axes, scatter_dimension=dim, tiled=True)  497 us
    all_gather x5, waiting for transfers between devices, gather(): return lax.all_gather(values, axes, axis=dim, tiled=True)  285 us
    dot_general x21, matrix products, dot(): return lax.dot_general(a, b, (dims, ((), ())), preferred_element_type=F32)  242 us
    all_gather x1, blocking collectives, gather(): return lax.all_gather(values, axes, axis=dim, tiled=True)  54.2 us
    concatenate x1, local copies, waits for them, and re-layouts, body(): jnp.concatenate([grad_query.astype(BF16), grad_output_t.astype(BF16), gra...  39.3 us
  transfers between devices with their start and end apart: 14, of which 12 were waited for; matrix products, arithmetic and copies ran while one was open for 23% of the time, Pallas kernels for 0%

profile of v1, /device:TPU:1, one launch (start us, length us, event | category | flops | bytes accessed | tf_op | source)
XLA Modules:
  0.0 1332.0 jit_solution(12871820721501999644)
XLA Ops:
  12.3 10.1 concatenate.56
  24.2 10.4 all-gather.6.cloned.1.call-done
  36.8 131.5 %all-gather.8.cloned.1.call-done = bf16[2048,2176]{0,1:T(8,128)(2,1)} async-done(((bf16[256,2176]{0,1:T(8,128)(2,1)}), bf16[2048,2176]{0,1:T(8,128)(2,1)}) %all-gather.8.cloned.1.call-update) | async-done | bytes 8912912 | tf_op jit(solution)/shard_map/all_gather | solution.py:69
  205.6 29.7 %reduce-scatter.7.cloned.1.call-done = bf16[128,2048]{1,0:T(8,128)(2,1)} async-done(((bf16[512,2048]{1,0:T(8,128)(2,1)}), bf16[128,2048]{1,0:T(8,128)(2,1)}) %reduce-scatter.7.cloned.1.call-update) | async-done | bytes 524304 | tf_op jit(solution)/shard_map/reduce_scatter | solution.py:73
  250.2 7.6 copy.203
  258.4 54.2 %all_gather.21 = bf16[4096,16]{0,1:T(8,128)(2,1)S(1)} all-gather(bf16[128,16]{0,1:T(8,128)(2,1)S(1)} %convert_element_type.206), channel_id=1, replica_groups=mesh['expert'=8,'shard'=4] {'expert','shard'}, dimensions={0}, use_global_device_ids=true | all-gather | bytes 135168 | tf_op jit(solution)/shard_map/all_gather | solution.py:69
  326.1 44.2 %all-gather.10.cloned.1.call-done = bf16[4096,2048]{1,0:T(8,128)(2,1)} async-done(((bf16[128,2048]{1,0:T(8,128)(2,1)}), bf16[4096,2048]{1,0:T(8,128)(2,1)}) %all-gather.10.cloned.1.call-update) | async-done | bytes 16777232 | tf_op jit(solution)/shard_map/all_gather | solution.py:69
  370.3 38.6 %fusion.104 = f32[4096,1792]{0,1:T(8,128)} fusion(bf16[4096,2048]{1,0:T(8,128)(2,1)} %all-gather.10.cloned.1.call-done, bf16[2048,1792]{0,1:T(8,128)(2,1)} %get-tuple-element.143), kind=kOutput, calls=%fused_computation.240 | convolution fusion | flops 30064771072 | bytes 53477376 | tf_op jit(solution)/shard_map/dot_general | solution.py:50
  412.2 74.3 %all-gather.12.cloned.1.call-done = bf16[4096,2048]{1,0:T(8,128)(2,1)} async-done(((bf16[128,2048]{1,0:T(8,128)(2,1)}), bf16[4096,2048]{1,0:T(8,128)(2,1)}) %all-gather.12.cloned.1.call-update) | async-done | bytes 16777232 | tf_op jit(solution)/shard_map/all_gather | solution.py:69
  486.5 36.9 %multiply_convert_fusion.1 = (bf16[4096,896]{0,1:T(8,128)(2,1)}, bf16[4096,896]{0,1:T(8,128)(2,1)}, f32[4096,896]{0,1:T(8,128)}, bf16[4096,896]{0,1:T(8,128)(2,1)}) fusion(f32[4096,1792]{0,1:T(8,128)} %fusion.104, f32[896]{0:T(1024)S(1)} %fusion.73, f32[4096]{0:T(1024)S(1)} %get-tuple-element.81, f32[4096]{0:T(1024)S(1)} %get-tuple-element.80, ...), kind=kOutput, calls=%fused_computation.7 | convolution fusion | flops 15105785856 | bytes 86545664 | tf_op jit(solution)/shard_map/dot_general | solution.py:50
  529.6 37.8 %convolution_convert_fusion = bf16[4096,2048]{1,0:T(8,128)(2,1)} fusion(bf16[2048,1792]{0,1:T(8,128)(2,1)} %get-tuple-element.142, bf16[4096,896]{0,1:T(8,128)(2,1)} %get-tuple-element.96, bf16[4096,896]{0,1:T(8,128)(2,1)} %get-tuple-element.95), kind=kOutput, calls=%fused_computation.1 | convolution fusion | flops 30102519808 | bytes 38797312 | tf_op jit(solution)/shard_map/dot_general | solution.py:50
  569.5 86.1 %reduce-scatter.13.cloned.1.call-done = f32[128,16]{0,1:T(8,128)} async-done(((f32[4096,16]{0,1:T(8,128)}), f32[128,16]{0,1:T(8,128)}) %reduce-scatter.13.cloned.1.call-update) | async-done | bytes 8208 | tf_op jit(solution)/shard_map/reduce_scatter | solution.py:73
  657.0 185.2 %reduce-scatter.11.cloned.1.call-done = bf16[128,2048]{1,0:T(8,128)(2,1)} async-done(((bf16[4096,2048]{1,0:T(8,128)(2,1)}), bf16[128,2048]{1,0:T(8,128)(2,1)}) %reduce-scatter.11.cloned.1.call-update) | async-done | bytes 524304 | tf_op jit(solution)/shard_map/reduce_scatter | solution.py:73
  846.1 24.2 %all-gather.14.cloned.1.call-done = bf16[512,2048]{1,0:T(8,128)(2,1)} async-done(((bf16[128,2048]{1,0:T(8,128)(2,1)}), bf16[512,2048]{1,0:T(8,128)(2,1)}) %all-gather.14.cloned.1.call-update) | async-done | bytes 2097168 | tf_op jit(solution)/shard_map/all_gather | solution.py:69
  879.3 5.7 convolution_bitcast_fusion
  899.2 24.6 %convolution_convert_fusion.1 = bf16[4096,2048]{1,0:T(8,128)(2,1)} fusion(bf16[4096,896]{0,1:T(8,128)(2,1)} %get-tuple-element.98, bf16[88,2048]{1,0:T(8,128)(2,1)S(1)} %copy-done.34, bf16[352,2048]{1,0:T(8,128)(2,1)} %copy-done.12, bf16[352,2048]{1,0:T(8,128)(2,1)S(1)} %copy-done.11), kind=kOutput, calls=%fused_computation.2 | convolution fusion | flops 15066464256 | bytes 27361280 | tf_op jit(solution)/shard_map/dot_general | solution.py:50
  943.2 39.3 %concatenate.68 = bf16[2048,2176]{0,1:T(8,128)(2,1)} concatenate(bf16[2048,768]{0,1:T(8,128)(2,1)} %convolution_convert_fusion.2, bf16[2048,512]{0,1:T(8,128)(2,1)} %convolution_convert_fusion.4, bf16[2048,256]{0,1:T(8,128)(2,1)S(1)} %copy.176, bf16[2048,576]{0,1:T(8,128)(2,1)} %convolution_convert_fusion.3, bf16[2048,16]{0,1:T(8,128)(2,1)S(1)} %convolution_convert_fusion.6, ...), dimensions={1} | concatenate | bytes 17825792 | tf_op jit(solution)/shard_map/concatenate | solution.py:382
  982.5 19.2 %fusion.105 = f32[896,2048]{1,0:T(8,128)S(1)} fusion(bf16[4096,896]{0,1:T(8,128)(2,1)} %get-tuple-element.98, bf16[4096,2048]{1,0:T(8,128)(2,1)} %all-gather.12.cloned.1.call-done), kind=kOutput, calls=%fused_computation.241 | convolution fusion | flops 15032385536 | bytes 31457280 | tf_op jit(solution)/shard_map/dot_general | solution.py:50
  1004.7 41.2 %fusion.103 = (bf16[2048,1792]{0,1:T(8,128)(2,1)}, f32[2048,1792]{0,1:T(8,128)}) fusion(bf16[4096,2048]{1,0:T(8,128)(2,1)} %all-gather.10.cloned.1.call-done, bf16[4096,896]{0,1:T(8,128)(2,1)} %get-tuple-element.96, bf16[4096,896]{0,1:T(8,128)(2,1)} %get-tuple-element.95), kind=kOutput, calls=%fused_computation.239 | convolution fusion | flops 30097801216 | bytes 53477376 | tf_op jit(solution)/shard_map/dot_general | solution.py:50
  1053.5 7.5 slice_bitcast_fusion.3
  1073.0 11.5 all-to-all-done.1
  1087.4 32.4 %reduce-scatter.9.cloned.1.call-done = bf16[128,2048]{1,0:T(8,128)(2,1)} async-done(((bf16[4096,2048]{1,0:T(8,128)(2,1)}), bf16[128,2048]{1,0:T(8,128)(2,1)}) %reduce-scatter.9.cloned.1.call-update) | async-done | bytes 524304 | tf_op jit(solution)/shard_map/reduce_scatter | solution.py:73
  1122.8 163.4 %reduce-scatter.17.cloned.1.call-done = bf16[256,2176]{0,1:T(8,128)(2,1)} async-done(((bf16[2048,2176]{0,1:T(8,128)(2,1)}), bf16[256,2176]{0,1:T(8,128)(2,1)}) %reduce-scatter.17.cloned.1.call-update) | async-done | bytes 1114128 | tf_op jit(solution)/shard_map/reduce_scatter | solution.py:73
  1293.1 25.9 %all-reduce.13.cloned.1.call-done = bf16[256,640]{0,1:T(8,128)(2,1)} async-done(((bf16[256,640]{0,1:T(8,128)(2,1)}), bf16[256,640]{0,1:T(8,128)(2,1)}) %all-reduce.13.cloned.1.call-update) | async-done | bytes 327696 | tf_op jit(solution)/shard_map/psum | solution.py:392
  (356 shorter events, 174.8 us)
Async XLA Ops:
  7.2 27.5 %all-gather.6.cloned.1.call-start = ((), (), s32[]{:S(2)}) async-start(), calls=%async_computation.8 | async-start | bytes 2621440 | tf_op jit(solution)/shard_map/all_gather | solution.py:69
  7.9 160.4 %all-gather.8.cloned.1.call-start = ((), (), s32[]{:S(2)}) async-start(), calls=%async_computation.9 | async-start | bytes 10027008 | tf_op jit(solution)/shard_map/all_gather | solution.py:69
  22.4 212.9 %reduce-scatter.7.cloned.1.call-start = ((), (), s32[]{:S(2)}) async-start(), calls=%async_computation.10 | async-start | bytes 2621440 | tf_op jit(solution)/shard_map/reduce_scatter | solution.py:73
  22.5 165.1 %copy-start.75 = (f32[32]{0:T(128)}, f32[32]{0:T(128)S(1)}, u32[]{:S(2)}) copy-start(f32[32]{0:T(128)S(1)} %multiply_power_fusion) | copy-start | bytes 388
  24.0 163.6 %copy-start.68 = (f32[512]{0:T(512)}, f32[512]{0:T(512)S(1)}, u32[]{:S(2)}) copy-start(f32[512]{0:T(512)S(1)} %select_convert_fusion) | copy-start | bytes 6148
  36.8 140.5 %copy-start.77 = (f32[512]{0:T(512)}, f32[512]{0:T(512)S(1)}, u32[]{:S(2)}) copy-start(f32[512]{0:T(512)S(1)} %add_rsqrt_fusion.1) | copy-start | bytes 6148
  169.2 68.0 %copy-start.54 = (f32[2048,1]{0,1:T(1,128)}, f32[2048,1]{0,1:T(1,128)S(1)}, u32[]{:S(2)}) copy-start(f32[2048,1]{0,1:T(1,128)S(1)} %get-tuple-element.103) | copy-start | bytes 24580
  205.1 165.2 %all-gather.10.cloned.1.call-start = ((), (), s32[]{:S(2)}) async-start(), calls=%async_computation.11 | async-start | bytes 17301504 | tf_op jit(solution)/shard_map/all_gather | solution.py:69
  239.2 247.3 %all-gather.12.cloned.1.call-start = ((), (), s32[]{:S(2)}) async-start(), calls=%async_computation.13 | async-start | bytes 17301504 | tf_op jit(solution)/shard_map/all_gather | solution.py:69
  242.1 72.7 %all-to-all-start = ((bf16[8,256,264]{1,2,0:T(8,128)(2,1)}), bf16[8,256,264]{1,2,0:T(8,128)(2,1)}, u32[]{:S(2)}, u32[]{:S(2)}) async-start(bf16[8,256,264]{1,2,0:T(8,128)(2,1)} %maximum_bitcast_fusion), calls=%async_computation.1 | async-start | bytes 2162688 | tf_op jit(solution)/shard_map/all_to_all | solution.py:213
  247.3 408.3 %reduce-scatter.13.cloned.1.call-start = ((), (), s32[]{:S(2)}) async-start(), calls=%async_computation.15 | async-start | bytes 270336 | tf_op jit(solution)/shard_map/reduce_scatter | solution.py:73
  529.5 312.7 %reduce-scatter.11.cloned.1.call-start = ((), (), s32[]{:S(2)}) async-start(), calls=%async_computation.14 | async-start | bytes 17301504 | tf_op jit(solution)/shard_map/reduce_scatter | solution.py:73
  567.3 274.9 %copy-start.1 = (bf16[128,2048]{1,0:T(8,128)(2,1)S(1)}, bf16[128,2048]{1,0:T(8,128)(2,1)}, u32[]{:S(2)}) copy-start(bf16[128,2048]{1,0:T(8,128)(2,1)} %param.18) | copy-start | bytes 1572868
  567.3 274.9 %copy-start.8 = (bf16[128,2048]{1,0:T(8,128)(2,1)S(1)}, bf16[128,2048]{1,0:T(8,128)(2,1)}, u32[]{:S(2)}) copy-start(bf16[128,2048]{1,0:T(8,128)(2,1)} %reduce-scatter.7.cloned.1.call-done) | copy-start | bytes 1572868
  567.4 274.9 %copy-start.55 = (f32[2048,1]{0,1:T(1,128)S(1)}, f32[2048,1]{0,1:T(1,128)}, u32[]{:S(2)}) copy-start(f32[2048,1]{0,1:T(1,128)} %copy-done.54) | copy-start | bytes 24580
  567.4 274.9 %copy-start.72 = (f32[128]{0:T(128)S(1)}, f32[128]{0:T(128)}, u32[]{:S(2)}) copy-start(f32[128]{0:T(128)} %copy-done.71) | copy-start | bytes 1540
  567.4 277.2 %copy-start.20 = (bf16[128,2048]{1,0:T(8,128)(2,1)S(1)}, bf16[128,2048]{1,0:T(8,128)(2,1)}, u32[]{:S(2)}) copy-start(bf16[128,2048]{1,0:T(8,128)(2,1)} %param.21) | copy-start | bytes 1572868
  567.4 277.2 %copy-start.79 = (f32[128]{0:T(128)S(1)}, f32[128]{0:T(128)}, u32[]{:S(2)}) copy-start(f32[128]{0:T(128)} %get-tuple-element.154) | copy-start | bytes 1540
  567.4 302.8 %all-gather.14.cloned.1.call-start = ((), (), s32[]{:S(2)}) async-start(), calls=%async_computation.16 | async-start | bytes 2621440 | tf_op jit(solution)/shard_map/all_gather | solution.py:69
  845.8 96.0 %reduce-scatter.15.cloned.1.call-start = ((), (), s32[]{:S(2)}) async-start(), calls=%async_computation.17 | async-start | bytes 2621440 | tf_op jit(solution)/shard_map/reduce_scatter | solution.py:73
  898.7 221.1 %reduce-scatter.9.cloned.1.call-start = ((), (), s32[]{:S(2)}) async-start(), calls=%async_computation.12 | async-start | bytes 17301504 | tf_op jit(solution)/shard_map/reduce_scatter | solution.py:73
  923.7 362.5 %reduce-scatter.17.cloned.1.call-start = ((), (), s32[]{:S(2)}) async-start(), calls=%async_computation.18 | async-start | bytes 10027008 | tf_op jit(solution)/shard_map/reduce_scatter | solution.py:73
  1048.3 36.3 %all-to-all-start.1 = ((bf16[8,256,264]{1,2,0:T(8,128)(2,1)}), bf16[8,256,264]{1,2,0:T(8,128)(2,1)}, u32[]{:S(2)}, u32[]{:S(2)}) async-start(bf16[8,256,264]{1,2,0:T(8,128)(2,1)} %bitcast.165), calls=%async_computation.7 | async-start | bytes 2162688 | tf_op jit(solution)/shard_map/all_to_all | solution.py:325
  1053.5 265.4 %all-reduce.13.cloned.1.call-start = ((), (), s32[]{:S(2)}) async-start(), calls=%async_computation.19 | async-start | bytes 655360 | tf_op jit(solution)/shard_map/psum | solution.py:392
  (84 other events, 965.0 us)
Sparse Core Ops, SparseCore 0:
  9.6 25.0 all-gather.5
  37.3 130.9 all-gather.7
  205.2 30.0 reduce-scatter.6
  239.3 130.9 all-gather.9
  373.5 113.0 all-gather.11
  529.6 125.9 reduce-scatter.12
  657.9 184.3 reduce-scatter.10
  845.9 24.2 all-gather.13
  898.8 31.0 reduce-scatter.14
  932.1 187.6 reduce-scatter.8
  1123.9 162.3 reduce-scatter.16
  1289.1 29.7 all-reduce.12

commit v2 on v1

v2 whole, which is shorter than its diff:
```python
import jax
import jax.numpy as jnp
from jax import lax
from jax.experimental import pallas as pl
from jax.experimental.pallas import tpu as pltpu
from jax.sharding import PartitionSpec as P

NOPE = 128
ROPE = 64
V_HEAD = 128
KV_RANK = 512
TOP = 6
LANES = 128

epsilon = 1e-06
F32 = jnp.float32
BF16 = jnp.bfloat16


def pad_to(n, m):
    return -(-n // m) * m


def angles(places, width):
    half_width = width // 2
    spacing = 10000.0 ** (-2.0 * jnp.arange(half_width, dtype=F32) / width)
    turned = places.astype(F32)[:, None] * spacing[None, :]
    return (jnp.cos(turned), jnp.sin(turned))


def positions(segment):
    indices = jnp.arange(segment.shape[0], dtype=jnp.int32)
    prompt_len = jnp.sum((segment == 0).astype(jnp.int32))
    earlier = jnp.sum((segment[None, :] < segment[:, None]).astype(jnp.int32), axis=1)
    return jnp.where(segment == 0, indices, prompt_len + indices - earlier)


def inverse_rms(values):
    return lax.rsqrt(jnp.mean(values * values, axis=-1, keepdims=True) + epsilon)


def norm_back(values, scaling, gain, incoming):
    weighted = incoming * gain
    inner = jnp.mean(weighted * values, axis=-1, keepdims=True)
    return (
        scaling * weighted - values * scaling**3 * inner,
        jnp.sum(incoming * values * scaling, axis=0),
    )


def dot(a, b, dims):
    return lax.dot_general(a, b, (dims, ((), ())), preferred_element_type=F32)


def mm(a, b):
    return dot(a, b, ((1,), (0,)))


def mm_t(a, b):
    return dot(a, b, ((1,), (1,)))


def t_mm(a, b):
    return dot(a, b, ((0,), (0,)))


BOTH = ("expert", "shard")


def add(a, b):
    return (a.astype(F32) + b.astype(F32)).astype(BF16)


def padded(parts, widths, dim):
    out = []
    for part, width in zip(parts, widths):
        pads = [(0, 0)] * part.ndim
        pads[dim] = (0, width - part.shape[dim])
        out.append(jnp.pad(part, pads))
    return jnp.concatenate(out, axis=dim)


def routes_of(peers, shards):
    def table(step):
        return [
            (e * shards + s, step(e, s)[0] * shards + step(e, s)[1])
            for e in range(peers)
            for s in range(shards)
        ]

    ring = peers // 2
    return {
        "y": table(lambda e, s: (e ^ 1, s)),
        "x": table(lambda e, s: (e, s ^ 2)),
        "pair": table(lambda e, s: (e, s ^ 1)),
        "ring": table(lambda e, s: ((e // 2 + 1) % ring * 2 + e % 2, s)),
    }


def ffn_kernel(
    local, segs_per, n_seg, steps, width,
    first_ref, x0, x1, g0, g1, router, wg, wu, wdt,
    dx_keep, dx_send, out_keep, out_send, x_all, g_all, hs_all, dg_all, du_all,
    acc_out, acc_dx, gates_s, dgates_s,
):
    j = pl.program_id(0)
    half = x0.shape[0]
    slot = half // 2
    block = wg.shape[1]
    x = jnp.concatenate([x0[...], x1[...]], axis=0)
    g_in = jnp.concatenate([g0[:, :width], g1[:, :width]], axis=0)
    first = first_ref[0]
    lane = lax.broadcasted_iota(jnp.int32, (1, LANES), 1)

    @pl.when(j == 0)
    def _():
        logits = mm(x, router[...])
        routed = jnp.concatenate([g0[:, width:], g1[:, width:]], axis=0) > 0
        masked = jnp.where(routed, logits, -1e30)
        raised = jnp.where(routed, jnp.exp(masked - jnp.max(masked, axis=1, keepdims=True)), 0.0)
        gates_s[...] = raised / jnp.sum(raised, axis=1, keepdims=True)
        dgates_s[...] = jnp.zeros_like(dgates_s)
        acc_out[...] = jnp.zeros_like(acc_out)
        acc_dx[...] = jnp.zeros_like(acc_dx)
        x_all[0] = x
        g_all[0] = g_in

    gates = gates_s[...]
    wanted, columns = [], []
    for part in range(2):
        expert = lax.rem(2 * j + part, n_seg) // segs_per
        want = jnp.where(expert < local, first + expert, -1)
        column = jnp.sum(jnp.where(lane == want, gates, 0.0), axis=1, keepdims=True)
        wanted.append(want)
        columns.append(jnp.where(expert < local, column, 1.0))
    lane_block = lax.broadcasted_iota(jnp.int32, (1, block), 1)
    column = jnp.where(lane_block < LANES, columns[0], columns[1])
    gate, up, d_hidden = mm(x, wg[...]), mm(x, wu[...]), mm(g_in, wdt[...])
    logistic = 1.0 / (1.0 + jnp.exp(-gate))
    silu = gate * logistic
    hidden = silu * up
    scaled = (hidden * column).astype(BF16)
    product = hidden * d_hidden
    for part in range(2):
        dots = jnp.sum(product[:, part * LANES : (part + 1) * LANES], axis=1, keepdims=True)
        dgates_s[...] += jnp.where(lane == wanted[part], dots, 0.0)
    d_hidden = d_hidden * column
    d_gate = (d_hidden * up * (logistic * (1.0 + gate * (1.0 - logistic)))).astype(BF16)
    d_up = (d_hidden * silu).astype(BF16)
    hs_all[0], dg_all[0], du_all[0] = scaled, d_gate, d_up
    acc_out[...] += mm_t(scaled, wdt[...])
    acc_dx[...] += mm_t(d_gate, wg[...]) + mm_t(d_up, wu[...])

    @pl.when(j == steps - 1)
    def _():
        dx_keep[:, :width] = acc_dx[:half].astype(BF16)
        dx_send[:, :width] = acc_dx[half:].astype(BF16)
        dx_keep[:, width:] = dgates_s[:half].astype(BF16)
        dx_send[:, width:] = dgates_s[half:].astype(BF16)
        out_keep[:slot] = acc_out[:slot].astype(BF16)
        out_send[:slot] = acc_out[slot:half].astype(BF16)
        out_keep[slot:] = acc_out[half : half + slot].astype(BF16)
        out_send[slot:] = acc_out[half + slot :].astype(BF16)


def ffn_plane(first, rows, grads, router, weights, local, plane, planes, kept):
    half, width = rows[0].shape
    hid = weights[0].shape[1]
    block = 2 * LANES
    steps = hid // block
    n_seg = hid // LANES // 2
    segs_per = (n_seg - 1) // local

    def fixed(*shape):
        return pl.BlockSpec(shape, lambda j: (0,) * len(shape), pipeline_mode=pl.Buffered(1))

    def whole(*shape):
        return pl.BlockSpec(shape, lambda j: (0,) * len(shape))

    columns = pl.BlockSpec((width, block), lambda j: (0, j))
    in_specs = [
        pl.BlockSpec(memory_space=pltpu.SMEM),
        fixed(half, width), fixed(half, width), fixed(half, width + LANES), fixed(half, width + LANES),
        fixed(width, LANES), columns, columns, columns,
    ]
    args = [first, *rows, *grads, router, *weights]
    plain = len(args)
    aliases = {}
    if kept is not None:
        in_specs += [pl.BlockSpec(memory_space=pl.ANY)] * len(kept)
        args += list(kept)
        aliases = {plain + i: 4 + i for i in range(len(kept))}
    plane_rows = pl.BlockSpec((1, 2 * half, width), lambda j: (plane, 0, 0))
    plane_hidden = pl.BlockSpec((1, 2 * half, block), lambda j: (plane, 0, j))
    shape = jax.ShapeDtypeStruct
    out_shape = (
        [shape((half, width + LANES), BF16)] * 2
        + [shape((half, width), BF16)] * 2
        + [shape((planes, 2 * half, width), BF16)] * 2
        + [shape((planes, 2 * half, hid), BF16)] * 3
    )
    out_specs = [whole(half, width + LANES)] * 2 + [whole(half, width)] * 2 + [plane_rows] * 2 + [plane_hidden] * 3

    def kernel(*refs):
        ffn_kernel(local, segs_per, n_seg, steps, width, *refs[:plain], *refs[len(args) :])

    outs = pl.pallas_call(
        kernel,
        grid=(steps,),
        in_specs=in_specs,
        out_specs=out_specs,
        out_shape=out_shape,
        scratch_shapes=[pltpu.VMEM((2 * half, width), F32)] * 2 + [pltpu.VMEM((2 * half, LANES), F32)] * 2,
        input_output_aliases=aliases,
        compiler_params=pltpu.CompilerParams(
            vmem_limit_bytes=56 * 2**20, dimension_semantics=("arbitrary",)
        ),
        cost_estimate=pl.CostEstimate(
            flops=24 * half * width * hid,
            bytes_accessed=6 * width * hid + 16 * half * width,
            transcendentals=2 * half * hid,
        ),
    )(*args)
    return outs[:4], outs[4:]


def body(
    tokens,
    segments,
    routes,
    cotangent,
    attn_gain,
    w_query,
    w_latent,
    latent_gain,
    w_expand,
    w_output,
    ffn_gain,
    w_router,
    w_shared_gate,
    w_shared_up,
    w_shared_down,
    w_expert_gate,
    w_expert_up,
    w_expert_down,
):
    own_rows, width = tokens.shape
    peers = lax.axis_size("expert")
    shards = lax.axis_size("shard")
    ring = peers // 2
    group_len = segments.shape[0]
    experts = w_router.shape[1]
    local, _, ff = w_expert_gate.shape
    rows_dev = w_query.shape[0]
    heads = w_query.shape[1] // (NOPE + ROPE)
    half = ROPE // 2
    rank_dev = w_expand.shape[0]
    expand_cols = w_expand.shape[1]
    value_cols = heads * V_HEAD
    query_cols = heads * (NOPE + ROPE)
    me_e = lax.axis_index("expert")
    me_s = lax.axis_index("shard")
    score_scale = (NOPE + ROPE) ** (-0.5)
    shared_dev = w_shared_gate.shape[1]
    shared = shared_dev // peers
    tables = routes_of(peers, shards)

    def send(values, way):
        return lax.ppermute(values, BOTH, tables[way])

    def group_gather(block):
        near = jnp.concatenate([block, send(block, "x")], axis=0)
        return jnp.concatenate([near, send(near, "pair")], axis=0)

    def group_sum(parts):
        n = parts.shape[0]
        near = add(parts[: n // 2], send(parts[n // 2 :], "pair"))
        return add(near[: n // 4], send(near[n // 4 :], "x"))

    def expert_at(k):
        return lax.rem(me_e // 2 + ring - k, ring) * 2 + lax.rem(me_e, 2)

    def expert_gather(block):
        n = block.shape[0]
        whole = jnp.zeros((n * peers, block.shape[1]), block.dtype)
        for k in range(ring):
            other = send(block, "y")
            whole = lax.dynamic_update_slice_in_dim(whole, block, expert_at(k) * n, 0)
            whole = lax.dynamic_update_slice_in_dim(whole, other, (expert_at(k) ^ 1) * n, 0)
            if k < ring - 1:
                block = send(block, "ring")
        return whole

    def ring_sum(plane_part):
        total = None
        for k in [*range(1, ring), 0]:
            part = plane_part(k)
            total = part if total is None else add(part, send(total, "ring"))
        return total

    def expert_sum(parts):
        n = parts.shape[0] // peers

        def plane_part(k):
            keep = lax.dynamic_slice_in_dim(parts, expert_at(k) * n, n, 0)
            away = lax.dynamic_slice_in_dim(parts, (expert_at(k) ^ 1) * n, n, 0)
            return add(keep, send(away, "y"))

        return ring_sum(plane_part)

    def ways(k):
        return ("y", "x") if k % 2 == 0 else ("x", "y")

    def plane_gather(block):
        planes = []
        for k in range(ring):
            first, second = ways(k)
            near = jnp.concatenate([block, send(block, first)], axis=0)
            planes.append((near, send(near, second)))
            if k < ring - 1:
                block = send(block, "ring")
        return planes

    token_group = group_gather(tokens)
    q3 = w_query.reshape(rows_dev, heads, NOPE + ROPE)
    query_parts = jnp.concatenate(
        [
            q3[..., :NOPE].reshape(rows_dev, -1),
            q3[..., NOPE : NOPE + half].reshape(rows_dev, -1),
            q3[..., NOPE + half :].reshape(rows_dev, -1),
        ],
        axis=1,
    )
    folds = rows_dev // rank_dev
    fold_cols = expand_cols // folds
    pack = jnp.concatenate([query_parts, w_output.T, w_expand.reshape(rows_dev, fold_cols)], axis=1)
    pack = expert_gather(pack)
    at = [0, query_cols, query_cols + value_cols, query_cols + value_cols + fold_cols]
    query_w = pack[:, at[0] : at[1]]
    output_t = pack[:, at[1] : at[2]]
    expand_w = pack[:, at[2] : at[3]].reshape(KV_RANK, expand_cols)

    base = KV_RANK + ROPE
    few = pad_to(base + experts, LANES)
    few_rows = rows_dev + 32
    part_rows = few_rows // shards
    gains = jnp.concatenate([attn_gain, ffn_gain, latent_gain])
    few_pack = jnp.pad(jnp.concatenate([w_latent, w_router], axis=1), ((0, 32), (0, few - base - experts)))
    few_pack = few_pack.at[rows_dev, : gains.shape[0]].set(gains)
    few_part = lax.dynamic_slice_in_dim(few_pack, me_s * part_rows, part_rows, 0)
    few_all = lax.all_gather(few_part, BOTH, axis=0, tiled=True).reshape(peers, few_rows, few)
    latent_w = few_all[:, :rows_dev, :base].reshape(width, base)
    router_w = few_all[:, :rows_dev, base : base + experts].reshape(width, experts)
    gain_rows = few_all[:, rows_dev].astype(F32)
    gain_attn = gain_rows[:, :rows_dev].reshape(-1)
    gain_ffn = gain_rows[:, rows_dev : 2 * rows_dev].reshape(-1)
    gain_latent = gain_rows[:, 2 * rows_dev : 2 * rows_dev + rank_dev].reshape(-1)

    shared_pack = jnp.concatenate(
        [
            w_shared_gate.reshape(rows_dev, peers, shared),
            w_shared_up.reshape(rows_dev, peers, shared),
            w_shared_down.T.reshape(rows_dev, peers, shared),
        ],
        axis=2,
    ).transpose(1, 0, 2)
    shared_all = lax.all_to_all(shared_pack, "expert", 0, 0, tiled=True).reshape(width, 3 * shared)

    seg = pad_to(ff, LANES)
    segs = [seg] * local + [pad_to(shared, LANES)]
    side = sum(segs)
    sides = []
    for i, parts in enumerate(
        (
            [w_expert_gate[j] for j in range(local)],
            [w_expert_up[j] for j in range(local)],
            [w_expert_down[j].T for j in range(local)],
        )
    ):
        own = padded([*parts, shared_all[:, i * shared : (i + 1) * shared]], segs, 1)
        sides.append(jnp.concatenate([own, send(own, "pair")], axis=1))

    lane_experts = jnp.arange(experts, dtype=jnp.int32)
    routed_own = jnp.any(routes[:, :, None] == lane_experts[None, None, :], axis=1)
    grad_pack = jnp.concatenate(
        [cotangent, jnp.pad(routed_own.astype(BF16), ((0, 0), (0, LANES - experts)))], axis=1
    )
    grad_planes = plane_gather(grad_pack)

    def by_group(values):
        return jnp.concatenate(
            [lax.dynamic_slice_in_dim(values, (me_s ^ r) * own_rows, own_rows, 0) for r in (0, 2, 1, 3)], axis=0
        )

    index = by_group(jnp.arange(group_len, dtype=jnp.int32))
    segment = by_group(segments)
    cos_group, sin_group = angles(by_group(positions(segments)), ROPE)
    token_float = token_group.astype(F32)
    normed_in = (token_float * inverse_rms(token_float) * gain_attn).astype(BF16)
    latent_raw = mm(normed_in, latent_w)
    compressed = latent_raw[:, :KV_RANK]
    scale_latent = inverse_rms(compressed)
    latent_use = (compressed * scale_latent * gain_latent).astype(BF16)
    key_a = latent_raw[:, KV_RANK : KV_RANK + half]
    key_b = latent_raw[:, KV_RANK + half :]
    rope_key = jnp.concatenate(
        [key_a * cos_group - key_b * sin_group, key_b * cos_group + key_a * sin_group], axis=1
    ).astype(BF16)
    query_raw = mm(normed_in, query_w)
    cos_heads = jnp.tile(cos_group, (1, heads))
    sin_heads = jnp.tile(sin_group, (1, heads))
    nope_cols = heads * NOPE
    rope_cols = heads * half
    query_a = query_raw[:, nope_cols : nope_cols + rope_cols]
    query_b = query_raw[:, nope_cols + rope_cols :]
    query_nope = query_raw[:, :nope_cols].astype(BF16).reshape(group_len, heads, NOPE)
    query_rope = jnp.concatenate(
        [
            (query_a * cos_heads - query_b * sin_heads).reshape(group_len, heads, half),
            (query_b * cos_heads + query_a * sin_heads).reshape(group_len, heads, half),
        ],
        axis=2,
    ).astype(BF16)
    expanded = mm(latent_use, expand_w).astype(BF16).reshape(group_len, heads, NOPE + V_HEAD)
    key_nope = expanded[..., :NOPE]
    value_heads = expanded[..., NOPE:]
    allowed = (index[None, :] <= index[:, None]) & (
        (segment[None, :] == 0) | (segment[None, :] == segment[:, None])
    )

    def es(spec, *values):
        return jnp.einsum(spec, *values, preferred_element_type=F32)

    scores = es("qhd,khd->hqk", query_nope, key_nope) + es("qhd,kd->hqk", query_rope, rope_key)
    scores = jnp.where(allowed[None], scores * score_scale, -1e30)
    raised = jnp.exp(scores - jnp.max(scores, axis=-1, keepdims=True))
    soft = raised / jnp.sum(raised, axis=-1, keepdims=True)
    soft_low = soft.astype(BF16)
    attn_mixed = es("hqk,khd->qhd", soft_low, value_heads).astype(BF16).reshape(group_len, value_cols)
    attn_term = group_sum(mm_t(attn_mixed, output_t).astype(BF16)).astype(F32)
    own_float = tokens.astype(F32)
    hidden_one = own_float + attn_term
    scale_ffn = inverse_rms(hidden_one)
    normed_ffn = (hidden_one * scale_ffn * gain_ffn).astype(BF16)
    logits = mm(normed_ffn, router_w)
    masked = jnp.where(routed_own, logits, -1e30)
    lifted = jnp.where(routed_own, jnp.exp(masked - jnp.max(masked, axis=1, keepdims=True)), 0.0)
    gates = lifted / jnp.sum(lifted, axis=1, keepdims=True)

    router_pad = jnp.pad(router_w, ((0, 0), (0, LANES - experts)))
    first_expert = (me_e * local).astype(jnp.int32).reshape(1)
    row_planes = plane_gather(normed_ffn)
    plane_outs, kept = [], None
    for k in range(ring):
        outs, kept = ffn_plane(
            first_expert, row_planes[k], grad_planes[k], router_pad, sides, local, k, ring, kept
        )
        plane_outs.append(outs)

    def halves(keep, away, way_one, way_two):
        near = add(keep, send(away, way_one))
        n = near.shape[0] // 2
        return add(near[:n], send(near[n:], way_two))

    def d_rows_part(k):
        first, second = ways(k)
        return halves(plane_outs[k][0], plane_outs[k][1], second, first)

    def out_part(k):
        first, second = ways(k)
        return halves(plane_outs[k][2], plane_outs[k][3], first, second)

    d_rows = ring_sum(d_rows_part)
    ffn_out = ring_sum(out_part).astype(F32)
    d_normed = d_rows[:, :width].astype(F32)
    d_gates = d_rows[:, width : width + experts].astype(F32)
    block_out = (hidden_one + ffn_out).astype(BF16)

    x_all, g_all, hs_all, dg_all, du_all = (v.reshape(-1, v.shape[-1]) for v in kept)
    from_pair = [
        send(t_mm(x_all, dg_all[:, side:]).astype(BF16), "pair"),
        send(t_mm(x_all, du_all[:, side:]).astype(BF16), "pair"),
        send(t_mm(hs_all[:, side:], g_all).astype(BF16), "pair"),
    ]
    grad_gate = t_mm(x_all, dg_all[:, :side]) + from_pair[0].astype(F32)
    grad_up = t_mm(x_all, du_all[:, :side]) + from_pair[1].astype(F32)
    grad_down = t_mm(hs_all[:, :side], g_all) + from_pair[2].astype(F32)
    grad_expert_gate = jnp.stack([grad_gate[:, j * seg : j * seg + ff] for j in range(local)])
    grad_expert_up = jnp.stack([grad_up[:, j * seg : j * seg + ff] for j in range(local)])
    grad_expert_down = jnp.stack([grad_down[j * seg : j * seg + ff] for j in range(local)])
    tail = local * seg
    shared_back = jnp.concatenate(
        [
            grad_gate[:, tail : tail + shared].astype(BF16),
            grad_up[:, tail : tail + shared].astype(BF16),
            grad_down[tail : tail + shared].T.astype(BF16),
        ],
        axis=1,
    ).reshape(peers, rows_dev, 3 * shared)
    shared_home = lax.all_to_all(shared_back, "expert", 0, 0, tiled=True).transpose(1, 0, 2).astype(F32)
    grad_shared_gate = shared_home[..., :shared].reshape(rows_dev, shared_dev)
    grad_shared_up = shared_home[..., shared : 2 * shared].reshape(rows_dev, shared_dev)
    grad_shared_down = shared_home[..., 2 * shared :].reshape(rows_dev, shared_dev).T

    grad_in = cotangent.astype(F32)
    d_logits = (gates * (d_gates - jnp.sum(gates * d_gates, axis=1, keepdims=True))).astype(BF16)
    d_normed = d_normed + mm_t(d_logits, router_w)
    grad_router = t_mm(normed_ffn, d_logits)
    d_norm, grad_gain_ffn = norm_back(hidden_one, scale_ffn, gain_ffn, d_normed)
    d_hidden_one = grad_in + d_norm
    d_attn_group = group_gather(d_hidden_one.astype(BF16))
    grad_output_t = t_mm(d_attn_group, attn_mixed).astype(BF16)
    d_mixed = mm(d_attn_group, output_t).astype(BF16).reshape(group_len, heads, V_HEAD)
    d_soft = es("qhd,khd->hqk", d_mixed, value_heads)
    d_values = es("hqk,qhd->khd", soft_low, d_mixed)
    d_scores = (score_scale * soft * (d_soft - jnp.sum(soft * d_soft, axis=-1, keepdims=True))).astype(BF16)
    d_query_nope = es("hqk,khd->qhd", d_scores, key_nope).reshape(group_len, nope_cols)
    d_query_rope = es("hqk,kd->qhd", d_scores, rope_key)
    d_key_nope = es("hqk,qhd->khd", d_scores, query_nope)
    d_key_rope = es("hqk,qhd->kd", d_scores, query_rope)
    d_expanded = jnp.concatenate([d_key_nope, d_values], axis=-1).reshape(group_len, expand_cols).astype(BF16)
    grad_expand = t_mm(latent_use, d_expanded)
    d_latent_use = mm_t(d_expanded, expand_w)
    d_compressed, grad_gain_latent = norm_back(compressed, scale_latent, gain_latent, d_latent_use)
    d_key_a, d_key_b = d_key_rope[:, :half], d_key_rope[:, half:]
    d_latent = jnp.concatenate(
        [
            d_compressed,
            d_key_a * cos_group + d_key_b * sin_group,
            d_key_b * cos_group - d_key_a * sin_group,
        ],
        axis=1,
    ).astype(BF16)
    d_a = d_query_rope[..., :half].reshape(group_len, rope_cols)
    d_b = d_query_rope[..., half:].reshape(group_len, rope_cols)
    d_query = jnp.concatenate(
        [d_query_nope, d_a * cos_heads + d_b * sin_heads, d_b * cos_heads - d_a * sin_heads], axis=1
    ).astype(BF16)
    grad_query = t_mm(normed_in, d_query)
    grad_latent = t_mm(normed_in, d_latent)
    d_normed_in = group_sum((mm_t(d_query, query_w) + mm_t(d_latent, latent_w)).astype(BF16)).astype(F32)
    d_token, grad_gain_attn = norm_back(own_float, inverse_rms(own_float), gain_attn, d_normed_in)
    tokens_grad = d_hidden_one + d_token

    back = jnp.concatenate(
        [grad_query.astype(BF16), grad_output_t, grad_expand.astype(BF16).reshape(width, fold_cols)], axis=1
    )
    home = expert_sum(back).astype(F32)
    gain_back = jnp.concatenate(
        [
            grad_gain_attn.reshape(peers, rows_dev),
            grad_gain_ffn.reshape(peers, rows_dev),
            grad_gain_latent.reshape(peers, rank_dev),
        ],
        axis=1,
    )
    few_back = jnp.concatenate([grad_latent, grad_router], axis=1).reshape(peers, rows_dev, base + experts)
    few_back = jnp.concatenate(
        [
            jnp.pad(few_back.astype(BF16), ((0, 0), (0, 0), (0, few - base - experts))),
            jnp.pad(gain_back.astype(BF16)[:, None], ((0, 0), (0, 31), (0, few - gain_back.shape[1]))),
        ],
        axis=1,
    ).reshape(peers * few_rows, few)
    few_home = lax.psum_scatter(few_back, BOTH, scatter_dimension=0, tiled=True)
    few_home = lax.all_gather(few_home, "shard", axis=0, tiled=True).astype(F32)
    gains_home = few_home[rows_dev]
    gq = home[:, : at[1]]
    grad_query_own = jnp.concatenate(
        [
            gq[:, :nope_cols].reshape(rows_dev, heads, NOPE),
            gq[:, nope_cols : nope_cols + rope_cols].reshape(rows_dev, heads, half),
            gq[:, nope_cols + rope_cols :].reshape(rows_dev, heads, half),
        ],
        axis=2,
    ).reshape(rows_dev, query_cols)
    return (
        block_out,
        tokens_grad,
        gains_home[:rows_dev],
        grad_query_own,
        few_home[:rows_dev, :base],
        gains_home[2 * rows_dev : 2 * rows_dev + rank_dev],
        home[:, at[2] : at[3]].reshape(rank_dev, expand_cols),
        home[:, at[1] : at[2]].T,
        gains_home[rows_dev : 2 * rows_dev],
        few_home[:rows_dev, base : base + experts],
        grad_shared_gate,
        grad_shared_up,
        grad_shared_down,
        grad_expert_gate,
        grad_expert_up,
        grad_expert_down,
    )


def solution(mesh):
    rows = P(("expert", "shard"), None)
    return jax.shard_map(
        body,
        mesh=mesh,
        in_specs=(
            rows,
            P("expert"),
            rows,
            rows,
            P("expert"),
            P("expert", "shard"),
            P("expert", None),
            P("expert"),
            P("expert", "shard"),
            P("shard", "expert"),
            P("expert"),
            P("expert", None),
            P("expert", "shard"),
            P("expert", "shard"),
            P("shard", "expert"),
            P("expert", None, "shard"),
            P("expert", None, "shard"),
            P("expert", "shard", None),
        ),
        out_specs=(
            rows,
            rows,
            P("expert"),
            P("expert", "shard"),
            P("expert", None),
            P("expert"),
            P("expert", "shard"),
            P("shard", "expert"),
            P("expert"),
            P("expert", None),
            P("expert", "shard"),
            P("expert", "shard"),
            P("shard", "expert"),
            P("expert", None, "shard"),
            P("expert", None, "shard"),
            P("expert", "shard", None),
        ),
        check_vma=False,
    )
```

time: 1350 us -> 902 us (0.67)
  waiting for transfers between devices: 820 us -> 243 us
  Pallas kernels: 0 us -> 154 us
  matrix products: 260 us -> 123 us
  starting transfers between devices: 12.2 us -> 83.7 us
  other arithmetic: 53.6 us -> 103 us
  blocking collectives: 54.2 us -> 8.83 us
  local copies, waits for them, and re-layouts: 116 us -> 159 us
    reduce_scatter x6 -> x0, waiting for transfers between devices: 497 us -> none  [total(): return lax.psum_scatter(values, axes, scatter_dimension=dim, tiled=True)]
    all_gather x5 -> x1, waiting for transfers between devices: 285 us -> 0.01 us  [body(): lax.all_gather(few_part, BOTH, axis=0, tiled=True)]
    ppermute x0 -> x72, waiting for transfers between devices: none -> 200 us  [send(): return lax.ppermute(values, BOTH, tables[way])]
    pallas_call x0 -> x4, Pallas kernels: none -> 154 us  [ffn_plane(): pl.pallas_call(kernel, grid=(steps,), in_specs=in_specs, out_specs=out_sp...]
    dot_general x21, matrix products: 242 us -> 105 us  [dot(): return lax.dot_general(a, b, (dims, ((), ())), preferred_element_type=F32)]
    ppermute x0 -> x72, starting transfers between devices: none -> 74.9 us  [send(): return lax.ppermute(values, BOTH, tables[way])]
    concatenate x1 -> x19, other arithmetic: 0.11 us -> 46.6 us  [the longest x3 16.7 us: body(): sides.append(jnp.concatenate([own, send(own, 'pair')], axis=1))]
    all_gather x1, blocking collectives: 54.2 us -> 8.83 us  [body(): few_home = lax.all_gather(few_home, 'shard', axis=0, tiled=True).astype(F32)]
  transfers between devices with their start and end apart: 14 -> 76, of which waited for: 12 -> 22; matrix products, arithmetic and copies ran while one was open for 23% -> 40% of each run, Pallas kernels for 0% -> 17%
where the time goes in v2:
time: 902 us; the launch traced here: 892 us
  waiting for transfers between devices  243 us (27%)
  local copies, waits for them, and re-layouts  159 us (18%)
  Pallas kernels  154 us (17%)
  matrix products  123 us (14%)
  other arithmetic  103 us (11%)
  starting transfers between devices  83.7 us (9%)
  between operations  16.8 us (2%)
    ppermute x72, waiting for transfers between devices, send(): return lax.ppermute(values, BOTH, tables[way])  200 us
    pallas_call x4, Pallas kernels, ffn_plane(): pl.pallas_call(kernel, grid=(steps,), in_specs=in_specs, out_specs=out_sp...  154 us
    dot_general x21, matrix products, dot(): return lax.dot_general(a, b, (dims, ((), ())), preferred_element_type=F32)  105 us
    ppermute x72, starting transfers between devices, send(): return lax.ppermute(values, BOTH, tables[way])  74.9 us
    unnamed x302, local copies, waits for them, and re-layouts  48.1 us
    unnamed x3, waiting for transfers between devices  42.6 us
    dot_general x9, matrix products, es(): return jnp.einsum(spec, *values, preferred_element_type=F32)  18.1 us
  transfers between devices with their start and end apart: 76, of which 22 were waited for; matrix products, arithmetic and copies ran while one was open for 40% of the time, Pallas kernels for 17%

profile of v2, /device:TPU:1, one launch (start us, length us, event | category | flops | bytes accessed | tf_op | source)
XLA Modules:
  0.0 891.6 jit_solution(4422340224427937675)
XLA Ops:
  90.7 13.0 %collective-permute-done.26 = bf16[128,2176]{1,0:T(8,128)(2,1)S(1)} collective-permute-done((bf16[128,2176]{1,0:T(8,128)(2,1)}, bf16[128,2176]{1,0:T(8,128)(2,1)S(1)}, u32[]{:S(2)}, u32[]{:S(2)}) %collective-permute-start.26) | collective-permute-done | bytes 557088 | tf_op jit(solution)/shard_map/ppermute | solution.py:269
  104.8 18.4 %collective-permute-done.36 = bf16[128,2176]{1,0:T(8,128)(2,1)} collective-permute-done((bf16[128,2176]{1,0:T(8,128)(2,1)}, bf16[128,2176]{1,0:T(8,128)(2,1)}, u32[]{:S(2)}, u32[]{:S(2)}) %collective-permute-start.36) | collective-permute-done | bytes 557088 | tf_op jit(solution)/shard_map/ppermute | solution.py:269
  276.5 32.3 %collective-permute-done.34 = bf16[128,2048]{1,0:T(8,128)(2,1)S(1)} collective-permute-done((bf16[128,2048]{1,0:T(8,128)(2,1)S(1)}, bf16[128,2048]{1,0:T(8,128)(2,1)S(1)}, u32[]{:S(2)}, u32[]{:S(2)}) %collective-permute-start.34) | collective-permute-done | bytes 524320 | tf_op jit(solution)/shard_map/ppermute | solution.py:269
  313.4 38.5 %shard_map.297 = (bf16[256,2176]{1,0:T(8,128)(2,1)}, bf16[256,2176]{1,0:T(8,128)(2,1)}, bf16[256,2048]{1,0:T(8,128)(2,1)}, bf16[256,2048]{1,0:T(8,128)(2,1)}, bf...) custom-call(s32[1]{0:T(128)} %bitcast.15.refs_0_, ...), custom_call_target="tpu_custom_call" | custom-call | flops 22548578304 | bytes 30408704 | tf_op jit(solution)/shard_map/pallas_call | solution.py:207
  356.7 38.5 %shard_map.298 = (bf16[256,2176]{1,0:T(8,128)(2,1)}, bf16[256,2176]{1,0:T(8,128)(2,1)}, bf16[256,2048]{1,0:T(8,128)(2,1)}, bf16[256,2048]{1,0:T(8,128)(2,1)}, bf...) custom-call(s32[1]{0:T(128)} %bitcast.15.refs_0_, ...), custom_call_target="tpu_custom_call", output_to_operand_aliasing={{4}: (9, {}), {5}: (10, {}), {6}: (11, {}), {7}: (12, {}), ... | custom-call | flops 22548578304 | bytes 30408704 | tf_op jit(solution)/shard_map/pallas_call | solution.py:207
  400.5 38.5 %shard_map.299 = (bf16[256,2176]{1,0:T(8,128)(2,1)}, bf16[256,2176]{1,0:T(8,128)(2,1)}, bf16[256,2048]{1,0:T(8,128)(2,1)}, bf16[256,2048]{1,0:T(8,128)(2,1)}, bf...) custom-call(s32[1]{0:T(128)} %bitcast.15.refs_0_, ...), custom_call_target="tpu_custom_call", output_to_operand_aliasing={{4}: (9, {}), {5}: (10, {}), {6}: (11, {}), {7}: (12, {}), ... | custom-call | flops 22548578304 | bytes 30408704 | tf_op jit(solution)/shard_map/pallas_call | solution.py:207
  445.0 38.7 %shard_map.300 = (bf16[256,2176]{1,0:T(8,128)(2,1)}, bf16[256,2176]{1,0:T(8,128)(2,1)}, bf16[256,2048]{1,0:T(8,128)(2,1)}, bf16[256,2048]{1,0:T(8,128)(2,1)}, bf...) custom-call(s32[1]{0:T(128)} %bitcast.15.refs_0_, ...), custom_call_target="tpu_custom_call", output_to_operand_aliasing={{4}: (9, {}), {5}: (10, {}), {6}: (11, {}), {7}: (12, {}), ... | custom-call | flops 22548578304 | bytes 30408704 | tf_op jit(solution)/shard_map/pallas_call | solution.py:207
  483.8 12.8 %fusion.29 = bf16[2048,896]{0,1:T(8,128)(2,1)} fusion(bf16[2048,2048]{1,0:T(8,128)(2,1)} %bitcast.225, bf16[2048,1792]{1,0:T(8,128)(2,1)} %bitcast.243), kind=kOutput, calls=%fused_computation.43 | convolution fusion | flops 7518027776 | bytes 15728640 | tf_op jit(solution)/shard_map/dot_general | solution.py:52
  506.7 19.6 %collective-permute-done.54 = bf16[128,2176]{1,0:T(8,128)(2,1)S(1)} collective-permute-done((bf16[128,2176]{1,0:T(8,128)(2,1)S(1)}, bf16[128,2176]{1,0:T(8,128)(2,1)S(1)}, u32[]{:S(2)}, u32[]{:S(2)}) %collective-permute-start.54) | collective-permute-done | bytes 557088 | tf_op jit(solution)/shard_map/ppermute | solution.py:269
  527.6 12.8 %collective-permute-done.52 = bf16[128,2176]{1,0:T(8,128)(2,1)S(1)} collective-permute-done((bf16[128,2176]{1,0:T(8,128)(2,1)S(1)}, bf16[128,2176]{1,0:T(8,128)(2,1)S(1)}, u32[]{:S(2)}, u32[]{:S(2)}) %collective-permute-start.52) | collective-permute-done | bytes 557088 | tf_op jit(solution)/shard_map/ppermute | solution.py:269
  542.0 11.3 %collective-permute-done.44 = bf16[128,2048]{1,0:T(8,128)(2,1)S(1)} collective-permute-done((bf16[128,2048]{1,0:T(8,128)(2,1)S(1)}, bf16[128,2048]{1,0:T(8,128)(2,1)S(1)}, u32[]{:S(2)}, u32[]{:S(2)}) %collective-permute-start.44) | collective-permute-done | bytes 524320 | tf_op jit(solution)/shard_map/ppermute | solution.py:269
  555.2 8.5 collective-permute-done.50
  568.5 11.8 %fusion.26 = bf16[2048,896]{0,1:T(8,128)(2,1)} fusion(bf16[2048,2048]{1,0:T(8,128)(2,1)S(1)} %bitcast.229, bf16[2048,1792]{1,0:T(8,128)(2,1)} %bitcast.241), kind=kOutput, calls=%fused_computation.42 | convolution fusion | flops 7518027776 | bytes 15728640 | tf_op jit(solution)/shard_map/dot_general | solution.py:52
  580.3 17.6 %collective-permute-start.70 = (bf16[2048,896]{0,1:T(8,128)(2,1)}, bf16[2048,896]{0,1:T(8,128)(2,1)}, u32[]{:S(2)}, u32[]{:S(2)}) collective-permute-start(bf16[2048,896]{0,1:T(8,128)(2,1)} %fusion.29), channel_id=1, source_target_pairs={{0,1},{1,0},{2,3},{3,2},{4,5},{5,4},{6,7},{7,6},{8,9},{9,8},{10,11... | collective-permute-start | bytes 11010056 | tf_op jit(solution)/shard_map/ppermute | solution.py:269
  600.7 13.0 %collective-permute-done.46 = bf16[128,2048]{1,0:T(8,128)(2,1)S(1)} collective-permute-done((bf16[128,2048]{1,0:T(8,128)(2,1)S(1)}, bf16[128,2048]{1,0:T(8,128)(2,1)S(1)}, u32[]{:S(2)}, u32[]{:S(2)}) %collective-permute-start.46) | collective-permute-done | bytes 524320 | tf_op jit(solution)/shard_map/ppermute | solution.py:269
  616.4 9.5 %fusion.32 = bf16[896,2048]{1,0:T(8,128)(2,1)} fusion(bf16[2048,2048]{1,0:T(8,128)(2,1)S(1)} %bitcast.236, bf16[2048,1792]{1,0:T(8,128)(2,1)S(1)} %bitcast.240), kind=kOutput, calls=%fused_computation.44 | convolution fusion | flops 7518027776 | bytes 15728640 | tf_op jit(solution)/shard_map/dot_general | solution.py:52
  631.0 13.1 %convert_add_fusion.1 = f32[2048,896]{0,1:T(8,128)S(1)} fusion(bf16[2048,896]{0,1:T(8,128)(2,1)} %collective-permute-done.70, bf16[2048,2048]{1,0:T(8,128)(2,1)} %bitcast.226, bf16[2048,1792]{1,0:T(8,128)(2,1)} %bitcast.244), kind=kOutput, calls=%fused_computation.5 | convolution fusion | flops 7519862784 | bytes 23068672 | tf_op jit(solution)/shard_map/dot_general | solution.py:52
  644.2 11.0 %convert_add_fusion.2 = f32[2048,896]{0,1:T(8,128)S(1)} fusion(bf16[2048,896]{0,1:T(8,128)(2,1)} %collective-permute-done.69, bf16[2048,2048]{1,0:T(8,128)(2,1)S(1)} %bitcast.232, bf16[2048,1792]{1,0:T(8,128)(2,1)} %bitcast.242), kind=kOutput, calls=%fused_computation.6 | convolution fusion | flops 7519862784 | bytes 23068672 | tf_op jit(solution)/shard_map/dot_general | solution.py:52
  660.2 12.1 %convert_add_fusion = f32[896,2048]{1,0:T(8,128)S(1)} fusion(bf16[896,2048]{1,0:T(8,128)(2,1)} %collective-permute-done.71, bf16[2048,2048]{1,0:T(8,128)(2,1)} %bitcast.233, bf16[2048,1792]{1,0:T(8,128)(2,1)} %bitcast.237), kind=kOutput, calls=%fused_computation.4 | convolution fusion | flops 7519862784 | bytes 23068672 | tf_op jit(solution)/shard_map/dot_general | solution.py:52
  733.8 9.7 %pad_maximum_fusion.3 = bf16[2048,1536]{0,1:T(8,128)(2,1)S(1)} fusion(bf16[2048,256]{0,1:T(8,128)(2,1)S(1)} %copy-done.39, bf16[2048,512]{0,1:T(8,128)(2,1)S(1)} %convolution_convert_fusion.2, bf16[2048,768]{0,1:T(8,128)(2,1)S(1)} %convolution_convert_fusion), kind=kLoop, calls=%fused_computation.7 | loop fusion | flops 18874368 | bytes 12582912 | tf_op jit(solution)/shard_map/concatenate | solution.py:545
  753.0 11.1 %collective-permute-done.65 = bf16[256,1536]{0,1:T(8,128)(2,1)S(1)} collective-permute-done((bf16[256,1536]{0,1:T(8,128)(2,1)S(1)}, bf16[256,1536]{0,1:T(8,128)(2,1)S(1)}, u32[]{:S(2)}, u32[]{:S(2)}) %collective-permute-start.65) | collective-permute-done | bytes 786464 | tf_op jit(solution)/shard_map/ppermute | solution.py:269
  813.3 12.1 %collective-permute-done.68 = bf16[256,1536]{0,1:T(8,128)(2,1)S(1)} collective-permute-done((bf16[256,1536]{0,1:T(8,128)(2,1)}, bf16[256,1536]{0,1:T(8,128)(2,1)S(1)}, u32[]{:S(2)}, u32[]{:S(2)}) %collective-permute-start.68) | collective-permute-done | bytes 786464 | tf_op jit(solution)/shard_map/ppermute | solution.py:269
  829.8 42.6 %reduce-scatter.4.cloned.1.call-done = bf16[72,640]{1,0:T(8,128)(2,1)} async-done(((bf16[2304,640]{1,0:T(8,128)(2,1)}), bf16[72,640]{1,0:T(8,128)(2,1)}) %reduce-scatter.4.cloned.1.call-update) | async-done | bytes 92176
  872.5 8.8 all_gather.7
  (662 shorter events, 419.3 us)
Async XLA Ops:
  7.3 178.1 %all-gather.2.cloned.1.call-start = ((), (), s32[]{:S(2)}) async-start(), calls=%async_computation.3 | async-start | bytes 3041280 | tf_op jit(solution)/shard_map/all_gather | solution.py:351
  13.1 70.5 %collective-permute-start.2 = (bf16[256,1536]{0,1:T(8,128)(2,1)}, bf16[256,1536]{0,1:T(8,128)(2,1)}, u32[]{:S(2)}, u32[]{:S(2)}) collective-permute-start(bf16[256,1536]{0,1:T(8,128)(2,1)} %constant_dynamic-update-slice_fusion), channel_id=1, source_target_pairs={{0,4},{1,5},{2,6},{3,7},{4,0},{5,1},{6,2},{7,3},{8,12},{9,13},{10,... | collective-permute-start | bytes 2359304 | tf_op jit(solution)/shard_map/ppermute | solution.py:269
  15.1 71.9 %collective-permute-start.3 = (bf16[256,1536]{0,1:T(8,128)(2,1)}, bf16[256,1536]{0,1:T(8,128)(2,1)}, u32[]{:S(2)}, u32[]{:S(2)}) collective-permute-start(bf16[256,1536]{0,1:T(8,128)(2,1)} %constant_dynamic-update-slice_fusion), channel_id=1, source_target_pairs={{0,8},{1,9},{2,10},{3,11},{4,12},{5,13},{6,14},{7,15},{8,16},{9,17... | collective-permute-start | bytes 2359304 | tf_op jit(solution)/shard_map/ppermute | solution.py:269
  17.5 62.3 %collective-permute-start.25 = (bf16[128,2176]{1,0:T(8,128)(2,1)}, bf16[128,2176]{1,0:T(8,128)(2,1)}, u32[]{:S(2)}, u32[]{:S(2)}) collective-permute-start(bf16[128,2176]{1,0:T(8,128)(2,1)} %pad_maximum_fusion.23), channel_id=1, source_target_pairs={{0,8},{1,9},{2,10},{3,11},{4,12},{5,13},{6,14},{7,15},{8,16},{9,17... | collective-permute-start | bytes 1671176 | tf_op jit(solution)/shard_map/ppermute | solution.py:269
  18.8 58.6 %collective-permute-start.13 = (bf16[128,2176]{1,0:T(8,128)(2,1)}, bf16[128,2176]{1,0:T(8,128)(2,1)}, u32[]{:S(2)}, u32[]{:S(2)}) collective-permute-start(bf16[128,2176]{1,0:T(8,128)(2,1)} %pad_maximum_fusion.23), channel_id=1, source_target_pairs={{0,4},{1,5},{2,6},{3,7},{4,0},{5,1},{6,2},{7,3},{8,12},{9,13},{10,... | collective-permute-start | bytes 1671176 | tf_op jit(solution)/shard_map/ppermute | solution.py:269
  29.5 116.5 %all-to-all-start = ((bf16[8,256,264]{1,2,0:T(8,128)(2,1)}), bf16[8,256,264]{1,2,0:T(8,128)(2,1)}, u32[]{:S(2)}, u32[]{:S(2)}) async-start(bf16[8,256,264]{1,2,0:T(8,128)(2,1)} %maximum_bitcast_fusion), calls=%async_computation | async-start | bytes 2162688 | tf_op jit(solution)/shard_map/all_to_all | solution.py:367
  75.1 51.8 %collective-permute-start.1 = (bf16[256,2048]{1,0:T(8,128)(2,1)}, bf16[256,2048]{1,0:T(8,128)(2,1)}, u32[]{:S(2)}, u32[]{:S(2)}) collective-permute-start(bf16[256,2048]{1,0:T(8,128)(2,1)} %pad_maximum_fusion.15), channel_id=1, source_target_pairs={{0,1},{1,0},{2,3},{3,2},{4,5},{5,4},{6,7},{7,6},{8,9},{9,8},{10,11... | collective-permute-start | bytes 3145736 | tf_op jit(solution)/shard_map/ppermute | solution.py:269
  79.5 231.7 %collective-permute-start.14 = (bf16[256,2176]{1,0:T(8,128)(2,1)}, bf16[256,2176]{1,0:T(8,128)(2,1)}, u32[]{:S(2)}, u32[]{:S(2)}) collective-permute-start(bf16[256,2176]{1,0:T(8,128)(2,1)} %pad_maximum_fusion.13.refs_3_), channel_id=1, source_target_pairs={{0,2},{1,3},{2,0},{3,1},{4,6},{5,7},{6,4},{7,5},{8,10},{9,11},{10,... | collective-permute-start | bytes 3342344 | tf_op jit(solution)/shard_map/ppermute | solution.py:269
  141.9 93.2 %collective-permute-start.28 = (bf16[128,2176]{1,0:T(8,128)(2,1)}, bf16[128,2176]{1,0:T(8,128)(2,1)}, u32[]{:S(2)}, u32[]{:S(2)}) collective-permute-start(bf16[128,2176]{1,0:T(8,128)(2,1)} %collective-permute-done.27), channel_id=1, source_target_pairs={{0,2},{1,3},{2,0},{3,1},{4,6},{5,7},{6,4},{7,5},{8,10},{9,11},{10,... | collective-permute-start | bytes 1671176 | tf_op jit(solution)/shard_map/ppermute | solution.py:269
  153.8 83.4 %collective-permute-start.15 = (bf16[2048,896]{1,0:T(8,128)(2,1)}, bf16[2048,896]{1,0:T(8,128)(2,1)}, u32[]{:S(2)}, u32[]{:S(2)}) collective-permute-start(bf16[2048,896]{1,0:T(8,128)(2,1)} %pad_maximum_fusion.7), channel_id=1, source_target_pairs={{0,1},{1,0},{2,3},{3,2},{4,5},{5,4},{6,7},{7,6},{8,9},{9,8},{10,11... | collective-permute-start | bytes 11010056 | tf_op jit(solution)/shard_map/ppermute | solution.py:269
  164.0 80.6 %collective-permute-start.16 = (bf16[2048,896]{1,0:T(8,128)(2,1)}, bf16[2048,896]{1,0:T(8,128)(2,1)}, u32[]{:S(2)}, u32[]{:S(2)}) collective-permute-start(bf16[2048,896]{1,0:T(8,128)(2,1)} %pad_maximum_fusion.8), channel_id=1, source_target_pairs={{0,1},{1,0},{2,3},{3,2},{4,5},{5,4},{6,7},{7,6},{8,9},{9,8},{10,11... | collective-permute-start | bytes 11010056 | tf_op jit(solution)/shard_map/ppermute | solution.py:269
  178.2 80.1 %collective-permute-start.17 = (bf16[2048,896]{1,0:T(8,128)(2,1)}, bf16[2048,896]{1,0:T(8,128)(2,1)}, u32[]{:S(2)}, u32[]{:S(2)}) collective-permute-start(bf16[2048,896]{1,0:T(8,128)(2,1)} %pad_maximum_fusion.9), channel_id=1, source_target_pairs={{0,1},{1,0},{2,3},{3,2},{4,5},{5,4},{6,7},{7,6},{8,9},{9,8},{10,11... | collective-permute-start | bytes 11010056 | tf_op jit(solution)/shard_map/ppermute | solution.py:269
  237.2 118.0 %collective-permute-start.37 = (bf16[256,2176]{1,0:T(8,128)(2,1)}, bf16[256,2176]{1,0:T(8,128)(2,1)}, u32[]{:S(2)}, u32[]{:S(2)}) collective-permute-start(bf16[256,2176]{1,0:T(8,128)(2,1)} %constant_dynamic-update-slice_fusion.14.refs_3_), channel_id=1, source_target_pairs={{0,4},{1,5},{2,6},{3,7},{4,0},{5,1},{6,2},{7,3},{8,12},{9,13},{10,... | collective-permute-start | bytes 3342344 | tf_op jit(solution)/shard_map/ppermute | solution.py:269
  308.8 90.4 %collective-permute-start.33 = (bf16[256,2176]{1,0:T(8,128)(2,1)}, bf16[256,2176]{1,0:T(8,128)(2,1)}, u32[]{:S(2)}, u32[]{:S(2)}) collective-permute-start(bf16[256,2176]{1,0:T(8,128)(2,1)} %constant_dynamic-update-slice_fusion.10.refs_3_), channel_id=1, source_target_pairs={{0,2},{1,3},{2,0},{3,1},{4,6},{5,7},{6,4},{7,5},{8,10},{9,11},{10,... | collective-permute-start | bytes 3342344 | tf_op jit(solution)/shard_map/ppermute | solution.py:269
  352.0 91.6 %collective-permute-start.29 = (bf16[256,2176]{1,0:T(8,128)(2,1)}, bf16[256,2176]{1,0:T(8,128)(2,1)}, u32[]{:S(2)}, u32[]{:S(2)}) collective-permute-start(bf16[256,2176]{1,0:T(8,128)(2,1)} %constant_dynamic-update-slice_fusion.6.refs_3_), channel_id=1, source_target_pairs={{0,4},{1,5},{2,6},{3,7},{4,0},{5,1},{6,2},{7,3},{8,12},{9,13},{10,... | collective-permute-start | bytes 3342344 | tf_op jit(solution)/shard_map/ppermute | solution.py:269
  397.6 99.0 %collective-permute-start.53 = (bf16[256,2176]{1,0:T(8,128)(2,1)}, bf16[256,2176]{1,0:T(8,128)(2,1)S(1)}, u32[]{:S(2)}, u32[]{:S(2)}) collective-permute-start(bf16[256,2176]{1,0:T(8,128)(2,1)} %get-tuple-element.94), channel_id=1, source_target_pairs={{0,4},{1,5},{2,6},{3,7},{4,0},{5,1},{6,2},{7,3},{8,12},{9,13},{10,... | collective-permute-start | bytes 3342344 | tf_op jit(solution)/shard_map/ppermute | solution.py:269
  439.0 161.6 %collective-permute-start.19 = (bf16[128,2048]{1,0:T(8,128)(2,1)}, bf16[128,2048]{1,0:T(8,128)(2,1)S(1)}, u32[]{:S(2)}, u32[]{:S(2)}) collective-permute-start(bf16[128,2048]{1,0:T(8,128)(2,1)} %slice.420), channel_id=1, source_target_pairs={{0,2},{1,3},{2,0},{3,1},{4,6},{5,7},{6,4},{7,5},{8,10},{9,11},{10,... | collective-permute-start | bytes 1572872 | tf_op jit(solution)/shard_map/ppermute | solution.py:269
  440.7 65.3 %collective-permute-start.51 = (bf16[256,2176]{1,0:T(8,128)(2,1)}, bf16[256,2176]{1,0:T(8,128)(2,1)S(1)}, u32[]{:S(2)}, u32[]{:S(2)}) collective-permute-start(bf16[256,2176]{1,0:T(8,128)(2,1)} %get-tuple-element.92), channel_id=1, source_target_pairs={{0,2},{1,3},{2,0},{3,1},{4,6},{5,7},{6,4},{7,5},{8,10},{9,11},{10,... | collective-permute-start | bytes 3342344 | tf_op jit(solution)/shard_map/ppermute | solution.py:269
  443.6 53.8 %collective-permute-start.40 = (bf16[256,2048]{1,0:T(8,128)(2,1)}, bf16[256,2048]{1,0:T(8,128)(2,1)}, u32[]{:S(2)}, u32[]{:S(2)}) collective-permute-start(bf16[256,2048]{1,0:T(8,128)(2,1)} %get-tuple-element.84), channel_id=1, source_target_pairs={{0,4},{1,5},{2,6},{3,7},{4,0},{5,1},{6,2},{7,3},{8,12},{9,13},{10,... | collective-permute-start | bytes 3145736 | tf_op jit(solution)/shard_map/ppermute | solution.py:269
  444.0 154.3 %collective-permute-start.48 = (bf16[128,2176]{1,0:T(8,128)(2,1)S(1)}, bf16[128,2176]{1,0:T(8,128)(2,1)}, u32[]{:S(2)}, u32[]{:S(2)}) collective-permute-start(bf16[128,2176]{1,0:T(8,128)(2,1)S(1)} %slice.428), channel_id=1, source_target_pairs={{0,4},{1,5},{2,6},{3,7},{4,0},{5,1},{6,2},{7,3},{8,12},{9,13},{10,... | collective-permute-start | bytes 1671176 | tf_op jit(solution)/shard_map/ppermute | solution.py:269
  580.3 50.7 %collective-permute-start.70 = (bf16[2048,896]{0,1:T(8,128)(2,1)}, bf16[2048,896]{0,1:T(8,128)(2,1)}, u32[]{:S(2)}, u32[]{:S(2)}) collective-permute-start(bf16[2048,896]{0,1:T(8,128)(2,1)} %fusion.29), channel_id=1, source_target_pairs={{0,1},{1,0},{2,3},{3,2},{4,5},{5,4},{6,7},{7,6},{8,9},{9,8},{10,11... | collective-permute-start | bytes 11010056 | tf_op jit(solution)/shard_map/ppermute | solution.py:269
  630.3 62.6 %collective-permute-start.59 = (bf16[256,2048]{1,0:T(8,128)(2,1)}, bf16[256,2048]{1,0:T(8,128)(2,1)}, u32[]{:S(2)}, u32[]{:S(2)}) collective-permute-start(bf16[256,2048]{1,0:T(8,128)(2,1)} %pad_maximum_fusion.17), channel_id=1, source_target_pairs={{0,1},{1,0},{2,3},{3,2},{4,5},{5,4},{6,7},{7,6},{8,9},{9,8},{10,11... | collective-permute-start | bytes 3145736 | tf_op jit(solution)/shard_map/ppermute | solution.py:269
  676.6 133.9 %all-to-all-start.1 = ((bf16[8,256,264]{1,2,0:T(8,128)(2,1)}), bf16[8,256,264]{1,2,0:T(8,128)(2,1)}, u32[]{:S(2)}, u32[]{:S(2)}) async-start(bf16[8,256,264]{1,2,0:T(8,128)(2,1)} %bitcast.180), calls=%async_computation.1 | async-start | bytes 2162688 | tf_op jit(solution)/shard_map/all_to_all | solution.py:500
  680.8 191.7 %reduce-scatter.4.cloned.1.call-start = ((), (), s32[]{:S(2)}) async-start(), calls=%async_computation.4 | async-start | bytes 3041280
  (189 other events, 2657.5 us)
Sparse Core Ops, SparseCore 0:
  26.0 80.4 all-gather.1
  779.6 92.8 reduce-scatter.3

commit v3 on v2

v3 whole, which is shorter than its diff:
```python
import jax
import jax.numpy as jnp
from jax import lax
from jax.experimental import pallas as pl
from jax.experimental.pallas import tpu as pltpu
from jax.sharding import PartitionSpec as P

NOPE = 128
ROPE = 64
V_HEAD = 128
KV_RANK = 512
TOP = 6
LANES = 128

epsilon = 1e-06
F32 = jnp.float32
BF16 = jnp.bfloat16


def pad_to(n, m):
    return -(-n // m) * m


def angles(places, width):
    half_width = width // 2
    spacing = 10000.0 ** (-2.0 * jnp.arange(half_width, dtype=F32) / width)
    turned = places.astype(F32)[:, None] * spacing[None, :]
    return (jnp.cos(turned), jnp.sin(turned))


def positions(segment):
    indices = jnp.arange(segment.shape[0], dtype=jnp.int32)
    prompt_len = jnp.sum((segment == 0).astype(jnp.int32))
    earlier = jnp.sum((segment[None, :] < segment[:, None]).astype(jnp.int32), axis=1)
    return jnp.where(segment == 0, indices, prompt_len + indices - earlier)


def inverse_rms(values):
    return lax.rsqrt(jnp.mean(values * values, axis=-1, keepdims=True) + epsilon)


def norm_back(values, scaling, gain, incoming):
    weighted = incoming * gain
    inner = jnp.mean(weighted * values, axis=-1, keepdims=True)
    return (
        scaling * weighted - values * scaling**3 * inner,
        jnp.sum(incoming * values * scaling, axis=0),
    )


def dot(a, b, dims):
    return lax.dot_general(a, b, (dims, ((), ())), preferred_element_type=F32)


def mm(a, b):
    return dot(a, b, ((1,), (0,)))


def mm_t(a, b):
    return dot(a, b, ((1,), (1,)))


def t_mm(a, b):
    return dot(a, b, ((0,), (0,)))


BOTH = ("expert", "shard")


def add(a, b):
    return (a.astype(F32) + b.astype(F32)).astype(BF16)


def routes_of(peers, shards):
    def table(step):
        return [
            (e * shards + s, step(e, s)[0] * shards + step(e, s)[1])
            for e in range(peers)
            for s in range(shards)
        ]

    ring = peers // 2

    def around(k):
        return table(lambda e, s: ((e // 2 + k) % ring * 2 + e % 2, s))

    return {
        "y": table(lambda e, s: (e ^ 1, s)),
        "x": table(lambda e, s: (e, s ^ 2)),
        "pair": table(lambda e, s: (e, s ^ 1)),
        "ring": around(1),
        **{k: around(k) for k in range(1 - ring, ring)},
    }


def spread(values, first, lane):
    kept = jnp.where((lane >= first) & (lane < first + ROPE // 2), values, 0.0)
    kept = kept + pltpu.roll(kept, ROPE // 2, 1)
    return kept + pltpu.roll(kept, ROPE, 1)


def attn_forward_kernel(
    heads, peers, score_scale,
    places, tokens, latent_x, latent_pair, cos, sin, index_c, index_r, segment_c, segment_r,
    small, mains,
    part_keep, part_send, normed_o, query_o, key_rope_o, expanded_o, soft_o, mixed_o, compressed_o, latent_o,
    gains, gain_latent, query_w, output_t, expand_w, extra_w, latent_w,
    *, gain_at,
):
    group = tokens.shape[0]
    rank = KV_RANK // peers
    rows = mains[0].shape[0]
    shards = latent_w.shape[0]
    cut = (query_w.shape[1], query_w.shape[1] + output_t.shape[1])
    for p in range(peers):
        to = pl.ds(pl.multiple_of(places[p] * rows, rows), rows)
        query_w[to, :] = mains[p][:, : cut[0]]
        output_t[to, :] = mains[p][:, cut[0] : cut[1]]
        expand_w[to, :] = mains[p][:, cut[1] :]
        at = slice(p * rows, (p + 1) * rows)
        latent_w[places[peers], to, :] = small[at, :LANES]
        extra_w[to, :] = small[at, LANES:]
        latent_w[places[peers + 1], to, :] = latent_x[at]
        latent_w[places[peers + 2], to, :] = latent_pair[0, at]
        latent_w[places[peers + 3], to, :] = latent_pair[1, at]
    block, at = gain_at // LANES * LANES, gain_at % LANES
    gains[...] = extra_w[:, block : block + LANES].astype(F32).T[at : at + 8]
    few_rows = [extra_w[p * rows : p * rows + rank, block : block + LANES] for p in range(peers)]
    gain_latent[...] = jnp.concatenate(few_rows, axis=0).astype(F32).T[at + 2 : at + 3]
    x = tokens[...].astype(F32)
    x = x * lax.rsqrt(jnp.mean(x * x, axis=1, keepdims=True) + epsilon) * gains[0:1]
    normed_o[...] = x.astype(BF16)
    normed = normed_o[...]
    lane = lax.broadcasted_iota(jnp.int32, (1, LANES), 1)
    c, s = cos[...], sin[...]
    raw = mm(normed, extra_w[:, :LANES])
    a, b = spread(raw, 0, lane), spread(raw, ROPE // 2, lane)
    key_rope_o[:, :LANES] = (a * c - b * s).astype(BF16)
    key_rope_o[:, LANES:] = (b * c + a * s).astype(BF16)
    for j in range(shards):
        compressed_o[:, j * LANES : (j + 1) * LANES] = mm(normed, latent_w[j])
    u = compressed_o[...]
    r = lax.rsqrt(jnp.mean(u * u, axis=1, keepdims=True) + epsilon)
    latent_o[...] = (u * r * gain_latent[...]).astype(BF16)
    q = mm(normed, query_w[...])
    nope = heads * NOPE
    query_o[:, :nope] = q[:, :nope].astype(BF16)
    a, b = q[:, nope : nope + LANES], q[:, nope + LANES :]
    query_o[:, nope : nope + LANES] = (a * c - b * s).astype(BF16)
    query_o[:, nope + LANES :] = (b * c + a * s).astype(BF16)
    allowed = (index_r[...] <= index_c[...]) & ((segment_r[...] == 0) | (segment_r[...] == segment_c[...]))
    lane2 = lax.rem(lax.broadcasted_iota(jnp.int32, (1, 2 * LANES), 1), LANES)
    for h in range(heads):
        w = jnp.concatenate(
            [expand_w[pl.ds((e * heads + h) * rank, rank), :] for e in range(peers)], axis=0
        )
        expanded_o[h] = mm(latent_o[...], w).astype(BF16)
        key_rope = jnp.where((lane2 >= h * ROPE // 2) & (lane2 < (h + 1) * ROPE // 2), key_rope_o[...], jnp.zeros((), BF16))
        scores = mm_t(query_o[:, h * NOPE : (h + 1) * NOPE], expanded_o[h, :, :NOPE]) + mm_t(query_o[:, nope:], key_rope)
        scores = jnp.where(allowed, scores * score_scale, -1e30)
        raised = jnp.exp(scores - jnp.max(scores, axis=1, keepdims=True))
        soft = raised * (1.0 / jnp.sum(raised, axis=1, keepdims=True))
        soft_o[h] = soft
        mixed_o[:, h * V_HEAD : (h + 1) * V_HEAD] = mm(soft.astype(BF16), expanded_o[h, :, NOPE:]).astype(BF16)
    half = group // 2
    part_keep[...] = mm_t(mixed_o[:half], output_t[...]).astype(BF16)
    part_send[...] = mm_t(mixed_o[half:], output_t[...]).astype(BF16)


def attn_backward_kernel(
    heads, peers, score_scale,
    places, d_attn, query_w, output_t, expand_w, extra_w, latent_w, gain_latent, cos, sin,
    normed, query, key_rope_all, expanded, soft_all, mixed, compressed, latent,
    normed_ffn, d_logits, tokens, g_gain_ffn,
    g_mains, near_keep, near_send, d_in_keep, d_in_send,
    g_all, g_few, d_query_s, d_latent_s, d_use_s,
    *, gain_at,
):
    group = d_attn.shape[0]
    rank = KV_RANK // peers
    shards = latent_w.shape[0]
    nope = heads * NOPE
    lane = lax.broadcasted_iota(jnp.int32, (1, LANES), 1)
    lane2 = lax.rem(lax.broadcasted_iota(jnp.int32, (1, 2 * LANES), 1), LANES)
    rows = g_mains[0].shape[0]
    cut = (query_w.shape[1], query_w.shape[1] + output_t.shape[1])
    width = d_attn.shape[1]
    strips = [slice(lo, lo + width // 4) for lo in range(0, width, width // 4)]
    value_cols = output_t.shape[1]
    for strip in strips:
        g_all[strip, :value_cols] = t_mm(d_attn[:, strip], mixed[...]).astype(BF16)
    d_mixed = mm(d_attn[...], output_t[...]).astype(BF16)
    d_query_rope = jnp.zeros((group, 2 * LANES), F32)
    d_key_rope = jnp.zeros((group, 2 * LANES), F32)
    for h in range(heads):
        mine = (lane2 >= h * ROPE // 2) & (lane2 < (h + 1) * ROPE // 2)
        key_rope = jnp.where(mine, key_rope_all[...], jnp.zeros((), BF16))
        soft = soft_all[h]
        d_out = d_mixed[:, h * V_HEAD : (h + 1) * V_HEAD]
        d_soft = mm_t(d_out, expanded[h, :, NOPE:])
        d_scores = score_scale * soft * (d_soft - jnp.sum(soft * d_soft, axis=1, keepdims=True))
        d_scores = d_scores.astype(BF16)
        d_query_s[:, h * NOPE : (h + 1) * NOPE] = mm(d_scores, expanded[h, :, :NOPE]).astype(BF16)
        d_query_rope = d_query_rope + mm(d_scores, key_rope)
        both = jnp.concatenate([query[:, h * NOPE : (h + 1) * NOPE], query[:, nope:]], axis=1)
        d_key = t_mm(d_scores, both)
        d_key_rope = d_key_rope + jnp.where(mine, d_key[:, NOPE:], 0.0)
        d_values = t_mm(soft.astype(BF16), d_out)
        d_expanded = jnp.concatenate([d_key[:, :NOPE], d_values], axis=1).astype(BF16)
        w = jnp.concatenate(
            [expand_w[pl.ds((e * heads + h) * rank, rank), :] for e in range(peers)], axis=0
        )
        g_w = t_mm(latent[...], d_expanded).astype(BF16)
        for e in range(peers):
            g_all[pl.ds((e * heads + h) * rank, rank), value_cols:] = g_w[e * rank : (e + 1) * rank]
        back = mm_t(d_expanded, w)
        if h == 0:
            d_use_s[...] = back
        else:
            d_use_s[...] += back
    for p in range(peers):
        g_mains[p][:, cut[0] :] = g_all[pl.ds(pl.multiple_of(places[p] * rows, rows), rows), :]
    c, s = cos[...], sin[...]
    a, b = d_query_rope[:, :LANES], d_query_rope[:, LANES:]
    d_query_s[:, nope : nope + LANES] = (a * c + b * s).astype(BF16)
    d_query_s[:, nope + LANES :] = (b * c - a * s).astype(BF16)
    u, n = compressed[...], d_use_s[...]
    r = lax.rsqrt(jnp.mean(u * u, axis=1, keepdims=True) + epsilon)
    weighted = n * gain_latent[...]
    inner = jnp.mean(weighted * u, axis=1, keepdims=True)
    g_gain_latent = jnp.sum(n * u * r, axis=0, keepdims=True)
    d_latent_s[...] = (r * weighted - u * (r * r * r * inner)).astype(BF16)

    def folded(v):
        v = v + pltpu.roll(v, ROPE // 2, 1)
        return v + pltpu.roll(v, ROPE, 1)

    a, b = folded(d_key_rope[:, :LANES]), folded(d_key_rope[:, LANES:])
    d_extra = jnp.where(
        lane < ROPE // 2, a * c + b * s, jnp.where(lane < ROPE, b * c - a * s, 0.0)
    ).astype(BF16)
    half = group // 2
    g_gain_attn = jnp.zeros((1, tokens.shape[1]), F32)
    fine = half // 2
    for lo in range(0, group, fine):
        part, to = slice(lo, lo + fine), (d_in_keep if lo < half else d_in_send).at[pl.ds(lo % half, fine)]
        total = mm_t(d_query_s[part], query_w[...]) + mm_t(d_extra[part], extra_w[:, :LANES])
        for j in range(shards):
            total = total + mm_t(d_latent_s[part, j * LANES : (j + 1) * LANES], latent_w[j])
        to[...] = total.astype(BF16)
        x = tokens[part].astype(F32)
        x = x * lax.rsqrt(jnp.mean(x * x, axis=1, keepdims=True) + epsilon)
        g_gain_attn = g_gain_attn + jnp.sum(total * x, axis=0, keepdims=True)
    for strip in strips:
        g_all[strip, :] = t_mm(normed[:, strip], d_query_s[...]).astype(BF16)
    wide = extra_w.shape[1] // LANES
    line = lax.broadcasted_iota(jnp.int32, (LANES, 1), 0)
    at_line = gain_at % LANES
    for j in range(wide):
        g_extra = t_mm(normed_ffn[...], d_logits[:, j * LANES : (j + 1) * LANES])
        if j == 0:
            g_extra = g_extra + t_mm(normed[...], d_extra)
        if j == gain_at // LANES:
            both = jnp.where(line == at_line, g_gain_attn, jnp.where(line == at_line + 1, g_gain_ffn[...], 0.0))
            g_extra = g_extra + both.T
        g_few[shards + j] = g_extra.astype(BF16)
    tall = jnp.where(line == at_line + 2, g_gain_latent, 0.0).T.astype(BF16)
    j = shards + gain_at // LANES
    for e in range(peers):
        at = slice(e * rows, e * rows + rank)
        g_few[j, at] = g_few[j, at] + tall[e * rank : (e + 1) * rank]
    for strip in strips:
        g_lat = t_mm(normed[:, strip], d_latent_s[...]).astype(BF16)
        for j in range(shards):
            g_few[j, strip] = g_lat[:, j * LANES : (j + 1) * LANES]
    for p in range(peers):
        at = pl.ds(pl.multiple_of(places[p] * rows, rows), rows)
        to = slice(p * rows, (p + 1) * rows)
        g_mains[p][:, : cut[0]] = g_all[at, :]
        for j in range(2):
            near_keep[j, to] = g_few[places[peers + j], at, :]
            near_send[j, to] = g_few[places[peers + 2 + j], at, :]
        for j in range(wide):
            near_keep[2 + j, to] = g_few[shards + j, at, :]
            near_send[2 + j, to] = g_few[shards + j, at, :]


def in_vmem(kernel, outs, scratch, flops, args):
    spec = pl.BlockSpec(memory_space=pltpu.VMEM)
    return pl.pallas_call(
        kernel,
        in_specs=[pl.BlockSpec(memory_space=pltpu.SMEM)] + [spec] * (len(args) - 1),
        out_specs=[spec] * len(outs),
        out_shape=outs,
        scratch_shapes=scratch,
        compiler_params=pltpu.CompilerParams(vmem_limit_bytes=60 * 2**20),
        cost_estimate=pl.CostEstimate(flops=flops, bytes_accessed=24 * 2**20, transcendentals=2**20),
    )(*args)


def attn_forward(heads, peers, score_scale, gain_at, args, small, mains):
    group, width = args[1].shape
    query_cols = heads * (NOPE + ROPE)
    shape = jax.ShapeDtypeStruct
    outs = [
        shape((group // 2, width), BF16), shape((group // 2, width), BF16), shape((group, width), BF16),
        shape((group, query_cols), BF16), shape((group, 2 * LANES), BF16),
        shape((heads, group, NOPE + V_HEAD), BF16), shape((heads, group, group), F32),
        shape((group, heads * V_HEAD), BF16), shape((group, KV_RANK), F32), shape((group, KV_RANK), BF16),
        shape((8, width), F32), shape((1, KV_RANK), F32),
        shape((width, query_cols), BF16), shape((width, heads * V_HEAD), BF16), shape((width, NOPE + V_HEAD), BF16),
        shape((width, small.shape[1] - LANES), BF16), shape((KV_RANK // LANES, width, LANES), BF16),
    ]
    n = len(args)

    def kernel(*refs):
        attn_forward_kernel(
            heads, peers, score_scale, *refs[: n + 1], refs[n + 1 : n + 1 + peers], *refs[n + 1 + peers :],
            gain_at=gain_at,
        )

    return in_vmem(kernel, outs, [], 6 * 10**9, [*args, small, *mains])


def attn_backward(heads, peers, score_scale, gain_at, rows, args):
    group, width = args[1].shape
    query_w, output_t, expand_w, extra_w, latent_w = args[2:7]
    main = query_w.shape[1] + output_t.shape[1] + expand_w.shape[1]
    few = extra_w.shape[1] // LANES
    shape = jax.ShapeDtypeStruct
    outs = [shape((rows, main), BF16)] * peers + [
        shape((2 + few, width, LANES), BF16), shape((2 + few, width, LANES), BF16),
        shape((group // 2, width), BF16), shape((group // 2, width), BF16),
    ]
    scratch = [
        pltpu.VMEM((width, query_w.shape[1]), BF16),
        pltpu.VMEM((latent_w.shape[0] + few, width, LANES), BF16),
        pltpu.VMEM((group, heads * NOPE + 2 * LANES), BF16),
        pltpu.VMEM((group, KV_RANK), BF16),
        pltpu.VMEM((group, KV_RANK), F32),
    ]
    n = len(args)

    def kernel(*refs):
        attn_backward_kernel(heads, peers, score_scale, *refs[:n], refs[n : n + peers], *refs[n + peers :], gain_at=gain_at)

    outs = in_vmem(kernel, outs, scratch, 12 * 10**9, args)
    return outs[:peers], outs[peers:]


def ffn_kernel(
    local, segs_side, steps, width, crossed,
    first_ref, x0, x1, g0, g1, router, wg, wu, wd,
    dx_keep, dx_send, out_keep, out_send, x_all, g_all, hs_all, dg_all, du_all,
    acc_out, acc_dx, gates_s, dgates_s,
):
    j = pl.program_id(0)
    half = x0.shape[0]
    slot = half // 2
    block = wg.shape[0]
    x = jnp.concatenate([x0[...], x1[...]], axis=0)
    g_in = jnp.concatenate([g0[:, :width], g1[:, :width]], axis=0)
    first = first_ref[0]
    lane = lax.broadcasted_iota(jnp.int32, (1, LANES), 1)

    @pl.when(j == 0)
    def _():
        logits = mm(x, router[...])
        routed = jnp.concatenate([g0[:, width:], g1[:, width:]], axis=0) > 0
        masked = jnp.where(routed, logits, -1e30)
        raised = jnp.where(routed, jnp.exp(masked - jnp.max(masked, axis=1, keepdims=True)), 0.0)
        gates_s[...] = raised / jnp.sum(raised, axis=1, keepdims=True)
        dgates_s[...] = jnp.zeros_like(dgates_s)
        acc_out[...] = jnp.zeros_like(acc_out)
        acc_dx[...] = jnp.zeros_like(acc_dx)
        x_all[0] = x
        g_all[0] = g_in

    gates = gates_s[...]
    wanted, columns = [], []
    for part in range(2):
        seg = 2 * j + part
        expert = jnp.where(seg < 2 * segs_side, lax.rem(seg, segs_side) * local // segs_side, local)
        want = jnp.where(expert < local, first + expert, -1)
        column = jnp.sum(jnp.where(lane == want, gates, 0.0), axis=1, keepdims=True)
        wanted.append(want)
        columns.append(jnp.where(expert < local, column, 1.0))
    lane_block = lax.broadcasted_iota(jnp.int32, (1, block), 1)
    column = jnp.where(lane_block < LANES, columns[0], columns[1])
    gate, up, d_hidden = mm_t(x, wg[...]), mm_t(x, wu[...]), mm_t(g_in, wd[...])
    logistic = 1.0 / (1.0 + jnp.exp(-gate))
    silu = gate * logistic
    hidden = silu * up
    scaled = (hidden * column).astype(BF16)
    product = hidden * d_hidden
    for part in range(2):
        dots = jnp.sum(product[:, part * LANES : (part + 1) * LANES], axis=1, keepdims=True)
        dgates_s[...] += jnp.where(lane == wanted[part], dots, 0.0)
    d_hidden = d_hidden * column
    d_gate = (d_hidden * up * (logistic * (1.0 + gate * (1.0 - logistic)))).astype(BF16)
    d_up = (d_hidden * silu).astype(BF16)
    hs_all[0], dg_all[0], du_all[0] = scaled, d_gate, d_up
    acc_out[...] += mm(scaled, wd[...])
    acc_dx[...] += mm(d_gate, wg[...]) + mm(d_up, wu[...])

    @pl.when(j == steps - 1)
    def _():
        straight = [(dx_keep, 0, 0, half), (dx_send, 0, half, 2 * half)]
        across = [
            (out_keep, 0, 0, slot), (out_send, 0, slot, half),
            (out_keep, slot, half, half + slot), (out_send, slot, half + slot, 2 * half),
        ]
        if crossed:
            swap = {id(dx_keep): out_keep, id(dx_send): out_send, id(out_keep): dx_keep, id(out_send): dx_send}
            straight = [(swap[id(ref)], *at) for ref, *at in straight]
            across = [(swap[id(ref)], *at) for ref, *at in across]
        for ref, at, lo, hi in straight + across:
            if ref is dx_keep or ref is dx_send:
                ref[at : at + hi - lo, :width] = acc_dx[lo:hi].astype(BF16)
                ref[at : at + hi - lo, width:] = dgates_s[lo:hi].astype(BF16)
            else:
                ref[at : at + hi - lo] = acc_out[lo:hi].astype(BF16)


def ffn_tile(first, rows, grads, router, weights, local, call, calls, kept, crossed):
    half, width = rows[0].shape
    hid = weights.shape[1]
    block = 2 * LANES
    steps = hid // block
    segs_side = (hid // LANES - 2) // 2

    def fixed(*shape):
        return pl.BlockSpec(shape, lambda j: (0,) * len(shape), pipeline_mode=pl.Buffered(1))

    def whole(*shape):
        return pl.BlockSpec(shape, lambda j: (0,) * len(shape))

    in_specs = [
        pl.BlockSpec(memory_space=pltpu.SMEM),
        fixed(half, width), fixed(half, width), fixed(half, width + LANES), fixed(half, width + LANES), fixed(width, LANES),
        *(pl.BlockSpec((None, block, width), lambda j, i=i: (i, j, 0)) for i in range(3)),
    ]
    args = [first, *rows, *grads, router, weights, weights, weights]
    plain = len(args)
    aliases = {}
    if kept is not None:
        in_specs += [pl.BlockSpec(memory_space=pl.ANY)] * len(kept)
        args += list(kept)
        aliases = {plain + i: 4 + i for i in range(len(kept))}
    tile_rows = pl.BlockSpec((1, 2 * half, width), lambda j: (call, 0, 0))
    tile_hidden = pl.BlockSpec((1, 2 * half, block), lambda j: (call, 0, j))
    shape = jax.ShapeDtypeStruct
    out_shape = (
        [shape((half, width + LANES), BF16)] * 2
        + [shape((half, width), BF16)] * 2
        + [shape((calls, 2 * half, width), BF16)] * 2
        + [shape((calls, 2 * half, hid), BF16)] * 3
    )
    out_specs = [whole(half, width + LANES)] * 2 + [whole(half, width)] * 2 + [tile_rows] * 2 + [tile_hidden] * 3

    def kernel(*refs):
        ffn_kernel(local, segs_side, steps, width, crossed, *refs[:plain], *refs[len(args) :])

    outs = pl.pallas_call(
        kernel,
        grid=(steps,),
        in_specs=in_specs,
        out_specs=out_specs,
        out_shape=out_shape,
        scratch_shapes=[pltpu.VMEM((2 * half, width), F32)] * 2
        + [pltpu.VMEM((2 * half, LANES), F32)] * 2,
        input_output_aliases=aliases,
        compiler_params=pltpu.CompilerParams(
            vmem_limit_bytes=56 * 2**20, dimension_semantics=("arbitrary",)
        ),
        cost_estimate=pl.CostEstimate(
            flops=24 * half * width * hid,
            bytes_accessed=6 * width * hid + 16 * half * width,
            transcendentals=2 * half * hid,
        ),
    )(*args)
    return outs[:4], outs[4:]


def pack_experts(parts, seg, room):
    local, ff, width = parts[0].shape
    side = local * seg
    block = 2 * LANES
    shape = jax.ShapeDtypeStruct

    def kernel(gate, up, down, own, both):
        for i, ref in enumerate((gate, up, down)):
            for j in range(local):
                own[i, j * seg : j * seg + ff] = ref[j]
                own[i, j * seg + ff : (j + 1) * seg] = jnp.zeros((seg - ff, block), BF16)
        both[...] = own[...]

    return pl.pallas_call(
        kernel,
        grid=(width // block,),
        in_specs=[pl.BlockSpec((local, ff, block), lambda i: (0, 0, i))] * 3,
        out_specs=[pl.BlockSpec((3, side, block), lambda i: (0, 0, i))] * 2,
        out_shape=[shape((3, side, width), BF16), shape((3, 2 * side + room, width), BF16)],
        compiler_params=pltpu.CompilerParams(vmem_limit_bytes=40 * 2**20),
        cost_estimate=pl.CostEstimate(flops=0, bytes_accessed=30 * 2**20, transcendentals=0),
    )(*parts)


def join_pair(both, other, shared):
    _, side, width = other.shape
    high, wide = shared.shape[1], 8 * LANES
    blocks = side // high

    def kernel(other_ref, shared_ref, _, out):
        @pl.when(pl.program_id(1) < blocks)
        def _():
            out[...] = other_ref[...]

        @pl.when(pl.program_id(1) == blocks)
        def _():
            out[...] = shared_ref[...]

    return pl.pallas_call(
        kernel,
        grid=(width // wide, blocks + 1),
        in_specs=[
            pl.BlockSpec((3, high, wide), lambda i, r: (0, jnp.minimum(r, blocks - 1), i)),
            pl.BlockSpec((3, high, wide), lambda i, r: (0, 0, i)),
            pl.BlockSpec(memory_space=pl.ANY),
        ],
        out_specs=pl.BlockSpec((3, high, wide), lambda i, r: (0, blocks + r, i)),
        out_shape=jax.ShapeDtypeStruct(both.shape, both.dtype),
        input_output_aliases={2: 0},
        compiler_params=pltpu.CompilerParams(vmem_limit_bytes=40 * 2**20),
        cost_estimate=pl.CostEstimate(flops=0, bytes_accessed=22 * 2**20, transcendentals=0),
    )(other, shared, both)


def after(values, *first):
    return lax.optimization_barrier((values, *first))[0]


def body(
    tokens,
    segments,
    routes,
    cotangent,
    attn_gain,
    w_query,
    w_latent,
    latent_gain,
    w_expand,
    w_output,
    ffn_gain,
    w_router,
    w_shared_gate,
    w_shared_up,
    w_shared_down,
    w_expert_gate,
    w_expert_up,
    w_expert_down,
):
    own_rows, width = tokens.shape
    peers = lax.axis_size("expert")
    shards = lax.axis_size("shard")
    ring = peers // 2
    group_len = segments.shape[0]
    experts = w_router.shape[1]
    local, _, ff = w_expert_gate.shape
    rows_dev = w_query.shape[0]
    heads = w_query.shape[1] // (NOPE + ROPE)
    half = ROPE // 2
    rank_dev = w_expand.shape[0]
    expand_cols = w_expand.shape[1]
    value_cols = heads * V_HEAD
    query_cols = heads * (NOPE + ROPE)
    me_e = lax.axis_index("expert").astype(jnp.int32)
    me_s = lax.axis_index("shard").astype(jnp.int32)
    score_scale = (NOPE + ROPE) ** (-0.5)
    shared_dev = w_shared_gate.shape[1]
    shared = shared_dev // peers
    tables = routes_of(peers, shards)
    last = []

    def send(values, way):
        return lax.ppermute(values, BOTH, tables[way])

    def step(sends, work=None, *args):
        nonlocal last
        values, args = after(([v for v, _ in sends], args), last)
        got = [send(v, way) for v, (_, way) in zip(values, sends)]
        done = work(*args) if work else None
        last = [got, done]
        return (got, done) if work else got

    plane_e = [lax.rem(me_e // 2 + ring - k, ring) * 2 + lax.rem(me_e, 2) for k in range(ring)]
    piece_e = plane_e + [e ^ 1 for e in plane_e]
    shard_order = [me_s, me_s ^ 2, me_s ^ 1, me_s ^ 3]
    places = jnp.stack([*piece_e, *shard_order]).astype(jnp.int32)

    orders = (("y", "x"), ("x", "y"))
    zones = [list(range(k, min(k + 2, ring))) for k in range(0, ring, 2)]
    calls = 2 * len(zones)

    def zone_halves(planes):
        zone = jnp.stack(planes)
        n = zone.shape[1] // 2
        return [zone[:, i * n : (i + 1) * n].reshape(zone.shape[0] * n, zone.shape[2]) for i in range(2)]

    def firsts(halves):
        return [(half, one) for half, (one, _) in zip(halves, orders)]

    def nears(halves, got):
        return [jnp.concatenate([half, g], axis=0) for half, g in zip(halves, got)]

    def split_half(near):
        n = near.shape[0] // 2
        return near[:n], near[n:]

    few = pad_to(ROPE + experts + 3, LANES)
    latent_own = lax.dynamic_slice_in_dim(w_latent, me_s * LANES, LANES, 1)
    gain_cols = jnp.stack([attn_gain, ffn_gain, jnp.pad(latent_gain, (0, rows_dev - rank_dev))], axis=1)
    small = jnp.concatenate(
        [
            latent_own,
            w_latent[:, KV_RANK:],
            w_router,
            gain_cols,
            jnp.zeros((rows_dev, few - ROPE - experts - 3), BF16),
        ],
        axis=1,
    )
    q3 = w_query.reshape(rows_dev, heads, NOPE + ROPE)
    main = jnp.concatenate(
        [
            q3[..., :NOPE].reshape(rows_dev, -1),
            q3[..., NOPE : NOPE + half].reshape(rows_dev, -1),
            q3[..., NOPE + half :].reshape(rows_dev, -1),
            w_output.T,
            jnp.concatenate([w_expand[:, h * (NOPE + V_HEAD) : (h + 1) * (NOPE + V_HEAD)] for h in range(heads)], axis=0),
        ],
        axis=1,
    )
    seg = pad_to(ff, LANES)
    side = seg * local
    tail = pad_to(shared, LANES)
    expert_parts = [w_expert_gate.transpose(0, 2, 1), w_expert_up.transpose(0, 2, 1), w_expert_down]
    shared_pack = jnp.concatenate(
        [
            w_shared_gate.T.reshape(peers, shared, rows_dev),
            w_shared_up.T.reshape(peers, shared, rows_dev),
            w_shared_down.reshape(peers, shared, rows_dev),
        ],
        axis=1,
    )
    lane_experts = jnp.arange(experts, dtype=jnp.int32)
    routed_own = jnp.any(routes[:, :, None] == lane_experts[None, None, :], axis=1)
    grad_pack = jnp.concatenate(
        [cotangent, jnp.pad(routed_own.astype(BF16), ((0, 0), (0, LANES - experts)))], axis=1
    )

    def pack(*parts):
        return pack_experts(parts, seg, 2 * tail)

    main_own, main_other = [main], []
    got, (own_side, both_sides) = step(
        [(main, "ring"), (main, "y")] + [(small, k) for k in range(1, ring)], pack, *expert_parts
    )
    main_own.append(got[0])
    main_other.append(got[1])
    small_own = jnp.concatenate([small, *got[2:]], axis=0)
    shared_all = lax.all_to_all(after(shared_pack, got), "expert", 0, 0, tiled=True)
    shared_all = shared_all.transpose(1, 0, 2).reshape(3, shared, width)
    shared_own = jnp.pad(shared_all, ((0, 0), (0, tail - shared), (0, 0)))

    got = step([(main_own[1], "ring"), (main_own[1], "y"), (small_own, "y"), (tokens, "x"), (own_side, "pair")])
    main_own.append(got[0])
    main_other.append(got[1])
    small_all = jnp.concatenate([small_own, got[2]], axis=0)
    latent_all = small_all[:, :LANES]
    token_near = jnp.concatenate([tokens, got[3]], axis=0)
    other_side = got[4]

    got = step(
        [(main_own[2], "ring"), (main_own[2], "y"), (latent_all, "x"), (token_near, "pair"), (shared_own, "pair")]
    )
    main_own.append(got[0])
    main_other.append(got[1])
    latent_x = got[2]
    token_group = jnp.concatenate([token_near, got[3]], axis=0)
    shared_both = jnp.concatenate([shared_own, got[4]], axis=1)

    got, both_sides = step(
        [(main_own[3], "y"), (jnp.stack([latent_all, latent_x]), "pair"), (grad_pack, "ring")],
        join_pair, both_sides, other_side, shared_both,
    )
    main_other.append(got[0])
    latent_pair = got[1]
    grad_blocks = [grad_pack, got[2]]
    for k in range(4, ring):
        got = step([(main_own[k - 1], "ring")])
        main_own.append(got[0])
        got = step([(main_own[k], "y")])
        main_other.append(got[0])
    mains = main_own + main_other

    def by_group(values):
        return jnp.concatenate(
            [lax.dynamic_slice_in_dim(values, s * own_rows, own_rows, 0) for s in shard_order], axis=0
        )

    index = by_group(jnp.arange(group_len, dtype=jnp.int32))
    segment = by_group(segments)
    cos, sin = angles(by_group(positions(segments)), ROPE)
    cos, sin = jnp.tile(cos, (1, heads)), jnp.tile(sin, (1, heads))
    gain_at = ROPE + experts
    def attend(small_in, mains_in, *args):
        return attn_forward(heads, peers, score_scale, gain_at, list(args), small_in, mains_in)

    grad_halves = zone_halves(grad_blocks)
    got, outs = step(
        firsts(grad_halves) + [(grad_blocks[1], "ring")],
        attend, small_all, mains,
        places, token_group, latent_x, latent_pair, cos, sin,
        index[:, None], index[None, :], segment[:, None], segment[None, :],
    )
    grad_nears = nears(grad_halves, got)
    grad_blocks.append(got[2])
    saved, attn_weights = outs[2:10], outs[12:]
    gain_attn, gain_ffn, gain_latent = outs[10][0:1], outs[10][1:2], outs[11]
    router_w = outs[15][:, ROPE : ROPE + experts]
    got = step([(outs[1], "pair")])
    keep, away = split_half(add(outs[0], got[0]))
    got = step([(away, "x"), (grad_blocks[2], "ring")])
    attn_term = keep.astype(F32) + got[0].astype(F32)
    grad_blocks.append(got[1])
    own_float = tokens.astype(F32)
    hidden_one = own_float + attn_term
    scale_ffn = inverse_rms(hidden_one)
    normed_ffn = (hidden_one * scale_ffn * gain_ffn).astype(BF16)
    logits = mm(normed_ffn, router_w)
    masked = jnp.where(routed_own, logits, -1e30)
    lifted = jnp.where(routed_own, jnp.exp(masked - jnp.max(masked, axis=1, keepdims=True)), 0.0)
    gates = lifted / jnp.sum(lifted, axis=1, keepdims=True)

    router_pad = jnp.pad(router_w, ((0, 0), (0, LANES - experts)))
    first_expert = (me_e * local).reshape(1)
    row_blocks = [normed_ffn]
    got = step([(normed_ffn, "ring")] + [(near, two) for near, (_, two) in zip(grad_nears, orders)])
    row_blocks.append(got[0])
    grad_tiles = {0: list(zip(grad_nears, got[1:]))}
    row_halves = zone_halves(row_blocks)
    got = step(firsts(row_halves) + [(row_blocks[1], "ring")])
    row_nears = nears(row_halves, got)
    row_blocks.append(got[2])
    got = step([(near, two) for near, (_, two) in zip(row_nears, orders)] + [(row_blocks[2], "ring")])
    row_tiles = {0: list(zip(row_nears, got))}
    row_blocks.append(got[2])

    kept = None
    dx, dx_near, dx_home, outs_of, out_near, out_home = {}, {}, {}, {}, {}, {}
    for_pair, from_pair = [], []

    def ways(call):
        one, two = orders[call % 2]
        return (two, one) if call == calls - 1 else (one, two)

    def moves(jobs):
        sends = []
        for what, call, stage in jobs:
            one, two = ways(call)
            if what == "out":
                one, two = two, one
            parts, near = (dx, dx_near) if what == "dx" else (outs_of, out_near)
            sends.append((parts[call][1], one) if stage == 1 else (split_half(near[call])[1], two))

        def arrived(got):
            for (what, call, stage), g in zip(jobs, got):
                parts, near, home = (dx, dx_near, dx_home) if what == "dx" else (outs_of, out_near, out_home)
                if stage == 1:
                    near[call] = add(parts[call][0], g)
                else:
                    home[call] = add(split_half(near[call])[0], g)

        return sends, arrived

    for call in range(calls):
        i, turn = call // 2, call % 2
        more = i + 1 < len(zones)
        sends, jobs = [], []
        if turn == 0 and more:
            row_halves = zone_halves([row_blocks[k] for k in zones[i + 1]])
            grad_halves = zone_halves([grad_blocks[k] for k in zones[i + 1]])
            sends += firsts(row_halves) + firsts(grad_halves)
        if turn == 1 and more:
            sends += [(near, two) for near, (_, two) in zip(row_nears, orders)] + [(grad_nears[0], orders[0][1])]
        if turn == 0 and i > 0:
            sends += [(grad_last, orders[1][1])]
        if len(row_blocks) < ring:
            sends += [(row_blocks[-1], "ring"), (grad_blocks[-1], "ring")]
        if call >= 1:
            jobs.append(("dx", call - 1, 1))
        if call >= 2:
            jobs.append(("dx", call - 2, 2))
        if call >= 3:
            jobs.append(("out", call - 3, 1))
        if call >= 4:
            jobs.append(("out", call - 4, 2))
        moved, arrived = moves(jobs)

        def tile(rows, grads, kept_in, call=call):
            return ffn_tile(
                first_expert, rows, grads, router_pad, both_sides, local, call, calls, kept_in, call < calls - 1
            )

        if turn == 1:
            grads = grad_tiles[i][1]
        else:
            grads = grad_tiles[i][0]
        got, (outs, kept) = step(moved + sends, tile, row_tiles[i][turn], grads, kept)
        arrived(got[: len(moved)])
        got = got[len(moved) :]
        dx[call], outs_of[call] = outs[:2], outs[2:4]
        if turn == 0 and i > 0:
            grad_tiles[i].append((grad_last, got[2 * len(orders) if more else 0]))
        if turn == 0 and more:
            row_nears = nears(row_halves, got[:2])
            grad_nears = nears(grad_halves, got[2:4])
        if turn == 1 and more:
            row_tiles[i + 1] = list(zip(row_nears, got[:2]))
            grad_tiles[i + 1] = [(grad_nears[0], got[2])]
            grad_last = grad_nears[1]
        if len(row_blocks) < ring:
            row_blocks.append(got[-2])
            grad_blocks.append(got[-1])

    def planes_of(home, zone_list, turns):
        return {
            (k, turn): home[2 * i + turn].reshape(len(zones[i]), -1, home[2 * i + turn].shape[1])[j]
            for i in zone_list
            for j, k in enumerate(zones[i])
            for turn in turns
        }

    def weight_part(d, v):
        return t_mm(d.reshape(-1, d.shape[-1])[:, side:], v.reshape(-1, v.shape[-1])).astype(BF16)

    x_all, g_all, hs_all, dg_all, du_all = kept
    end = calls - 1
    early = planes_of(dx_home, range(len(zones) - 1), range(2))
    early_keys = [key for key in early if key[0] > 0]
    jobs = [("dx", end, 1), ("dx", end - 1, 2)]
    moved, arrived = moves(jobs)
    got, part = step(moved + [(early[key], -key[0]) for key in early_keys], weight_part, dg_all, x_all)
    arrived(got)
    ring_terms = {turn: [early[(0, turn)]] for turn in range(2)}
    for key, g in zip(early_keys, got[2:]):
        ring_terms[key[1]].append(g)
    for_pair.append(part)

    a_late = planes_of(dx_home, [len(zones) - 1], [0])
    moved, arrived = moves([("dx", end, 2)])
    got, part = step(
        moved + [(v, -k) for (k, _), v in a_late.items()] + [(for_pair[0], "pair")], weight_part, du_all, x_all
    )
    arrived(got)
    ring_terms[0] += got[1:-1]
    from_pair.append(got[-1])
    for_pair.append(part)

    b_late = planes_of(dx_home, [len(zones) - 1], [1])
    moved, arrived = moves([("out", end - 3, 2), ("out", end - 1, 1)])
    got, part = step(
        [(v, -k) for (k, _), v in b_late.items()] + [(for_pair[1], "pair")] + moved, weight_part, hs_all, g_all
    )
    ring_terms[1] += got[: len(b_late)]
    from_pair.append(got[len(b_late)])
    arrived(got[len(b_late) + 1 :])
    for_pair.append(part)

    def summed(terms):
        total = terms[0].astype(F32)
        for term in terms[1:]:
            total = total + term.astype(F32)
        return total

    d_rows = jnp.concatenate([summed(ring_terms[turn]) for turn in range(2)], axis=0)
    d_normed = d_rows[:, :width]
    d_gates = d_rows[:, width : width + experts]
    grad_in = cotangent.astype(F32)
    d_logits = (gates * (d_gates - jnp.sum(gates * d_gates, axis=1, keepdims=True))).astype(BF16)
    d_normed = d_normed + mm_t(d_logits, router_w)
    d_norm, grad_gain_ffn = norm_back(hidden_one, scale_ffn, gain_ffn, d_normed)
    d_hidden_one = grad_in + d_norm
    d_attn_own = d_hidden_one.astype(BF16)
    moved, arrived = moves([("out", end - 2, 1)])
    got = step([(d_attn_own, "x"), (for_pair[2], "pair")] + moved)
    d_near = jnp.concatenate([d_attn_own, got[0]], axis=0)
    from_pair.append(got[1])
    arrived(got[2:])
    got = step([(d_near, "pair")])
    d_attn_group = jnp.concatenate([d_near, got[0]], axis=0)
    shared_back = jnp.concatenate(
        [
            add(own[side : side + shared], g[side + tail : side + tail + shared]).reshape(shared, peers, rows_dev)
            for own, g in zip(for_pair, from_pair)
        ],
        axis=0,
    ).transpose(1, 0, 2)

    def attend_back(*args):
        return attn_backward(heads, peers, score_scale, gain_at, rows_dev, list(args))

    waiting = [("out", end, 1)]
    waiting += [("out", call, 2) for call in range(calls) if call not in out_home and call in out_near]
    waiting += [("out", call, 1) for call in range(calls) if call not in out_near and call != end]
    moved, arrived = moves(waiting)
    got, (g_mains, (near_keep, near_send, d_in_keep, d_in_send)) = step(
        moved, attend_back,
        places, d_attn_group, *attn_weights, gain_latent, cos, sin, *saved, normed_ffn,
        jnp.pad(d_logits, ((0, 0), (ROPE, few - ROPE - experts))), token_group, grad_gain_ffn.reshape(1, width),
    )
    arrived(got)
    waiting = [("out", call, 2) for call in range(calls) if call not in out_home]

    def own_part(d, v, g):
        return t_mm(d.reshape(-1, d.shape[-1])[:, :side], v.reshape(-1, v.shape[-1])) + g[:side].astype(F32)

    parts = {}

    def mains_y(k):
        return (g_mains[ring + k], "y")

    order = [*range(1, ring), 0]
    moved, arrived = moves(waiting)
    got, grad_gate = step(
        [mains_y(order[0]), (near_send, "pair"), (d_in_send, "pair")] + moved, own_part, dg_all, x_all, from_pair[0]
    )
    total = add(g_mains[order[0]], got[0])
    near = add(near_keep, got[1])
    keep, d_away = split_half(add(d_in_keep, got[2]))
    arrived(got[3:])
    out_planes = planes_of(out_home, range(len(zones)), range(2))
    out_rows = [jnp.concatenate([out_planes[(k, turn)] for turn in range(2)], axis=0) for k in range(ring)]
    out_terms = [out_rows[0]]

    few_away = jnp.concatenate([near[1:2], near[2:]], axis=0)
    few_keep = jnp.concatenate([near[0:1], near[2:]], axis=0)
    got, grad_up = step(
        [mains_y(order[1]), (total, "ring"), (few_away, "x"), (d_away, "x"), (out_rows[1], -1)],
        own_part, du_all, x_all, from_pair[1],
    )
    total = add(add(g_mains[order[1]], got[0]), got[1])
    few_sum = add(few_keep, got[2])
    few_sum = jnp.concatenate([few_sum[j] for j in range(few_sum.shape[0])], axis=1)
    d_normed_in = keep.astype(F32) + got[3].astype(F32)
    out_terms.append(got[4])

    few_half = few_sum.shape[0] // 2
    got, grad_down = step(
        [mains_y(order[2]), (total, "ring"), (few_sum[few_half:], "y")], own_part, hs_all, g_all, from_pair[2]
    )
    total = add(add(g_mains[order[2]], got[0]), got[1])
    few_sum = add(few_sum[:few_half], got[2])
    few_planes = [few_sum[k * rows_dev : (k + 1) * rows_dev] for k in range(ring)]
    shared_home = lax.all_to_all(after(shared_back, got), "expert", 0, 0, tiled=True).astype(F32)

    got = step([mains_y(order[3]), (total, "ring"), *((few_planes[k], -k) for k in range(1, ring))])
    total = add(add(g_mains[order[3]], got[0]), got[1])
    few_home = summed([few_planes[0], *got[2:]])
    latent_home = few_home[:, :LANES].astype(BF16)
    for j in order[4:]:
        got = step([mains_y(j), (total, "ring")])
        total = add(add(g_mains[j], got[0]), got[1])
    home = total.astype(F32)

    got = step([(latent_home, "x")] + [(out_rows[k], -k) for k in range(2, ring)])
    latent_two = jnp.stack([latent_home, got[0]])
    block_out = (hidden_one + summed(out_terms + got[1:])).astype(BF16)
    got = step([(latent_two, "pair")])
    latent_four = jnp.concatenate([latent_two, got[0]], axis=0)
    grad_latent = jnp.zeros((shards, rows_dev, LANES), BF16)
    for r in range(shards):
        grad_latent = lax.dynamic_update_slice_in_dim(grad_latent, latent_four[r : r + 1], shard_order[r], 0)
    grad_latent = jnp.concatenate([*(grad_latent[j] for j in range(shards)), few_home[:, LANES : LANES + ROPE].astype(BF16)], axis=1)
    grad_router = few_home[:, LANES + ROPE : LANES + ROPE + experts].astype(F32)
    d_token, _ = norm_back(own_float, inverse_rms(own_float), gain_attn, d_normed_in)
    tokens_grad = d_hidden_one + d_token
    gain_home = few_home[:, LANES + gain_at : LANES + gain_at + 3].astype(F32).T

    grad_experts = [
        jnp.stack([g[j * seg : j * seg + ff] for j in range(local)]) for g in (grad_gate, grad_up, grad_down)
    ]
    grad_shared = [shared_home[:, i * shared : (i + 1) * shared].reshape(shared_dev, rows_dev) for i in range(3)]

    nope_cols = heads * NOPE
    rope_cols = heads * half
    gq = home[:, :query_cols]
    grad_query_own = jnp.concatenate(
        [
            gq[:, :nope_cols].reshape(rows_dev, heads, NOPE),
            gq[:, nope_cols : nope_cols + rope_cols].reshape(rows_dev, heads, half),
            gq[:, nope_cols + rope_cols :].reshape(rows_dev, heads, half),
        ],
        axis=2,
    ).reshape(rows_dev, query_cols)
    g_expand = home[:, query_cols + value_cols :]
    return (
        block_out,
        tokens_grad,
        gain_home[0],
        grad_query_own,
        grad_latent.astype(F32),
        gain_home[2, :rank_dev],
        jnp.concatenate([g_expand[h * rank_dev : (h + 1) * rank_dev] for h in range(heads)], axis=1),
        home[:, query_cols : query_cols + value_cols].T,
        gain_home[1],
        grad_router,
        grad_shared[0].T,
        grad_shared[1].T,
        grad_shared[2],
        grad_experts[0].transpose(0, 2, 1),
        grad_experts[1].transpose(0, 2, 1),
        grad_experts[2],
    )


def solution(mesh):
    rows = P(("expert", "shard"), None)
    return jax.shard_map(
        body,
        mesh=mesh,
        in_specs=(
            rows,
            P("expert"),
            rows,
            rows,
            P("expert"),
            P("expert", "shard"),
            P("expert", None),
            P("expert"),
            P("expert", "shard"),
            P("shard", "expert"),
            P("expert"),
            P("expert", None),
            P("expert", "shard"),
            P("expert", "shard"),
            P("shard", "expert"),
            P("expert", None, "shard"),
            P("expert", None, "shard"),
            P("expert", "shard", None),
        ),
        out_specs=(
            rows,
            rows,
            P("expert"),
            P("expert", "shard"),
            P("expert", None),
            P("expert"),
            P("expert", "shard"),
            P("shard", "expert"),
            P("expert"),
            P("expert", None),
            P("expert", "shard"),
            P("expert", "shard"),
            P("shard", "expert"),
            P("expert", None, "shard"),
            P("expert", None, "shard"),
            P("expert", "shard", None),
        ),
        check_vma=False,
    )
```

time: 902 us -> 802 us (0.89)
  local copies, waits for them, and re-layouts: 159 us -> 72 us
  Pallas kernels: 154 us -> 227 us
  matrix products: 123 us -> 67.8 us
  other arithmetic: 103 us -> 54.4 us
  starting transfers between devices: 83.7 us -> 110 us
  waiting for transfers between devices: 243 us -> 260 us
  between operations: 16.8 us -> 3.04 us
    pallas_call x4 -> x8, Pallas kernels: 154 us -> 227 us  [the longest x4 155 us: ffn_tile(): pl.pallas_call(kernel, grid=(steps,), in_specs=in_specs, out_specs=out_sp...]
    ppermute x72 -> x88, waiting for transfers between devices: 200 us -> 245 us  [send(): return lax.ppermute(values, BOTH, tables[way])]
    unnamed x3 -> x0, waiting for transfers between devices: 42.6 us -> none
    dot_general x21 -> x8, matrix products: 105 us -> 67.8 us  [dot(): return lax.dot_general(a, b, (dims, ((), ())), preferred_element_type=F32)]
    concatenate x18 -> x22, other arithmetic: 45.7 us -> 12.9 us  [the longest x8 2.78 us: nears(): return [jnp.concatenate([half, g], axis=0) for half, g in zip(halves, got)]]
    ppermute x72 -> x88, starting transfers between devices: 74.9 us -> 98.7 us  [send(): return lax.ppermute(values, BOTH, tables[way])]
    dot_general x9 -> x0, matrix products: 18.1 us -> none  [es(): return jnp.einsum(spec, *values, preferred_element_type=F32)]
    unnamed x302 -> x244, local copies, waits for them, and re-layouts: 48.1 us -> 30.2 us
  transfers between devices with their start and end apart: 76 -> 90, of which waited for: 22 -> 32; matrix products, arithmetic and copies ran while one was open for 40% -> 19% of each run, Pallas kernels for 17% -> 29%
where the time goes in v3:
time: 802 us; the launch traced here: 794 us
  waiting for transfers between devices  260 us (32%)
  Pallas kernels  227 us (28%)
  starting transfers between devices  110 us (14%)
  local copies, waits for them, and re-layouts  72 us (9%)
  matrix products  67.8 us (8%)
  other arithmetic  54.4 us (7%)
    ppermute x88, waiting for transfers between devices, send(): return lax.ppermute(values, BOTH, tables[way])  245 us
    pallas_call x4, Pallas kernels, ffn_tile(): pl.pallas_call(kernel, grid=(steps,), in_specs=in_specs, out_specs=out_sp...  155 us
    ppermute x88, starting transfers between devices, send(): return lax.ppermute(values, BOTH, tables[way])  98.7 us
    dot_general x8, matrix products, dot(): return lax.dot_general(a, b, (dims, ((), ())), preferred_element_type=F32)  67.8 us
    pallas_call x2, Pallas kernels, in_vmem(): pl.pallas_call(kernel, in_specs=[pl.BlockSpec(memory_space=pltpu.SMEM)] +...  51.7 us
    unnamed x244, local copies, waits for them, and re-layouts  30.2 us
  transfers between devices with their start and end apart: 90, of which 32 were waited for; matrix products, arithmetic and copies ran while one was open for 19% of the time, Pallas kernels for 29%

profile of v3, /device:TPU:1, one launch (start us, length us, event | category | flops | bytes accessed | tf_op | source)
XLA Modules:
  0.0 794.5 jit_solution(2210717474403943503)
XLA Ops:
  67.0 15.1 %collective-permute-done.6 = bf16[1024,256]{1,0:T(8,128)(2,1)S(1)} collective-permute-done((bf16[1024,256]{1,0:T(8,128)(2,1)S(1)}, bf16[1024,256]{1,0:T(8,128)(2,1)S(1)}, u32[]{:S(2)}, u32[]{:S(2)}) %collective-permute-start.6) | collective-permute-done | bytes 524320 | tf_op jit(solution)/shard_map/ppermute | solution.py:586
  85.5 14.7 %all-to-all-done = bf16[8,264,256]{2,1,0:T(8,128)(2,1)S(1)} async-done(((bf16[8,264,256]{2,1,0:T(8,128)(2,1)}), bf16[8,264,256]{2,1,0:T(8,128)(2,1)S(1)}, u32[]{:S(2)}, u32[]{:S(2)}) %all-to-all-start) | async-done | bytes 1081376 | tf_op jit(solution)/shard_map/all_to_all | solution.py:672
  112.2 9.8 %collective-permute-done.11.refs_2_ = bf16[2048,128]{1,0:T(8,128)(2,1)} collective-permute-done((bf16[2048,128]{1,0:T(8,128)(2,1)}, bf16[2048,128]{1,0:T(8,128)(2,1)}, u32[]{:S(2)}, u32[]{:S(2)}) %collective-permute-start.11) | collective-permute-done | bytes 524320 | tf_op jit(solution)/shard_map/ppermute | solution.py:586
  134.5 12.3 %shard_map.298.refs_6_.refs_7_.refs_8_ = bf16[3,1792,2048]{2,1,0:T(8,128)(2,1)} custom-call(bf16[3,768,2048]{2,1,0:T(8,128)(2,1)} %collective-permute-done.9.other_ref, bf16[3,256,2048]{2,1,0:T(8,128)(2,1)S(1)} %pad_maximum_fusion.1.shared_ref, bf16[3,1792,2048]{2,1,0:T(8,128)(2,1)} %get-tuple-element.292._), custom_call_target="tpu_custom_call", output_to_operand_aliasing={{}: (2, {})} | custom-call | bytes 23068672 | tf_op jit(solution)/shard_map/pallas_call | solution.py:523
  157.5 21.6 %shard_map.299 = (bf16[256,2048]{1,0:T(8,128)(2,1)}, bf16[256,2048]{1,0:T(8,128)(2,1)}, bf16[512,2048]{1,0:T(8,128)(2,1)}, bf16[512,768]{1,0:T(8,128)(2,1)}, bf1...) custom-call(s32[12]{0:T(128)} %stack.150.refs_0_, ...), custom_call_target="tpu_custom_call" | custom-call | flops 6000000000 | bytes 25165824 | tf_op jit(solution)/shard_map/pallas_call | solution.py:290
  204.2 13.3 %collective-permute-done.24 = bf16[128,2048]{1,0:T(8,128)(2,1)S(1)} collective-permute-done((bf16[128,2048]{1,0:T(8,128)(2,1)S(1)}, bf16[128,2048]{1,0:T(8,128)(2,1)S(1)}, u32[]{:S(2)}, u32[]{:S(2)}) %collective-permute-start.24) | collective-permute-done | bytes 524320 | tf_op jit(solution)/shard_map/ppermute | solution.py:586
  217.5 10.4 %collective-permute-done.25.refs_4_ = bf16[256,2176]{1,0:T(8,128)(2,1)S(1)} collective-permute-done((bf16[256,2176]{1,0:T(8,128)(2,1)S(1)}, bf16[256,2176]{1,0:T(8,128)(2,1)S(1)}, u32[]{:S(2)}, u32[]{:S(2)}) %collective-permute-start.25) | collective-permute-done | bytes 1114144 | tf_op jit(solution)/shard_map/ppermute | solution.py:586
  266.6 39.0 %shard_map.300 = (bf16[256,2176]{1,0:T(8,128)(2,1)}, bf16[256,2176]{1,0:T(8,128)(2,1)}, bf16[256,2048]{1,0:T(8,128)(2,1)}, bf16[256,2048]{1,0:T(8,128)(2,1)}, bf...) custom-call(s32[1]{0:T(128)} %bitcast.37.refs_0_, ...), custom_call_target="tpu_custom_call" | custom-call | flops 22548578304 | bytes 30408704 | tf_op jit(solution)/shard_map/pallas_call | solution.py:464
  309.1 38.9 %shard_map.301 = (bf16[256,2176]{1,0:T(8,128)(2,1)}, bf16[256,2176]{1,0:T(8,128)(2,1)}, bf16[256,2048]{1,0:T(8,128)(2,1)}, bf16[256,2048]{1,0:T(8,128)(2,1)}, bf...) custom-call(s32[1]{0:T(128)} %bitcast.37.refs_0_, ...), custom_call_target="tpu_custom_call", output_to_operand_aliasing={{4}: (9, {}), {5}: (10, {}), {6}: (11, {}), {7}: (12, {}), ... | custom-call | flops 22548578304 | bytes 30408704 | tf_op jit(solution)/shard_map/pallas_call | solution.py:464
  352.7 38.7 %shard_map.302 = (bf16[256,2176]{1,0:T(8,128)(2,1)}, bf16[256,2176]{1,0:T(8,128)(2,1)}, bf16[256,2048]{1,0:T(8,128)(2,1)}, bf16[256,2048]{1,0:T(8,128)(2,1)}, bf...) custom-call(s32[1]{0:T(128)} %bitcast.37.refs_0_, ...), custom_call_target="tpu_custom_call", output_to_operand_aliasing={{4}: (9, {}), {5}: (10, {}), {6}: (11, {}), {7}: (12, {}), ... | custom-call | flops 22548578304 | bytes 30408704 | tf_op jit(solution)/shard_map/pallas_call | solution.py:464
  395.4 38.7 %shard_map.303 = (bf16[256,2176]{1,0:T(8,128)(2,1)}, bf16[256,2176]{1,0:T(8,128)(2,1)}, bf16[256,2048]{1,0:T(8,128)(2,1)}, bf16[256,2048]{1,0:T(8,128)(2,1)}, bf...) custom-call(s32[1]{0:T(128)} %bitcast.37.refs_0_, ...), custom_call_target="tpu_custom_call", output_to_operand_aliasing={{4}: (9, {}), {5}: (10, {}), {6}: (11, {}), {7}: (12, {}), ... | custom-call | flops 22548578304 | bytes 30408704 | tf_op jit(solution)/shard_map/pallas_call | solution.py:464
  439.5 12.5 %fusion.6 = bf16[1024,2048]{1,0:T(8,128)(2,1)} fusion(bf16[2048,2048]{1,0:T(8,128)(2,1)S(1)} %bitcast.150, bf16[2048,1792]{1,0:T(8,128)(2,1)} %bitcast.165), kind=kOutput, calls=%fused_computation.12 | convolution fusion | flops 8592031744 | bytes 16777216 | tf_op jit(solution)/shard_map/dot_general | solution.py:52
  453.6 11.5 %collective-permute-start.54 = (bf16[1024,2048]{1,0:T(8,128)(2,1)}, bf16[1024,2048]{1,0:T(8,128)(2,1)}, u32[]{:S(2)}, u32[]{:S(2)}) collective-permute-start(bf16[1024,2048]{1,0:T(8,128)(2,1)} %fusion.6), channel_id=1, source_target_pairs={{0,1},{1,0},{2,3},{3,2},{4,5},{5,4},{6,7},{7,6},{8,9},{9,8},{10,11... | collective-permute-start | bytes 12582920 | tf_op jit(solution)/shard_map/ppermute | solution.py:586
  468.2 12.8 %fusion.9 = bf16[1024,2048]{1,0:T(8,128)(2,1)} fusion(bf16[2048,2048]{1,0:T(8,128)(2,1)S(1)} %bitcast.151, bf16[2048,1792]{1,0:T(8,128)(2,1)} %bitcast.167), kind=kOutput, calls=%fused_computation.13 | convolution fusion | flops 8592031744 | bytes 16777216 | tf_op jit(solution)/shard_map/dot_general | solution.py:52
  490.3 11.3 %fusion.12 = bf16[1024,2048]{1,0:T(8,128)(2,1)} fusion(bf16[2048,2048]{1,0:T(8,128)(2,1)S(1)} %bitcast.157, bf16[2048,1792]{1,0:T(8,128)(2,1)S(1)} %bitcast.164), kind=kOutput, calls=%fused_computation.14 | convolution fusion | flops 8592031744 | bytes 16777216 | tf_op jit(solution)/shard_map/dot_general | solution.py:52
  531.0 11.4 %collective-permute-done.60 = bf16[256,2048]{1,0:T(8,128)(2,1)S(1)} collective-permute-done((bf16[256,2048]{1,0:T(8,128)(2,1)S(1)}, bf16[256,2048]{1,0:T(8,128)(2,1)S(1)}, u32[]{:S(2)}, u32[]{:S(2)}) %collective-permute-start.60) | collective-permute-done | bytes 1048608 | tf_op jit(solution)/shard_map/ppermute | solution.py:586
  553.0 30.1 %shard_map.304 = (bf16[256,1536]{1,0:T(8,128)(2,1)}, bf16[256,1536]{1,0:T(8,128)(2,1)}, bf16[256,1536]{1,0:T(8,128)(2,1)}, bf16[256,1536]{1,0:T(8,128)(2,1)}, bf...) custom-call(s32[12]{0:T(128)} %stack.150.refs_0_, ...), custom_call_target="tpu_custom_call" | custom-call | flops 12000000000 | bytes 25165824 | tf_op jit(solution)/shard_map/pallas_call | solution.py:290
  592.3 11.1 %convert_add_fusion.2 = f32[768,2048]{1,0:T(8,128)S(1)} fusion(bf16[2048,2048]{1,0:T(8,128)(2,1)} %bitcast.149, bf16[2048,1792]{1,0:T(8,128)(2,1)} %bitcast.166, bf16[1024,2048]{1,0:T(8,128)(2,1)} %collective-permute-done.54), kind=kOutput, calls=%fused_computation.2 | convolution fusion | flops 6445596672 | bytes 20971520 | tf_op jit(solution)/shard_map/dot_general | solution.py:52
  607.0 13.7 %collective-permute-done.70 = bf16[128,2048]{1,0:T(8,128)(2,1)S(1)} collective-permute-done((bf16[128,2048]{1,0:T(8,128)(2,1)S(1)}, bf16[128,2048]{1,0:T(8,128)(2,1)S(1)}, u32[]{:S(2)}, u32[]{:S(2)}) %collective-permute-start.70) | collective-permute-done | bytes 524320 | tf_op jit(solution)/shard_map/ppermute | solution.py:586
  643.8 15.5 %collective-permute-done.75 = bf16[128,2048]{1,0:T(8,128)(2,1)S(1)} collective-permute-done((bf16[128,2048]{1,0:T(8,128)(2,1)S(1)}, bf16[128,2048]{1,0:T(8,128)(2,1)S(1)}, u32[]{:S(2)}, u32[]{:S(2)}) %collective-permute-start.75) | collective-permute-done | bytes 524320 | tf_op jit(solution)/shard_map/ppermute | solution.py:586
  677.5 13.8 %collective-permute-done.76 = bf16[1024,256]{1,0:T(8,128)(2,1)S(1)} collective-permute-done((bf16[1024,256]{1,0:T(8,128)(2,1)S(1)}, bf16[1024,256]{1,0:T(8,128)(2,1)S(1)}, u32[]{:S(2)}, u32[]{:S(2)}) %collective-permute-start.76) | collective-permute-done | bytes 524320 | tf_op jit(solution)/shard_map/ppermute | solution.py:586
  711.2 21.7 %collective-permute-done.82 = bf16[256,1536]{1,0:T(8,128)(2,1)} collective-permute-done((bf16[256,1536]{1,0:T(8,128)(2,1)}, bf16[256,1536]{1,0:T(8,128)(2,1)}, u32[]{:S(2)}, u32[]{:S(2)}) %collective-permute-start.82) | collective-permute-done | bytes 786464 | tf_op jit(solution)/shard_map/ppermute | solution.py:586
  743.7 9.8 %collective-permute-start.84 = (bf16[128,2048]{1,0:T(8,128)(2,1)}, bf16[128,2048]{1,0:T(8,128)(2,1)}, u32[]{:S(2)}, u32[]{:S(2)}) collective-permute-start(bf16[128,2048]{1,0:T(8,128)(2,1)} %pad_maximum_fusion.24), channel_id=1, source_target_pairs={{0,16},{1,17},{2,18},{3,19},{4,20},{5,21},{6,22},{7,23},{8,24},{9,... | collective-permute-start | bytes 1572872 | tf_op jit(solution)/shard_map/ppermute | solution.py:586
  764.5 24.0 %collective-permute-done.84 = bf16[128,2048]{1,0:T(8,128)(2,1)} collective-permute-done((bf16[128,2048]{1,0:T(8,128)(2,1)}, bf16[128,2048]{1,0:T(8,128)(2,1)}, u32[]{:S(2)}, u32[]{:S(2)}) %collective-permute-start.84) | collective-permute-done | bytes 524320 | tf_op jit(solution)/shard_map/ppermute | solution.py:586
  (605 shorter events, 339.6 us)
Async XLA Ops:
  48.9 54.6 %collective-permute-start.9 = (bf16[3,768,2048]{2,1,0:T(8,128)(2,1)}, bf16[3,768,2048]{2,1,0:T(8,128)(2,1)}, u32[]{:S(2)}, u32[]{:S(2)}) collective-permute-start(bf16[3,768,2048]{2,1,0:T(8,128)(2,1)} %get-tuple-element.281), channel_id=1, source_target_pairs={{0,1},{1,0},{2,3},{3,2},{4,5},{5,4},{6,7},{7,6},{8,9},{9,8},{10,11... | collective-permute-start | bytes 28311560 | tf_op jit(solution)/shard_map/ppermute | solution.py:586
  52.3 47.9 %all-to-all-start = ((bf16[8,264,256]{2,1,0:T(8,128)(2,1)}), bf16[8,264,256]{2,1,0:T(8,128)(2,1)S(1)}, u32[]{:S(2)}, u32[]{:S(2)}) async-start(bf16[8,264,256]{2,1,0:T(8,128)(2,1)} %pad_maximum_fusion.7), calls=%async_computation | async-start | bytes 2162688 | tf_op jit(solution)/shard_map/all_to_all | solution.py:672
  65.5 37.9 %collective-permute-start.5 = (bf16[256,1536]{1,0:T(8,128)(2,1)}, bf16[256,1536]{1,0:T(8,128)(2,1)}, u32[]{:S(2)}, u32[]{:S(2)}) collective-permute-start(bf16[256,1536]{1,0:T(8,128)(2,1)} %copy-done.97), channel_id=1, source_target_pairs={{0,8},{1,9},{2,10},{3,11},{4,12},{5,13},{6,14},{7,15},{8,16},{9,17... | collective-permute-start | bytes 2359304 | tf_op jit(solution)/shard_map/ppermute | solution.py:586
  66.7 36.7 %collective-permute-start.8 = (bf16[256,1536]{1,0:T(8,128)(2,1)}, bf16[256,1536]{1,0:T(8,128)(2,1)}, u32[]{:S(2)}, u32[]{:S(2)}) collective-permute-start(bf16[256,1536]{1,0:T(8,128)(2,1)} %copy-done.97), channel_id=1, source_target_pairs={{0,4},{1,5},{2,6},{3,7},{4,0},{5,1},{6,2},{7,3},{8,12},{9,13},{10,... | collective-permute-start | bytes 2359304 | tf_op jit(solution)/shard_map/ppermute | solution.py:586
  263.7 42.4 %collective-permute-start.36 = (bf16[128,2176]{1,0:T(8,128)(2,1)S(1)}, bf16[128,2176]{1,0:T(8,128)(2,1)S(1)}, u32[]{:S(2)}, u32[]{:S(2)}) collective-permute-start(bf16[128,2176]{1,0:T(8,128)(2,1)S(1)} %bitcast.175), channel_id=1, source_target_pairs={{0,2},{1,3},{2,0},{3,1},{4,6},{5,7},{6,4},{7,5},{8,10},{9,11},{10,... | collective-permute-start | bytes 1671176 | tf_op jit(solution)/shard_map/ppermute | solution.py:586
  264.6 41.3 %collective-permute-start.35 = (bf16[128,2176]{1,0:T(8,128)(2,1)S(1)}, bf16[128,2176]{1,0:T(8,128)(2,1)S(1)}, u32[]{:S(2)}, u32[]{:S(2)}) collective-permute-start(bf16[128,2176]{1,0:T(8,128)(2,1)S(1)} %bitcast.181), channel_id=1, source_target_pairs={{0,4},{1,5},{2,6},{3,7},{4,0},{5,1},{6,2},{7,3},{8,12},{9,13},{10,... | collective-permute-start | bytes 1671176 | tf_op jit(solution)/shard_map/ppermute | solution.py:586
  265.6 40.1 %collective-permute-start.34 = (bf16[128,2048]{1,0:T(8,128)(2,1)S(1)}, bf16[128,2048]{1,0:T(8,128)(2,1)S(1)}, u32[]{:S(2)}, u32[]{:S(2)}) collective-permute-start(bf16[128,2048]{1,0:T(8,128)(2,1)S(1)} %bitcast.186), channel_id=1, source_target_pairs={{0,2},{1,3},{2,0},{3,1},{4,6},{5,7},{6,4},{7,5},{8,10},{9,11},{10,... | collective-permute-start | bytes 1572872 | tf_op jit(solution)/shard_map/ppermute | solution.py:586
  266.2 39.7 %collective-permute-start.33 = (bf16[128,2048]{1,0:T(8,128)(2,1)S(1)}, bf16[128,2048]{1,0:T(8,128)(2,1)S(1)}, u32[]{:S(2)}, u32[]{:S(2)}) collective-permute-start(bf16[128,2048]{1,0:T(8,128)(2,1)S(1)} %bitcast.184), channel_id=1, source_target_pairs={{0,4},{1,5},{2,6},{3,7},{4,0},{5,1},{6,2},{7,3},{8,12},{9,13},{10,... | collective-permute-start | bytes 1572872 | tf_op jit(solution)/shard_map/ppermute | solution.py:586
  306.1 42.1 %collective-permute-start.37 = (bf16[256,2176]{1,0:T(8,128)(2,1)}, bf16[256,2176]{1,0:T(8,128)(2,1)S(1)}, u32[]{:S(2)}, u32[]{:S(2)}) collective-permute-start(bf16[256,2176]{1,0:T(8,128)(2,1)} %get-tuple-element.371), channel_id=1, source_target_pairs={{0,4},{1,5},{2,6},{3,7},{4,0},{5,1},{6,2},{7,3},{8,12},{9,13},{10,... | collective-permute-start | bytes 3342344 | tf_op jit(solution)/shard_map/ppermute | solution.py:586
  307.1 42.9 %collective-permute-start.39 = (bf16[256,2176]{1,0:T(8,128)(2,1)S(1)}, bf16[256,2176]{1,0:T(8,128)(2,1)S(1)}, u32[]{:S(2)}, u32[]{:S(2)}) collective-permute-start(bf16[256,2176]{1,0:T(8,128)(2,1)S(1)} %pad_maximum_fusion.5.refs_3_), channel_id=1, source_target_pairs={{0,2},{1,3},{2,0},{3,1},{4,6},{5,7},{6,4},{7,5},{8,10},{9,11},{10,... | collective-permute-start | bytes 3342344 | tf_op jit(solution)/shard_map/ppermute | solution.py:586
  308.1 42.0 %collective-permute-start.38 = (bf16[256,2048]{1,0:T(8,128)(2,1)S(1)}, bf16[256,2048]{1,0:T(8,128)(2,1)}, u32[]{:S(2)}, u32[]{:S(2)}) collective-permute-start(bf16[256,2048]{1,0:T(8,128)(2,1)S(1)} %pad_maximum_fusion.12.refs_1_), channel_id=1, source_target_pairs={{0,2},{1,3},{2,0},{3,1},{4,6},{5,7},{6,4},{7,5},{8,10},{9,11},{10,... | collective-permute-start | bytes 3145736 | tf_op jit(solution)/shard_map/ppermute | solution.py:586
  308.6 41.4 %collective-permute-start.40 = (bf16[256,2048]{1,0:T(8,128)(2,1)S(1)}, bf16[256,2048]{1,0:T(8,128)(2,1)}, u32[]{:S(2)}, u32[]{:S(2)}) collective-permute-start(bf16[256,2048]{1,0:T(8,128)(2,1)S(1)} %pad_maximum_fusion.13.refs_1_), channel_id=1, source_target_pairs={{0,4},{1,5},{2,6},{3,7},{4,0},{5,1},{6,2},{7,3},{8,12},{9,13},{10,... | collective-permute-start | bytes 3145736 | tf_op jit(solution)/shard_map/ppermute | solution.py:586
  350.1 41.4 %collective-permute-start.41 = (bf16[256,2176]{1,0:T(8,128)(2,1)}, bf16[256,2176]{1,0:T(8,128)(2,1)S(1)}, u32[]{:S(2)}, u32[]{:S(2)}) collective-permute-start(bf16[256,2176]{1,0:T(8,128)(2,1)} %get-tuple-element.393), channel_id=1, source_target_pairs={{0,2},{1,3},{2,0},{3,1},{4,6},{5,7},{6,4},{7,5},{8,10},{9,11},{10,... | collective-permute-start | bytes 3342344 | tf_op jit(solution)/shard_map/ppermute | solution.py:586
  351.1 41.9 %collective-permute-start.42 = (bf16[256,2176]{1,0:T(8,128)(2,1)S(1)}, bf16[256,2176]{1,0:T(8,128)(2,1)S(1)}, u32[]{:S(2)}, u32[]{:S(2)}) collective-permute-start(bf16[256,2176]{1,0:T(8,128)(2,1)S(1)} %pad_maximum_fusion.6.refs_3_), channel_id=1, source_target_pairs={{0,4},{1,5},{2,6},{3,7},{4,0},{5,1},{6,2},{7,3},{8,12},{9,13},{10,... | collective-permute-start | bytes 3342344 | tf_op jit(solution)/shard_map/ppermute | solution.py:586
  352.1 39.2 %collective-permute-start.43 = (bf16[128,2176]{1,0:T(8,128)(2,1)S(1)}, bf16[128,2176]{1,0:T(8,128)(2,1)S(1)}, u32[]{:S(2)}, u32[]{:S(2)}) collective-permute-start(bf16[128,2176]{1,0:T(8,128)(2,1)S(1)} %slice.496), channel_id=1, source_target_pairs={{0,2},{1,3},{2,0},{3,1},{4,6},{5,7},{6,4},{7,5},{8,10},{9,11},{10,... | collective-permute-start | bytes 1671176 | tf_op jit(solution)/shard_map/ppermute | solution.py:586
  392.9 41.4 %collective-permute-start.44 = (bf16[256,2048]{1,0:T(8,128)(2,1)}, bf16[256,2048]{1,0:T(8,128)(2,1)S(1)}, u32[]{:S(2)}, u32[]{:S(2)}) collective-permute-start(bf16[256,2048]{1,0:T(8,128)(2,1)} %get-tuple-element.404), channel_id=1, source_target_pairs={{0,2},{1,3},{2,0},{3,1},{4,6},{5,7},{6,4},{7,5},{8,10},{9,11},{10,... | collective-permute-start | bytes 3145736 | tf_op jit(solution)/shard_map/ppermute | solution.py:586
  393.9 40.2 %collective-permute-start.46 = (bf16[128,2176]{1,0:T(8,128)(2,1)S(1)}, bf16[128,2176]{1,0:T(8,128)(2,1)S(1)}, u32[]{:S(2)}, u32[]{:S(2)}) collective-permute-start(bf16[128,2176]{1,0:T(8,128)(2,1)S(1)} %slice.497), channel_id=1, source_target_pairs={{0,4},{1,5},{2,6},{3,7},{4,0},{5,1},{6,2},{7,3},{8,12},{9,13},{10,... | collective-permute-start | bytes 1671176 | tf_op jit(solution)/shard_map/ppermute | solution.py:586
  394.3 42.2 %collective-permute-start.45 = (bf16[256,2176]{1,0:T(8,128)(2,1)}, bf16[256,2176]{1,0:T(8,128)(2,1)S(1)}, u32[]{:S(2)}, u32[]{:S(2)}) collective-permute-start(bf16[256,2176]{1,0:T(8,128)(2,1)} %get-tuple-element.416), channel_id=1, source_target_pairs={{0,4},{1,5},{2,6},{3,7},{4,0},{5,1},{6,2},{7,3},{8,12},{9,13},{10,... | collective-permute-start | bytes 3342344 | tf_op jit(solution)/shard_map/ppermute | solution.py:586
  548.7 38.4 %collective-permute-start.65 = (bf16[256,2048]{1,0:T(8,128)(2,1)}, bf16[256,2048]{1,0:T(8,128)(2,1)}, u32[]{:S(2)}, u32[]{:S(2)}) collective-permute-start(bf16[256,2048]{1,0:T(8,128)(2,1)} %get-tuple-element.476), channel_id=1, source_target_pairs={{0,2},{1,3},{2,0},{3,1},{4,6},{5,7},{6,4},{7,5},{8,10},{9,11},{10,... | collective-permute-start | bytes 3145736 | tf_op jit(solution)/shard_map/ppermute | solution.py:586
  551.9 35.1 %collective-permute-start.66 = (bf16[128,2048]{1,0:T(8,128)(2,1)}, bf16[128,2048]{1,0:T(8,128)(2,1)S(1)}, u32[]{:S(2)}, u32[]{:S(2)}) collective-permute-start(bf16[128,2048]{1,0:T(8,128)(2,1)} %slice.522), channel_id=1, source_target_pairs={{0,4},{1,5},{2,6},{3,7},{4,0},{5,1},{6,2},{7,3},{8,12},{9,13},{10,... | collective-permute-start | bytes 1572872 | tf_op jit(solution)/shard_map/ppermute | solution.py:586
  624.6 36.9 %collective-permute-start.72 = (bf16[2,2048,128]{2,1,0:T(8,128)(2,1)S(1)}, bf16[2,2048,128]{2,1,0:T(8,128)(2,1)S(1)}, u32[]{:S(2)}, u32[]{:S(2)}) collective-permute-start(bf16[2,2048,128]{2,1,0:T(8,128)(2,1)S(1)} %concatenate.147), channel_id=1, source_target_pairs={{0,2},{1,3},{2,0},{3,1},{4,6},{5,7},{6,4},{7,5},{8,10},{9,11},{10,... | collective-permute-start | bytes 3145736 | tf_op jit(solution)/shard_map/ppermute | solution.py:586
  625.7 35.5 %collective-permute-start.73 = (bf16[256,1536]{1,0:T(8,128)(2,1)S(1)}, bf16[256,1536]{1,0:T(8,128)(2,1)S(1)}, u32[]{:S(2)}, u32[]{:S(2)}) collective-permute-start(bf16[256,1536]{1,0:T(8,128)(2,1)S(1)} %copy-done.100), channel_id=1, source_target_pairs={{0,4},{1,5},{2,6},{3,7},{4,0},{5,1},{6,2},{7,3},{8,12},{9,13},{10,... | collective-permute-start | bytes 2359304 | tf_op jit(solution)/shard_map/ppermute | solution.py:586
  699.8 93.0 %all-to-all-start.1 = ((bf16[8,264,256]{2,1,0:T(8,128)(2,1)}), bf16[8,264,256]{2,1,0:T(8,128)(2,1)S(1)}, u32[]{:S(2)}, u32[]{:S(2)}) async-start(bf16[8,264,256]{2,1,0:T(8,128)(2,1)} %maximum_bitcast_fusion.2), calls=%async_computation.1 | async-start | bytes 2162688 | tf_op jit(solution)/shard_map/all_to_all | solution.py:966
  743.7 44.8 %collective-permute-start.84 = (bf16[128,2048]{1,0:T(8,128)(2,1)}, bf16[128,2048]{1,0:T(8,128)(2,1)}, u32[]{:S(2)}, u32[]{:S(2)}) collective-permute-start(bf16[128,2048]{1,0:T(8,128)(2,1)} %pad_maximum_fusion.24), channel_id=1, source_target_pairs={{0,16},{1,17},{2,18},{3,19},{4,20},{5,21},{6,22},{7,23},{8,24},{9,... | collective-permute-start | bytes 1572872 | tf_op jit(solution)/shard_map/ppermute | solution.py:586
  (177 other events, 2548.1 us)

commit v4 on v3

--- a/solution.py
+++ b/solution.py
@@ -116,7 +116,7 @@
         to = pl.ds(pl.multiple_of(places[p] * rows, rows), rows)
         query_w[to, :] = mains[p][:, : cut[0]]
         output_t[to, :] = mains[p][:, cut[0] : cut[1]]
-        expand_w[to, :] = mains[p][:, cut[1] :]
+        expand_w[to, :] = mains[p][:, cut[1] : cut[1] + expand_w.shape[1]]
         at = slice(p * rows, (p + 1) * rows)
         latent_w[places[peers], to, :] = small[at, :LANES]
         extra_w[to, :] = small[at, LANES:]
@@ -170,7 +170,7 @@
 def attn_backward_kernel(
     heads, peers, score_scale,
     places, d_attn, query_w, output_t, expand_w, extra_w, latent_w, gain_latent, cos, sin,
-    normed, query, key_rope_all, expanded, soft_all, mixed, compressed, latent,
+    normed, query, key_rope_all, expanded, soft_all, compressed, latent,
     normed_ffn, d_logits, tokens, g_gain_ffn,
     g_mains, near_keep, near_send, d_in_keep, d_in_send,
     g_all, g_few, d_query_s, d_latent_s, d_use_s,
@@ -182,13 +182,11 @@
     nope = heads * NOPE
     lane = lax.broadcasted_iota(jnp.int32, (1, LANES), 1)
     lane2 = lax.rem(lax.broadcasted_iota(jnp.int32, (1, 2 * LANES), 1), LANES)
-    rows = g_mains[0].shape[0]
-    cut = (query_w.shape[1], query_w.shape[1] + output_t.shape[1])
+    rows = g_mains[0][0].shape[0]
+    query_cols = query_w.shape[1]
     width = d_attn.shape[1]
     strips = [slice(lo, lo + width // 4) for lo in range(0, width, width // 4)]
-    value_cols = output_t.shape[1]
-    for strip in strips:
-        g_all[strip, :value_cols] = t_mm(d_attn[:, strip], mixed[...]).astype(BF16)
+    expand_cols = expand_w.shape[1]
     d_mixed = mm(d_attn[...], output_t[...]).astype(BF16)
     d_query_rope = jnp.zeros((group, 2 * LANES), F32)
     d_key_rope = jnp.zeros((group, 2 * LANES), F32)
@@ -212,14 +210,15 @@
         )
         g_w = t_mm(latent[...], d_expanded).astype(BF16)
         for e in range(peers):
-            g_all[pl.ds((e * heads + h) * rank, rank), value_cols:] = g_w[e * rank : (e + 1) * rank]
+            g_all[pl.ds((e * heads + h) * rank, rank), :expand_cols] = g_w[e * rank : (e + 1) * rank]
         back = mm_t(d_expanded, w)
         if h == 0:
             d_use_s[...] = back
         else:
             d_use_s[...] += back
     for p in range(peers):
-        g_mains[p][:, cut[0] :] = g_all[pl.ds(pl.multiple_of(places[p] * rows, rows), rows), :]
+        ref, to = g_mains[p]
+        ref[to : to + rows, query_cols:] = g_all[pl.ds(pl.multiple_of(places[p] * rows, rows), rows), :expand_cols]
     c, s = cos[...], sin[...]
     a, b = d_query_rope[:, :LANES], d_query_rope[:, LANES:]
     d_query_s[:, nope : nope + LANES] = (a * c + b * s).astype(BF16)
@@ -276,7 +275,8 @@
     for p in range(peers):
         at = pl.ds(pl.multiple_of(places[p] * rows, rows), rows)
         to = slice(p * rows, (p + 1) * rows)
-        g_mains[p][:, : cut[0]] = g_all[at, :]
+        ref, down = g_mains[p]
+        ref[down : down + rows, :query_cols] = g_all[at, :]
         for j in range(2):
             near_keep[j, to] = g_few[places[peers + j], at, :]
             near_send[j, to] = g_few[places[peers + 2 + j], at, :]
@@ -325,10 +325,12 @@
 def attn_backward(heads, peers, score_scale, gain_at, rows, args):
     group, width = args[1].shape
     query_w, output_t, expand_w, extra_w, latent_w = args[2:7]
-    main = query_w.shape[1] + output_t.shape[1] + expand_w.shape[1]
+    main = query_w.shape[1] + expand_w.shape[1]
     few = extra_w.shape[1] // LANES
     shape = jax.ShapeDtypeStruct
-    outs = [shape((rows, main), BF16)] * peers + [
+    ring = peers // 2
+    order = [*range(1, ring), 0]
+    outs = [shape((rows, main), BF16)] * ring + [shape((2 * rows, main), BF16)] * (ring // 2) + [
         shape((2 + few, width, LANES), BF16), shape((2 + few, width, LANES), BF16),
         shape((group // 2, width), BF16), shape((group // 2, width), BF16),
     ]
@@ -342,21 +344,32 @@
     n = len(args)
 
     def kernel(*refs):
-        attn_backward_kernel(heads, peers, score_scale, *refs[:n], refs[n : n + peers], *refs[n + peers :], gain_at=gain_at)
+        pieces = [(ref, 0) for ref in refs[n : n + ring]] + [None] * ring
+        for i, k in enumerate(order):
+            pieces[ring + k] = (refs[n + ring + i // 2], i % 2 * rows)
+        rest = refs[n + ring + ring // 2 :]
+        attn_backward_kernel(heads, peers, score_scale, *refs[:n], pieces, *rest, gain_at=gain_at)
 
     outs = in_vmem(kernel, outs, scratch, 12 * 10**9, args)
-    return outs[:peers], outs[peers:]
+    return outs[:ring], outs[ring : ring + ring // 2], outs[ring + ring // 2 :]
+
+
+PARTS = {
+    "far": ((0, 1, 2, 3), (4, 5, 6, 7)),
+    "near": ((0, 1, 4, 5), (2, 3, 6, 7)),
+    "ring": ((0, 2, 4, 6), (1, 3, 5, 7)),
+}
 
 
 def ffn_kernel(
-    local, segs_side, steps, width, crossed,
+    local, segs_side, steps, width, dx_mode, out_mode,
     first_ref, x0, x1, g0, g1, router, wg, wu, wd,
     dx_keep, dx_send, out_keep, out_send, x_all, g_all, hs_all, dg_all, du_all,
     acc_out, acc_dx, gates_s, dgates_s,
 ):
     j = pl.program_id(0)
     half = x0.shape[0]
-    slot = half // 2
+    unit = half // 4
     block = wg.shape[0]
     x = jnp.concatenate([x0[...], x1[...]], axis=0)
     g_in = jnp.concatenate([g0[:, :width], g1[:, :width]], axis=0)
@@ -405,24 +418,21 @@
 
     @pl.when(j == steps - 1)
     def _():
-        straight = [(dx_keep, 0, 0, half), (dx_send, 0, half, 2 * half)]
-        across = [
-            (out_keep, 0, 0, slot), (out_send, 0, slot, half),
-            (out_keep, slot, half, half + slot), (out_send, slot, half + slot, 2 * half),
-        ]
-        if crossed:
-            swap = {id(dx_keep): out_keep, id(dx_send): out_send, id(out_keep): dx_keep, id(out_send): dx_send}
-            straight = [(swap[id(ref)], *at) for ref, *at in straight]
-            across = [(swap[id(ref)], *at) for ref, *at in across]
-        for ref, at, lo, hi in straight + across:
-            if ref is dx_keep or ref is dx_send:
-                ref[at : at + hi - lo, :width] = acc_dx[lo:hi].astype(BF16)
-                ref[at : at + hi - lo, width:] = dgates_s[lo:hi].astype(BF16)
-            else:
-                ref[at : at + hi - lo] = acc_out[lo:hi].astype(BF16)
-
-
-def ffn_tile(first, rows, grads, router, weights, local, call, calls, kept, crossed):
+        for (keep, away), ranges, is_dx in (
+            ((dx_keep, dx_send), PARTS[dx_mode], True),
+            ((out_keep, out_send), PARTS[out_mode], False),
+        ):
+            for ref, blocks in zip((keep, away), ranges):
+                for at, block_of in enumerate(blocks):
+                    to, rows = pl.ds(at * unit, unit), pl.ds(block_of * unit, unit)
+                    if is_dx:
+                        ref[to, :width] = acc_dx[rows].astype(BF16)
+                        ref[to, width:] = dgates_s[rows].astype(BF16)
+                    else:
+                        ref[to] = acc_out[rows].astype(BF16)
+
+
+def ffn_tile(first, rows, grads, router, weights, local, call, calls, kept, dx_mode, out_mode):
     half, width = rows[0].shape
     hid = weights.shape[1]
     block = 2 * LANES
@@ -459,7 +469,7 @@
     out_specs = [whole(half, width + LANES)] * 2 + [whole(half, width)] * 2 + [tile_rows] * 2 + [tile_hidden] * 3
 
     def kernel(*refs):
-        ffn_kernel(local, segs_side, steps, width, crossed, *refs[:plain], *refs[len(args) :])
+        ffn_kernel(local, segs_side, steps, width, dx_mode, out_mode, *refs[:plain], *refs[len(args) :])
 
     outs = pl.pallas_call(
         kernel,
@@ -480,6 +490,60 @@
         ),
     )(*args)
     return outs[:4], outs[4:]
+
+
+def pick_pieces(order, sources):
+    n, lanes = sources[0].shape[0], sources[0].shape[2]
+    heights = [v.shape[1] for v in sources]
+    shape = (n, sum(heights), lanes)
+
+    def kernel(_, *refs):
+        at = 0
+        for ref, high in zip(refs, heights):
+            refs[-1][0, at : at + high] = ref[0]
+            at += high
+
+    return pl.pallas_call(
+        kernel,
+        grid_spec=pltpu.PrefetchScalarGridSpec(
+            num_scalar_prefetch=1,
+            grid=(n,),
+            in_specs=[pl.BlockSpec((1, h, lanes), lambda p, order: (order[p], 0, 0)) for h in heights],
+            out_specs=pl.BlockSpec((1, *shape[1:]), lambda p, order: (p, 0, 0)),
+        ),
+        out_shape=jax.ShapeDtypeStruct(shape, sources[0].dtype),
+        cost_estimate=pl.CostEstimate(flops=0, bytes_accessed=2**21, transcendentals=0),
+    )(order, *sources)
+
+
+def expert_grad(d, v, got, local, ff, seg):
+    rows, width = v.shape
+    side = local * seg
+    block = 2 * LANES
+
+    def kernel(d_ref, v_ref, got_ref, out, turned):
+        @pl.when(pl.program_id(0) == 0)
+        def _():
+            turned[...] = d_ref[...].T
+
+        total = mm(turned[...], v_ref[...]) + got_ref[...].astype(F32)
+        for j in range(local):
+            out[j] = total[j * seg : j * seg + ff]
+
+    return pl.pallas_call(
+        kernel,
+        grid=(width // block,),
+        in_specs=[
+            pl.BlockSpec((rows, side), lambda i: (0, 0), pipeline_mode=pl.Buffered(1)),
+            pl.BlockSpec((rows, block), lambda i: (0, i)),
+            pl.BlockSpec((side, block), lambda i: (0, i)),
+        ],
+        out_specs=pl.BlockSpec((local, ff, block), lambda i: (0, 0, i)),
+        out_shape=jax.ShapeDtypeStruct((local, ff, width), F32),
+        scratch_shapes=[pltpu.VMEM((side, rows), BF16)],
+        compiler_params=pltpu.CompilerParams(vmem_limit_bytes=56 * 2**20, dimension_semantics=("arbitrary",)),
+        cost_estimate=pl.CostEstimate(flops=2 * rows * width * side, bytes_accessed=20 * 2**20, transcendentals=0),
+    )(d, v, got)
 
 
 def pack_experts(parts, seg, room):
@@ -597,6 +661,9 @@
     piece_e = plane_e + [e ^ 1 for e in plane_e]
     shard_order = [me_s, me_s ^ 2, me_s ^ 1, me_s ^ 3]
     places = jnp.stack([*piece_e, *shard_order]).astype(jnp.int32)
+    piece_of = jnp.stack(
+        [lax.rem(me_e // 2 + ring - e // 2, ring) + ring * (lax.rem(me_e, 2) ^ (e % 2)) for e in range(peers)]
+    ).astype(jnp.int32)
 
     orders = (("y", "x"), ("x", "y"))
     zones = [list(range(k, min(k + 2, ring))) for k in range(0, ring, 2)]
@@ -645,14 +712,16 @@
     side = seg * local
     tail = pad_to(shared, LANES)
     expert_parts = [w_expert_gate.transpose(0, 2, 1), w_expert_up.transpose(0, 2, 1), w_expert_down]
-    shared_pack = jnp.concatenate(
+    ahead = [lax.rem(me_e // 2 + k, ring) * 2 + lax.rem(me_e, 2) for k in range(ring)]
+    shared_pack = pick_pieces(
+        jnp.stack(ahead + [e ^ 1 for e in ahead]).astype(jnp.int32),
         [
             w_shared_gate.T.reshape(peers, shared, rows_dev),
             w_shared_up.T.reshape(peers, shared, rows_dev),
             w_shared_down.reshape(peers, shared, rows_dev),
         ],
-        axis=1,
-    )
+    )
+    shared_keep, shared_away = shared_pack[:ring], shared_pack[ring:]
     lane_experts = jnp.arange(experts, dtype=jnp.int32)
     routed_own = jnp.any(routes[:, :, None] == lane_experts[None, None, :], axis=1)
     grad_pack = jnp.concatenate(
@@ -662,41 +731,71 @@
     def pack(*parts):
         return pack_experts(parts, seg, 2 * tail)
 
-    main_own, main_other = [main], []
+    got = step([(tokens, "x"), (grad_pack, "ring"), (shared_away, "y")])
+    token_near = jnp.concatenate([tokens, got[0]], axis=0)
+    grad_blocks = [grad_pack, got[1]]
+    grad_halves = zone_halves(grad_blocks)
+    shared_ways = [jnp.stack([shared_keep[k], got[2][k]]) for k in range(ring)]
+
+    def places_in_group():
+        order = jnp.concatenate([s * own_rows + jnp.arange(own_rows, dtype=jnp.int32) for s in shard_order])
+        segment = jnp.concatenate(
+            [lax.dynamic_slice_in_dim(segments, s * own_rows, own_rows, 0) for s in shard_order], axis=0
+        )
+        place = positions(segments)
+        place = jnp.concatenate(
+            [lax.dynamic_slice_in_dim(place, s * own_rows, own_rows, 0) for s in shard_order], axis=0
+        )
+        cos, sin = angles(place, ROPE)
+        return (
+            jnp.tile(cos, (1, heads)), jnp.tile(sin, (1, heads)),
+            order[:, None], order[None, :], segment[:, None], segment[None, :],
+        )
+
+    piece = jnp.concatenate([main, small], axis=1)
+    main_own, main_other = [piece], []
     got, (own_side, both_sides) = step(
-        [(main, "ring"), (main, "y")] + [(small, k) for k in range(1, ring)], pack, *expert_parts
+        [(piece, "ring"), (piece, "y"), firsts(grad_halves)[0]] + [(small, k) for k in range(2, ring)],
+        pack, *expert_parts,
     )
     main_own.append(got[0])
     main_other.append(got[1])
-    small_own = jnp.concatenate([small, *got[2:]], axis=0)
-    shared_all = lax.all_to_all(after(shared_pack, got), "expert", 0, 0, tiled=True)
-    shared_all = shared_all.transpose(1, 0, 2).reshape(3, shared, width)
-    shared_own = jnp.pad(shared_all, ((0, 0), (0, tail - shared), (0, 0)))
-
-    got = step([(main_own[1], "ring"), (main_own[1], "y"), (small_own, "y"), (tokens, "x"), (own_side, "pair")])
+    grad_first = [got[2]]
+    main_cols = main.shape[1]
+    small_far = jnp.concatenate(got[3:], axis=0)
+
+    got, around = step(
+        [
+            (main_own[1][:, :main_cols], "ring"), (main_own[1], "y"), (small_far, "y"), (token_near, "pair"),
+            (own_side, "pair"),
+        ],
+        places_in_group,
+    )
+    cos, sin = around[:2]
     main_own.append(got[0])
     main_other.append(got[1])
-    small_all = jnp.concatenate([small_own, got[2]], axis=0)
+    small_all = jnp.concatenate(
+        [
+            main_own[0][:, main_cols:], main_own[1][:, main_cols:], small_far,
+            main_other[0][:, main_cols:], main_other[1][:, main_cols:], got[2],
+        ],
+        axis=0,
+    )
     latent_all = small_all[:, :LANES]
-    token_near = jnp.concatenate([tokens, got[3]], axis=0)
+    token_group = jnp.concatenate([token_near, got[3]], axis=0)
     other_side = got[4]
 
-    got = step(
-        [(main_own[2], "ring"), (main_own[2], "y"), (latent_all, "x"), (token_near, "pair"), (shared_own, "pair")]
-    )
+    got = step([(main_own[2], "ring"), (main_own[2], "y"), (latent_all, "x"), firsts(grad_halves)[1]])
     main_own.append(got[0])
     main_other.append(got[1])
     latent_x = got[2]
-    token_group = jnp.concatenate([token_near, got[3]], axis=0)
-    shared_both = jnp.concatenate([shared_own, got[4]], axis=1)
-
-    got, both_sides = step(
-        [(main_own[3], "y"), (jnp.stack([latent_all, latent_x]), "pair"), (grad_pack, "ring")],
-        join_pair, both_sides, other_side, shared_both,
-    )
+    grad_first.append(got[3])
+    grad_nears = nears(grad_halves, grad_first)
+
+    got = step([(main_own[3], "y"), (jnp.stack([latent_all, latent_x]), "pair"), (grad_blocks[1], "ring")])
     main_other.append(got[0])
     latent_pair = got[1]
-    grad_blocks = [grad_pack, got[2]]
+    grad_blocks.append(got[2])
     for k in range(4, ring):
         got = step([(main_own[k - 1], "ring")])
         main_own.append(got[0])
@@ -704,34 +803,32 @@
         main_other.append(got[0])
     mains = main_own + main_other
 
-    def by_group(values):
-        return jnp.concatenate(
-            [lax.dynamic_slice_in_dim(values, s * own_rows, own_rows, 0) for s in shard_order], axis=0
-        )
-
-    index = by_group(jnp.arange(group_len, dtype=jnp.int32))
-    segment = by_group(segments)
-    cos, sin = angles(by_group(positions(segments)), ROPE)
-    cos, sin = jnp.tile(cos, (1, heads)), jnp.tile(sin, (1, heads))
     gain_at = ROPE + experts
     def attend(small_in, mains_in, *args):
         return attn_forward(heads, peers, score_scale, gain_at, list(args), small_in, mains_in)
 
-    grad_halves = zone_halves(grad_blocks)
     got, outs = step(
-        firsts(grad_halves) + [(grad_blocks[1], "ring")],
+        [(near, two) for near, (_, two) in zip(grad_nears, orders)] + [(shared_ways[k], k) for k in range(1, ring)],
         attend, small_all, mains,
-        places, token_group, latent_x, latent_pair, cos, sin,
-        index[:, None], index[None, :], segment[:, None], segment[None, :],
-    )
-    grad_nears = nears(grad_halves, got)
-    grad_blocks.append(got[2])
+        places, token_group, latent_x, latent_pair, *around,
+    )
+    grad_tiles = {0: list(zip(grad_nears, got))}
+    shared_all = pick_pieces(
+        piece_of, [jnp.stack([pieces[flip] for flip in range(2) for pieces in (shared_ways[0], *got[2:])])]
+    )
+    shared_all = shared_all.transpose(1, 0, 2).reshape(3, shared, width)
+    shared_own = jnp.pad(shared_all, ((0, 0), (0, tail - shared), (0, 0)))
     saved, attn_weights = outs[2:10], outs[12:]
     gain_attn, gain_ffn, gain_latent = outs[10][0:1], outs[10][1:2], outs[11]
     router_w = outs[15][:, ROPE : ROPE + experts]
-    got = step([(outs[1], "pair")])
+    got = step([(outs[1], "pair"), (shared_own, "pair")])
     keep, away = split_half(add(outs[0], got[0]))
-    got = step([(away, "x"), (grad_blocks[2], "ring")])
+    shared_both = jnp.concatenate([shared_own, got[1]], axis=1)
+    def grads_near(i, turn):
+        half = zone_halves([grad_blocks[k] for k in zones[i]])[turn]
+        return half, orders[turn][0]
+
+    got, both_sides = step([(away, "x"), (grad_blocks[2], "ring")], join_pair, both_sides, other_side, shared_both)
     attn_term = keep.astype(F32) + got[0].astype(F32)
     grad_blocks.append(got[1])
     own_float = tokens.astype(F32)
@@ -746,9 +843,10 @@
     router_pad = jnp.pad(router_w, ((0, 0), (0, LANES - experts)))
     first_expert = (me_e * local).reshape(1)
     row_blocks = [normed_ffn]
-    got = step([(normed_ffn, "ring")] + [(near, two) for near, (_, two) in zip(grad_nears, orders)])
+    next_halves = [grads_near(1, turn) for turn in range(2)]
+    got = step([(normed_ffn, "ring"), *next_halves])
     row_blocks.append(got[0])
-    grad_tiles = {0: list(zip(grad_nears, got[1:]))}
+    grad_nears = nears([half for half, _ in next_halves], got[1:])
     row_halves = zone_halves(row_blocks)
     got = step(firsts(row_halves) + [(row_blocks[1], "ring")])
     row_nears = nears(row_halves, got)
@@ -757,126 +855,92 @@
     row_tiles = {0: list(zip(row_nears, got))}
     row_blocks.append(got[2])
 
+    for _ in range(4, ring):
+        got = step([(row_blocks[-1], "ring"), (grad_blocks[-1], "ring")])
+        row_blocks.append(got[0])
+        grad_blocks.append(got[1])
+
     kept = None
     dx, dx_near, dx_home, outs_of, out_near, out_home = {}, {}, {}, {}, {}, {}
     for_pair, from_pair = [], []
 
-    def ways(call):
-        one, two = orders[call % 2]
-        return (two, one) if call == calls - 1 else (one, two)
+    last_call = calls - 1
+
+    def modes(call):
+        if call < 2:
+            return "ring", "ring"
+        return ("near", "far") if call == last_call else ("far", "far")
 
     def moves(jobs):
         sends = []
         for what, call, stage in jobs:
-            one, two = ways(call)
-            if what == "out":
-                one, two = two, one
+            one, two = orders[call % 2]
+            mode = modes(call)[what == "out"]
+            ways = {"far": (two, one), "near": (one, two), "ring": (-1, two, one)}[mode]
             parts, near = (dx, dx_near) if what == "dx" else (outs_of, out_near)
-            sends.append((parts[call][1], one) if stage == 1 else (split_half(near[call])[1], two))
+            value = parts[call][1] if stage == 1 else split_half(near[call])[1]
+            sends.append((value, ways[stage - 1]))
 
         def arrived(got):
             for (what, call, stage), g in zip(jobs, got):
                 parts, near, home = (dx, dx_near, dx_home) if what == "dx" else (outs_of, out_near, out_home)
                 if stage == 1:
                     near[call] = add(parts[call][0], g)
+                elif stage == 2 and modes(call)[what == "out"] == "ring":
+                    near[call] = add(split_half(near[call])[0], g)
                 else:
                     home[call] = add(split_half(near[call])[0], g)
 
         return sends, arrived
 
+    plan = {
+        1: [("dx", 0, 1), ("out", 0, 1)],
+        2: [("dx", 1, 1), ("dx", 0, 2), ("out", 0, 2)],
+        3: [("out", 1, 1), ("dx", 1, 2), ("dx", 0, 3), ("out", 0, 3), ("dx", 2, 1)],
+        4: [("out", 1, 2), ("dx", 1, 3)],
+        5: [("out", 1, 3)],
+    }
     for call in range(calls):
         i, turn = call // 2, call % 2
         more = i + 1 < len(zones)
-        sends, jobs = [], []
+        jobs = list(plan.get(call, []))
+        if call >= 4:
+            jobs += [("dx", call - 1, 1), ("dx", call - 2, 2), ("out", call - 2, 1)]
+            jobs += [("out", call - 3, 2)] if call >= 5 else []
+        sends = []
         if turn == 0 and more:
             row_halves = zone_halves([row_blocks[k] for k in zones[i + 1]])
-            grad_halves = zone_halves([grad_blocks[k] for k in zones[i + 1]])
-            sends += firsts(row_halves) + firsts(grad_halves)
+            sends += firsts(row_halves) + [(near, two) for near, (_, two) in zip(grad_nears, orders)]
         if turn == 1 and more:
-            sends += [(near, two) for near, (_, two) in zip(row_nears, orders)] + [(grad_nears[0], orders[0][1])]
-        if turn == 0 and i > 0:
-            sends += [(grad_last, orders[1][1])]
-        if len(row_blocks) < ring:
-            sends += [(row_blocks[-1], "ring"), (grad_blocks[-1], "ring")]
-        if call >= 1:
-            jobs.append(("dx", call - 1, 1))
-        if call >= 2:
-            jobs.append(("dx", call - 2, 2))
-        if call >= 3:
-            jobs.append(("out", call - 3, 1))
-        if call >= 4:
-            jobs.append(("out", call - 4, 2))
+            sends += [(near, two) for near, (_, two) in zip(row_nears, orders)]
+            if i + 2 < len(zones):
+                next_halves = [grads_near(i + 2, turn) for turn in range(2)]
+                sends += next_halves
         moved, arrived = moves(jobs)
 
         def tile(rows, grads, kept_in, call=call):
             return ffn_tile(
-                first_expert, rows, grads, router_pad, both_sides, local, call, calls, kept_in, call < calls - 1
+                first_expert, rows, grads, router_pad, both_sides, local, call, calls, kept_in, *modes(call)
             )
 
-        if turn == 1:
-            grads = grad_tiles[i][1]
-        else:
-            grads = grad_tiles[i][0]
-        got, (outs, kept) = step(moved + sends, tile, row_tiles[i][turn], grads, kept)
-        arrived(got[: len(moved)])
+        got, (outs, kept) = step(moved + sends, tile, row_tiles[i][turn], grad_tiles[i][turn], kept)
+        arrived(got)
         got = got[len(moved) :]
         dx[call], outs_of[call] = outs[:2], outs[2:4]
-        if turn == 0 and i > 0:
-            grad_tiles[i].append((grad_last, got[2 * len(orders) if more else 0]))
         if turn == 0 and more:
-            row_nears = nears(row_halves, got[:2])
-            grad_nears = nears(grad_halves, got[2:4])
+            row_nears = nears(row_halves, got)
+            grad_tiles[i + 1] = list(zip(grad_nears, got[2:]))
         if turn == 1 and more:
-            row_tiles[i + 1] = list(zip(row_nears, got[:2]))
-            grad_tiles[i + 1] = [(grad_nears[0], got[2])]
-            grad_last = grad_nears[1]
-        if len(row_blocks) < ring:
-            row_blocks.append(got[-2])
-            grad_blocks.append(got[-1])
-
-    def planes_of(home, zone_list, turns):
-        return {
-            (k, turn): home[2 * i + turn].reshape(len(zones[i]), -1, home[2 * i + turn].shape[1])[j]
-            for i in zone_list
-            for j, k in enumerate(zones[i])
-            for turn in turns
-        }
-
-    def weight_part(d, v):
-        return t_mm(d.reshape(-1, d.shape[-1])[:, side:], v.reshape(-1, v.shape[-1])).astype(BF16)
-
-    x_all, g_all, hs_all, dg_all, du_all = kept
-    end = calls - 1
-    early = planes_of(dx_home, range(len(zones) - 1), range(2))
-    early_keys = [key for key in early if key[0] > 0]
-    jobs = [("dx", end, 1), ("dx", end - 1, 2)]
-    moved, arrived = moves(jobs)
-    got, part = step(moved + [(early[key], -key[0]) for key in early_keys], weight_part, dg_all, x_all)
-    arrived(got)
-    ring_terms = {turn: [early[(0, turn)]] for turn in range(2)}
-    for key, g in zip(early_keys, got[2:]):
-        ring_terms[key[1]].append(g)
-    for_pair.append(part)
-
-    a_late = planes_of(dx_home, [len(zones) - 1], [0])
-    moved, arrived = moves([("dx", end, 2)])
-    got, part = step(
-        moved + [(v, -k) for (k, _), v in a_late.items()] + [(for_pair[0], "pair")], weight_part, du_all, x_all
-    )
-    arrived(got)
-    ring_terms[0] += got[1:-1]
-    from_pair.append(got[-1])
-    for_pair.append(part)
-
-    b_late = planes_of(dx_home, [len(zones) - 1], [1])
-    moved, arrived = moves([("out", end - 3, 2), ("out", end - 1, 1)])
-    got, part = step(
-        [(v, -k) for (k, _), v in b_late.items()] + [(for_pair[1], "pair")] + moved, weight_part, hs_all, g_all
-    )
-    ring_terms[1] += got[: len(b_late)]
-    from_pair.append(got[len(b_late)])
-    arrived(got[len(b_late) + 1 :])
-    for_pair.append(part)
+            row_tiles[i + 1] = list(zip(row_nears, got))
+            if i + 2 < len(zones):
+                grad_nears = nears([half for half, _ in next_halves], got[2:])
+
+    def planes_of(home, i, turn):
+        part = home[2 * i + turn]
+        if i == 0:
+            return {0: part}
+        part = part.reshape(len(zones[i]), -1, part.shape[1])
+        return {k: part[j] for j, k in enumerate(zones[i])}
 
     def summed(terms):
         total = terms[0].astype(F32)
@@ -884,7 +948,49 @@
             total = total + term.astype(F32)
         return total
 
-    d_rows = jnp.concatenate([summed(ring_terms[turn]) for turn in range(2)], axis=0)
+    def weight_part(d, v):
+        return t_mm(d.reshape(-1, d.shape[-1])[:, side:], v.reshape(-1, v.shape[-1])).astype(BF16)
+
+    x_all, g_all, hs_all, dg_all, du_all = kept
+    dx_terms, out_terms = {0: [], 1: []}, {0: [], 1: []}
+
+    def homeward(home, keys):
+        return [(planes_of(home, i, turn)[k], -k) for i, turn, k in keys]
+
+    late = range(1, len(zones) - 1)
+    jobs = [("dx", last_call, 1), ("dx", last_call - 1, 2)]
+    jobs += [("out", 1, 2)] if 1 not in out_near or out_near[1].shape[0] == 4 * own_rows // 2 else []
+    moved, arrived = moves(jobs)
+    keys = [(i, turn, k) for i in late for turn in range(2) for k in zones[i]]
+    got, part = step(moved + homeward(dx_home, keys), weight_part, dg_all, x_all)
+    arrived(got)
+    for (_, turn, _), g in zip(keys, got[len(jobs) :]):
+        dx_terms[turn].append(g)
+    for_pair.append(part)
+
+    jobs = [("dx", last_call, 2)] + [(what, 1, 3) for what, home in (("dx", dx_home), ("out", out_home)) if 1 not in home]
+    moved, arrived = moves(jobs)
+    keys = [(len(zones) - 1, 0, k) for k in zones[-1]]
+    got, part = step(
+        moved + homeward(dx_home, keys) + [(for_pair[0], "pair")], weight_part, du_all, x_all
+    )
+    arrived(got)
+    dx_terms[0] += got[len(jobs) : -1]
+    from_pair.append(got[-1])
+    for_pair.append(part)
+
+    jobs = [("out", call, 1) for call in range(2, calls) if call not in out_near]
+    moved, arrived = moves(jobs)
+    keys = [(len(zones) - 1, 1, k) for k in zones[-1]]
+    got, part = step(
+        moved + homeward(dx_home, keys) + [(for_pair[1], "pair")], weight_part, hs_all, g_all
+    )
+    arrived(got)
+    dx_terms[1] += got[len(jobs) : -1]
+    from_pair.append(got[-1])
+    for_pair.append(part)
+
+    d_rows = jnp.concatenate([summed([dx_home[turn], *dx_terms[turn]]) for turn in range(2)], axis=0)
     d_normed = d_rows[:, :width]
     d_gates = d_rows[:, width : width + experts]
     grad_in = cotangent.astype(F32)
@@ -893,7 +999,7 @@
     d_norm, grad_gain_ffn = norm_back(hidden_one, scale_ffn, gain_ffn, d_normed)
     d_hidden_one = grad_in + d_norm
     d_attn_own = d_hidden_one.astype(BF16)
-    moved, arrived = moves([("out", end - 2, 1)])
+    moved, arrived = moves([("out", call, 2) for call in range(2, last_call) if call not in out_home])
     got = step([(d_attn_own, "x"), (for_pair[2], "pair")] + moved)
     d_near = jnp.concatenate([d_attn_own, got[0]], axis=0)
     from_pair.append(got[1])
@@ -907,76 +1013,84 @@
         ],
         axis=0,
     ).transpose(1, 0, 2)
+    g_output = t_mm(d_attn_group, saved[5]).astype(BF16)
+    g_output = [lax.dynamic_slice_in_dim(g_output, e * rows_dev, rows_dev, 0) for e in piece_e]
 
     def attend_back(*args):
         return attn_backward(heads, peers, score_scale, gain_at, rows_dev, list(args))
 
-    waiting = [("out", end, 1)]
-    waiting += [("out", call, 2) for call in range(calls) if call not in out_home and call in out_near]
-    waiting += [("out", call, 1) for call in range(calls) if call not in out_near and call != end]
-    moved, arrived = moves(waiting)
-    got, (g_mains, (near_keep, near_send, d_in_keep, d_in_send)) = step(
-        moved, attend_back,
-        places, d_attn_group, *attn_weights, gain_latent, cos, sin, *saved, normed_ffn,
+    keys = [(i, turn, k) for i in range(1, len(zones)) for turn in range(2) for k in zones[i] if 2 * i + turn < last_call]
+    moved, arrived = moves([("out", last_call, 2)])
+    shared_home = lax.all_to_all(shared_back, "expert", 0, 0, tiled=True).astype(F32)
+    got, (g_mains, g_others, (near_keep, near_send, d_in_keep, d_in_send)) = step(
+        [(jnp.concatenate(g_output[ring:], axis=0), "y")] + moved + homeward(out_home, keys), attend_back,
+        places, d_attn_group, *attn_weights, gain_latent, cos, sin, *saved[:5], *saved[6:], normed_ffn,
         jnp.pad(d_logits, ((0, 0), (ROPE, few - ROPE - experts))), token_group, grad_gain_ffn.reshape(1, width),
     )
-    arrived(got)
-    waiting = [("out", call, 2) for call in range(calls) if call not in out_home]
+    output_parts = [add(g_output[k], got[0][k * rows_dev : (k + 1) * rows_dev]) for k in range(ring)]
+    arrived(got[1:2])
+    for (_, turn, _), g in zip(keys, got[2:]):
+        out_terms[turn].append(g)
 
     def own_part(d, v, g):
-        return t_mm(d.reshape(-1, d.shape[-1])[:, :side], v.reshape(-1, v.shape[-1])) + g[:side].astype(F32)
-
-    parts = {}
-
-    def mains_y(k):
-        return (g_mains[ring + k], "y")
+        return expert_grad(d.reshape(-1, d.shape[-1]), v.reshape(-1, v.shape[-1]), g, local, ff, seg)
 
     order = [*range(1, ring), 0]
-    moved, arrived = moves(waiting)
+
+    def two_parts(i, got):
+        return [add(g_mains[k], got[j * rows_dev : (j + 1) * rows_dev]) for j, k in enumerate(order[2 * i : 2 * i + 2])]
+
+    keys = [(len(zones) - 1, 1, k) for k in zones[-1]]
     got, grad_gate = step(
-        [mains_y(order[0]), (near_send, "pair"), (d_in_send, "pair")] + moved, own_part, dg_all, x_all, from_pair[0]
-    )
-    total = add(g_mains[order[0]], got[0])
+        [(g_others[0], "y"), (near_send, "pair"), (d_in_send, "pair"), *homeward(out_home, keys)],
+        own_part, dg_all, x_all, from_pair[0],
+    )
+    main_parts = two_parts(0, got[0])
     near = add(near_keep, got[1])
     keep, d_away = split_half(add(d_in_keep, got[2]))
-    arrived(got[3:])
-    out_planes = planes_of(out_home, range(len(zones)), range(2))
-    out_rows = [jnp.concatenate([out_planes[(k, turn)] for turn in range(2)], axis=0) for k in range(ring)]
-    out_terms = [out_rows[0]]
-
     few_away = jnp.concatenate([near[1:2], near[2:]], axis=0)
     few_keep = jnp.concatenate([near[0:1], near[2:]], axis=0)
+    out_terms[1] += got[3:]
+    ffn_out = jnp.concatenate([summed([out_home[turn], *out_terms[turn]]) for turn in range(2)], axis=0)
+    block_out = (hidden_one + ffn_out).astype(BF16)
+
     got, grad_up = step(
-        [mains_y(order[1]), (total, "ring"), (few_away, "x"), (d_away, "x"), (out_rows[1], -1)],
+        [(g_others[1], "y"), (few_away, "x"), (main_parts[0], "ring"), (output_parts[order[0]], "ring")],
         own_part, du_all, x_all, from_pair[1],
     )
-    total = add(add(g_mains[order[1]], got[0]), got[1])
-    few_sum = add(few_keep, got[2])
+    main_parts += two_parts(1, got[0])
+    few_sum = add(few_keep, got[1])
     few_sum = jnp.concatenate([few_sum[j] for j in range(few_sum.shape[0])], axis=1)
-    d_normed_in = keep.astype(F32) + got[3].astype(F32)
-    out_terms.append(got[4])
+    total = add(main_parts[1], got[2])
+    total_out = add(output_parts[order[1]], got[3])
 
     few_half = few_sum.shape[0] // 2
     got, grad_down = step(
-        [mains_y(order[2]), (total, "ring"), (few_sum[few_half:], "y")], own_part, hs_all, g_all, from_pair[2]
-    )
-    total = add(add(g_mains[order[2]], got[0]), got[1])
-    few_sum = add(few_sum[:few_half], got[2])
+        [(few_sum[few_half:], "y"), (d_away, "x"), (total, "ring"), (total_out, "ring")],
+        own_part, hs_all, g_all, from_pair[2],
+    )
+    few_sum = add(few_sum[:few_half], got[0])
     few_planes = [few_sum[k * rows_dev : (k + 1) * rows_dev] for k in range(ring)]
-    shared_home = lax.all_to_all(after(shared_back, got), "expert", 0, 0, tiled=True).astype(F32)
-
-    got = step([mains_y(order[3]), (total, "ring"), *((few_planes[k], -k) for k in range(1, ring))])
-    total = add(add(g_mains[order[3]], got[0]), got[1])
+    d_normed_in = keep.astype(F32) + got[1].astype(F32)
+    total = add(main_parts[2], got[2])
+    total_out = add(output_parts[order[2]], got[3])
+
+    got = step([(total, "ring"), (total_out, "ring"), *((few_planes[k], -k) for k in range(1, ring))])
+    total = add(main_parts[3], got[0])
+    total_out = add(output_parts[order[3]], got[1])
     few_home = summed([few_planes[0], *got[2:]])
     latent_home = few_home[:, :LANES].astype(BF16)
-    for j in order[4:]:
-        got = step([mains_y(j), (total, "ring")])
-        total = add(add(g_mains[j], got[0]), got[1])
-    home = total.astype(F32)
-
-    got = step([(latent_home, "x")] + [(out_rows[k], -k) for k in range(2, ring)])
+    for i in range(2, ring // 2):
+        got = step([(g_others[i], "y")])
+        parts = two_parts(i, got[0])
+        for j, part in zip(order[2 * i : 2 * i + 2], parts):
+            got = step([(total, "ring"), (total_out, "ring")])
+            total = add(part, got[0])
+            total_out = add(output_parts[j], got[1])
+    home, home_out = total.astype(F32), total_out.astype(F32)
+
+    got = step([(latent_home, "x")])
     latent_two = jnp.stack([latent_home, got[0]])
-    block_out = (hidden_one + summed(out_terms + got[1:])).astype(BF16)
     got = step([(latent_two, "pair")])
     latent_four = jnp.concatenate([latent_two, got[0]], axis=0)
     grad_latent = jnp.zeros((shards, rows_dev, LANES), BF16)
@@ -988,9 +1102,7 @@
     tokens_grad = d_hidden_one + d_token
     gain_home = few_home[:, LANES + gain_at : LANES + gain_at + 3].astype(F32).T
 
-    grad_experts = [
-        jnp.stack([g[j * seg : j * seg + ff] for j in range(local)]) for g in (grad_gate, grad_up, grad_down)
-    ]
+    grad_experts = [grad_gate, grad_up, grad_down]
     grad_shared = [shared_home[:, i * shared : (i + 1) * shared].reshape(shared_dev, rows_dev) for i in range(3)]
 
     nope_cols = heads * NOPE
@@ -1004,7 +1116,7 @@
         ],
         axis=2,
     ).reshape(rows_dev, query_cols)
-    g_expand = home[:, query_cols + value_cols :]
+    g_expand = home[:, query_cols:]
     return (
         block_out,
         tokens_grad,
@@ -1013,7 +1125,7 @@
         grad_latent.astype(F32),
         gain_home[2, :rank_dev],
         jnp.concatenate([g_expand[h * rank_dev : (h + 1) * rank_dev] for h in range(heads)], axis=1),
-        home[:, query_cols : query_cols + value_cols].T,
+        home_out.T,
         gain_home[1],
         grad_router,
         grad_shared[0].T,

time: 802 us -> 737 us (0.919)
  waiting for transfers between devices: 260 us -> 184 us
  Pallas kernels: 227 us -> 280 us
  matrix products: 67.8 us -> 40.8 us
  local copies, waits for them, and re-layouts: 72 us -> 63.1 us
    ppermute x88 -> x96, waiting for transfers between devices: 245 us -> 184 us  [send(): return lax.ppermute(values, BOTH, tables[way])]
    pallas_call x0 -> x5, Pallas kernels: none -> 54.5 us  [the longest x3 42.7 us: expert_grad(): pl.pallas_call(kernel, grid=(width // block,), in_specs=[pl.BlockSpec((ro...]
    dot_general x8 -> x6, matrix products: 67.8 us -> 40.8 us  [dot(): return lax.dot_general(a, b, (dims, ((), ())), preferred_element_type=F32)]
    all_to_all x2 -> x1, waiting for transfers between devices: 14.7 us -> 0.01 us  [body(): lax.all_to_all(shared_back, 'expert', 0, 0, tiled=True).astype(F32)]
    convert_element_type x27 -> x30, other arithmetic: 15.6 us -> 22.1 us  [add(): return (a.astype(F32) + b.astype(F32)).astype(BF16)]
    unnamed x244 -> x287, local copies, waits for them, and re-layouts: 30.2 us -> 24.8 us
    ppermute x88 -> x96, starting transfers between devices: 98.7 us -> 98.5 us  [send(): return lax.ppermute(values, BOTH, tables[way])]
  transfers between devices with their start and end apart: 90 -> 97, of which waited for: 32 -> 30; matrix products, arithmetic and copies ran while one was open for 19% -> 19% of each run, Pallas kernels for 29% -> 38%
where the time goes in v4:
time: 737 us; the launch traced here: 729 us
  Pallas kernels  280 us (38%)
  waiting for transfers between devices  184 us (25%)
  starting transfers between devices  103 us (14%)
  local copies, waits for them, and re-layouts  63.1 us (9%)
  other arithmetic  55.2 us (7%)
  matrix products  40.8 us (6%)
    ppermute x96, waiting for transfers between devices, send(): return lax.ppermute(values, BOTH, tables[way])  184 us
    pallas_call x4, Pallas kernels, ffn_tile(): pl.pallas_call(kernel, grid=(steps,), in_specs=in_specs, out_specs=out_sp...  155 us
    ppermute x96, starting transfers between devices, send(): return lax.ppermute(values, BOTH, tables[way])  98.5 us
    pallas_call x2, Pallas kernels, in_vmem(): pl.pallas_call(kernel, in_specs=[pl.BlockSpec(memory_space=pltpu.SMEM)] +...  50.2 us
    pallas_call x3, Pallas kernels, expert_grad(): pl.pallas_call(kernel, grid=(width // block,), in_specs=[pl.BlockSpec((ro...  42.7 us
    dot_general x6, matrix products, dot(): return lax.dot_general(a, b, (dims, ((), ())), preferred_element_type=F32)  40.8 us
    unnamed x287, local copies, waits for them, and re-layouts  24.8 us
    convert_element_type x30, other arithmetic, add(): return (a.astype(F32) + b.astype(F32)).astype(BF16)  22.1 us
  transfers between devices with their start and end apart: 97, of which 30 were waited for; matrix products, arithmetic and copies ran while one was open for 19% of the time, Pallas kernels for 38%

profile of v4, /device:TPU:1, one launch (start us, length us, event | category | flops | bytes accessed | tf_op | source)
XLA Modules:
  0.0 728.9 jit_solution(17112795335228511387)
XLA Ops:
  38.1 8.0 %shard_map.298 = (bf16[3,768,2048]{2,1,0:T(8,128)(2,1)}, bf16[3,1792,2048]{2,1,0:T(8,128)(2,1)}) custom-call(bf16[2,352,2048]{2,1,0:T(8,128)(2,1)S(1)} %bitcast.140, bf16[2,352,2048]{2,1,0:T(8,128)(2,1)S(1)} %bitcast.141, bf16[2,352,2048]{2,1,0:T(8,128)(2,1)S(1)} %copy-done.2), custom_call_target="tpu_custom_call" | custom-call | bytes 31457280 | tf_op jit(solution)/shard_map/pallas_call | solution.py:562
  46.2 13.2 %collective-permute-done.5 = bf16[256,256]{1,0:T(8,128)(2,1)S(1)} collective-permute-done((bf16[256,256]{1,0:T(8,128)(2,1)S(1)}, bf16[256,256]{1,0:T(8,128)(2,1)S(1)}, u32[]{:S(2)}, u32[]{:S(2)}) %collective-permute-start.5) | collective-permute-done | bytes 131104 | tf_op jit(solution)/shard_map/ppermute | solution.py:650
  73.3 18.2 %collective-permute-done.9.refs_16_ = bf16[256,1792]{1,0:T(8,128)(2,1)S(1)} collective-permute-done((bf16[256,1792]{1,0:T(8,128)(2,1)S(1)}, bf16[256,1792]{1,0:T(8,128)(2,1)S(1)}, u32[]{:S(2)}, u32[]{:S(2)}) %collective-permute-start.9) | collective-permute-done | bytes 917536 | tf_op jit(solution)/shard_map/ppermute | solution.py:650
  110.9 11.8 %collective-permute-done.13 = bf16[128,2176]{1,0:T(8,128)(2,1)S(1)} collective-permute-done((bf16[128,2176]{1,0:T(8,128)(2,1)S(1)}, bf16[128,2176]{1,0:T(8,128)(2,1)S(1)}, u32[]{:S(2)}, u32[]{:S(2)}) %collective-permute-start.13) | collective-permute-done | bytes 557088 | tf_op jit(solution)/shard_map/ppermute | solution.py:650
  127.5 14.1 %collective-permute-done.19 = bf16[128,2176]{1,0:T(8,128)(2,1)S(1)} collective-permute-done((bf16[128,2176]{1,0:T(8,128)(2,1)}, bf16[128,2176]{1,0:T(8,128)(2,1)S(1)}, u32[]{:S(2)}, u32[]{:S(2)}) %collective-permute-start.19) | collective-permute-done | bytes 557088 | tf_op jit(solution)/shard_map/ppermute | solution.py:650
  152.8 21.5 %shard_map.299 = (bf16[256,2048]{1,0:T(8,128)(2,1)}, bf16[256,2048]{1,0:T(8,128)(2,1)}, bf16[512,2048]{1,0:T(8,128)(2,1)}, bf16[512,768]{1,0:T(8,128)(2,1)}, bf1...) custom-call(s32[12]{0:T(128)} %stack.186.refs_0_, ...), custom_call_target="tpu_custom_call" | custom-call | flops 6000000000 | bytes 25165824 | tf_op jit(solution)/shard_map/pallas_call | solution.py:290
  203.2 11.5 %shard_map.301.refs_6_.refs_7_.refs_8_ = bf16[3,1792,2048]{2,1,0:T(8,128)(2,1)} custom-call(bf16[3,768,2048]{2,1,0:T(8,128)(2,1)} %collective-permute-done.12.other_ref, bf16[3,256,2048]{2,1,0:T(8,128)(2,1)S(1)} %pad_maximum_fusion.shared_ref, bf16[3,1792,2048]{2,1,0:T(8,128)(2,1)} %get-tuple-element.341._), custom_call_target="tpu_custom_call", output_to_operand_aliasing={{}: (2, {})} | custom-call | bytes 23068672 | tf_op jit(solution)/shard_map/pallas_call | solution.py:587
  219.4 12.0 %collective-permute-done.29 = bf16[128,2048]{1,0:T(8,128)(2,1)S(1)} collective-permute-done((bf16[128,2048]{1,0:T(8,128)(2,1)S(1)}, bf16[128,2048]{1,0:T(8,128)(2,1)S(1)}, u32[]{:S(2)}, u32[]{:S(2)}) %collective-permute-start.29) | collective-permute-done | bytes 524320 | tf_op jit(solution)/shard_map/ppermute | solution.py:650
  249.7 10.5 %collective-permute-done.35 = bf16[128,2048]{1,0:T(8,128)(2,1)S(1)} collective-permute-done((bf16[128,2048]{1,0:T(8,128)(2,1)S(1)}, bf16[128,2048]{1,0:T(8,128)(2,1)S(1)}, u32[]{:S(2)}, u32[]{:S(2)}) %collective-permute-start.35) | collective-permute-done | bytes 524320 | tf_op jit(solution)/shard_map/ppermute | solution.py:650
  271.0 38.9 %shard_map.302 = (bf16[256,2176]{1,0:T(8,128)(2,1)}, bf16[256,2176]{1,0:T(8,128)(2,1)}, bf16[256,2048]{1,0:T(8,128)(2,1)}, bf16[256,2048]{1,0:T(8,128)(2,1)}, bf...) custom-call(s32[1]{0:T(128)} %bitcast.47.refs_0_, ...), custom_call_target="tpu_custom_call" | custom-call | flops 22548578304 | bytes 30408704 | tf_op jit(solution)/shard_map/pallas_call | solution.py:474
  313.4 39.0 %shard_map.303 = (bf16[256,2176]{1,0:T(8,128)(2,1)}, bf16[256,2176]{1,0:T(8,128)(2,1)}, bf16[256,2048]{1,0:T(8,128)(2,1)}, bf16[256,2048]{1,0:T(8,128)(2,1)}, bf...) custom-call(s32[1]{0:T(128)} %bitcast.47.refs_0_, ...), custom_call_target="tpu_custom_call", output_to_operand_aliasing={{4}: (9, {}), {5}: (10, {}), {6}: (11, {}), {7}: (12, {}), ... | custom-call | flops 22548578304 | bytes 30408704 | tf_op jit(solution)/shard_map/pallas_call | solution.py:474
  357.9 38.6 %shard_map.304 = (bf16[256,2176]{1,0:T(8,128)(2,1)}, bf16[256,2176]{1,0:T(8,128)(2,1)}, bf16[256,2048]{1,0:T(8,128)(2,1)}, bf16[256,2048]{1,0:T(8,128)(2,1)}, bf...) custom-call(s32[1]{0:T(128)} %bitcast.47.refs_0_, ...), custom_call_target="tpu_custom_call", output_to_operand_aliasing={{4}: (9, {}), {5}: (10, {}), {6}: (11, {}), {7}: (12, {}), ... | custom-call | flops 22548578304 | bytes 30408704 | tf_op jit(solution)/shard_map/pallas_call | solution.py:474
  403.5 38.7 %shard_map.305 = (bf16[256,2176]{1,0:T(8,128)(2,1)}, bf16[256,2176]{1,0:T(8,128)(2,1)}, bf16[256,2048]{1,0:T(8,128)(2,1)}, bf16[256,2048]{1,0:T(8,128)(2,1)}, bf...) custom-call(s32[1]{0:T(128)} %bitcast.47.refs_0_, ...), custom_call_target="tpu_custom_call", output_to_operand_aliasing={{4}: (9, {}), {5}: (10, {}), {6}: (11, {}), {7}: (12, {}), ... | custom-call | flops 22548578304 | bytes 30408704 | tf_op jit(solution)/shard_map/pallas_call | solution.py:474
  447.4 12.5 %fusion.6 = bf16[1024,2048]{1,0:T(8,128)(2,1)} fusion(bf16[2048,2048]{1,0:T(8,128)(2,1)S(1)} %bitcast.144, bf16[2048,1792]{1,0:T(8,128)(2,1)} %bitcast.154), kind=kOutput, calls=%fused_computation.6 | convolution fusion | flops 8592031744 | bytes 16777216 | tf_op jit(solution)/shard_map/dot_general | solution.py:52
  462.6 11.9 %collective-permute-start.62 = (bf16[1024,2048]{1,0:T(8,128)(2,1)}, bf16[1024,2048]{1,0:T(8,128)(2,1)S(1)}, u32[]{:S(2)}, u32[]{:S(2)}) collective-permute-start(bf16[1024,2048]{1,0:T(8,128)(2,1)} %fusion.6), channel_id=1, source_target_pairs={{0,1},{1,0},{2,3},{3,2},{4,5},{5,4},{6,7},{7,6},{8,9},{9,8},{10,11... | collective-permute-start | bytes 12582920 | tf_op jit(solution)/shard_map/ppermute | solution.py:650
  477.0 13.1 %fusion.9 = bf16[1024,2048]{1,0:T(8,128)(2,1)} fusion(bf16[2048,2048]{1,0:T(8,128)(2,1)S(1)} %bitcast.145, bf16[2048,1792]{1,0:T(8,128)(2,1)} %bitcast.156), kind=kOutput, calls=%fused_computation.7 | convolution fusion | flops 8592031744 | bytes 16777216 | tf_op jit(solution)/shard_map/dot_general | solution.py:52
  506.9 10.9 %fusion.12 = bf16[1024,2048]{1,0:T(8,128)(2,1)} fusion(bf16[2048,2048]{1,0:T(8,128)(2,1)S(1)} %bitcast.149, bf16[2048,1792]{1,0:T(8,128)(2,1)S(1)} %bitcast.153), kind=kOutput, calls=%fused_computation.8 | convolution fusion | flops 8592031744 | bytes 16777216 | tf_op jit(solution)/shard_map/dot_general | solution.py:52
  539.6 8.3 %collective-permute-done.68 = bf16[128,2048]{1,0:T(8,128)(2,1)S(1)} collective-permute-done((bf16[128,2048]{1,0:T(8,128)(2,1)S(1)}, bf16[128,2048]{1,0:T(8,128)(2,1)S(1)}, u32[]{:S(2)}, u32[]{:S(2)}) %collective-permute-start.68) | collective-permute-done | bytes 524320 | tf_op jit(solution)/shard_map/ppermute | solution.py:650
  575.0 28.7 %shard_map.306 = (bf16[256,1024]{1,0:T(8,128)(2,1)}, bf16[256,1024]{1,0:T(8,128)(2,1)}, bf16[256,1024]{1,0:T(8,128)(2,1)}, bf16[256,1024]{1,0:T(8,128)(2,1)}, bf...) custom-call(s32[12]{0:T(128)} %stack.186.refs_0_, ...), custom_call_target="tpu_custom_call" | custom-call | flops 12000000000 | bytes 25165824 | tf_op jit(solution)/shard_map/pallas_call | solution.py:290
  613.0 14.3 %shard_map.307 = f32[2,352,2048]{2,1,0:T(8,128)} custom-call(bf16[2048,1792]{1,0:T(8,128)(2,1)} %bitcast.155, bf16[2048,2048]{1,0:T(8,128)(2,1)} %bitcast.142, bf16[1024,2048]{1,0:T(8,128)(2,1)} %copy-done.8), custom_call_target="tpu_custom_call" | custom-call | flops 6442450944 | bytes 20971520 | tf_op jit(solution)/shard_map/pallas_call | solution.py:533
  637.8 14.2 %shard_map.308 = f32[2,352,2048]{2,1,0:T(8,128)} custom-call(bf16[2048,1792]{1,0:T(8,128)(2,1)} %bitcast.157, bf16[2048,2048]{1,0:T(8,128)(2,1)} %bitcast.143, bf16[1024,2048]{1,0:T(8,128)(2,1)} %collective-permute-done.67.got_ref), custom_call_target="tpu_custom_call" | custom-call | flops 6442450944 | bytes 20971520 | tf_op jit(solution)/shard_map/pallas_call | solution.py:533
  665.0 14.2 %shard_map.309 = f32[2,352,2048]{2,1,0:T(8,128)} custom-call(bf16[2048,1792]{1,0:T(8,128)(2,1)} %bitcast.150, bf16[2048,2048]{1,0:T(8,128)(2,1)} %bitcast.146, bf16[1024,2048]{1,0:T(8,128)(2,1)} %collective-permute-done.69.got_ref), custom_call_target="tpu_custom_call" | custom-call | flops 6442450944 | bytes 20971520 | tf_op jit(solution)/shard_map/pallas_call | solution.py:533
  688.7 11.6 %collective-permute-done.89 = bf16[256,256]{1,0:T(8,128)(2,1)S(1)} collective-permute-done((bf16[256,256]{1,0:T(8,128)(2,1)S(1)}, bf16[256,256]{1,0:T(8,128)(2,1)S(1)}, u32[]{:S(2)}, u32[]{:S(2)}) %collective-permute-start.89) | collective-permute-done | bytes 131104 | tf_op jit(solution)/shard_map/ppermute | solution.py:650
  700.3 14.0 %collective-permute-done.90 = bf16[256,256]{1,0:T(8,128)(2,1)S(1)} collective-permute-done((bf16[256,256]{1,0:T(8,128)(2,1)S(1)}, bf16[256,256]{1,0:T(8,128)(2,1)S(1)}, u32[]{:S(2)}, u32[]{:S(2)}) %collective-permute-start.90) | collective-permute-done | bytes 131104 | tf_op jit(solution)/shard_map/ppermute | solution.py:650
  (667 shorter events, 295.5 us)
Async XLA Ops:
  150.6 41.7 %collective-permute-start.23 = (bf16[256,2176]{1,0:T(8,128)(2,1)}, bf16[256,2176]{1,0:T(8,128)(2,1)}, u32[]{:S(2)}, u32[]{:S(2)}) collective-permute-start(bf16[256,2176]{1,0:T(8,128)(2,1)} %pad_maximum_fusion.2.refs_3_), channel_id=1, source_target_pairs={{0,2},{1,3},{2,0},{3,1},{4,6},{5,7},{6,4},{7,5},{8,10},{9,11},{10,... | collective-permute-start | bytes 3342344 | tf_op jit(solution)/shard_map/ppermute | solution.py:650
  151.6 40.8 %collective-permute-start.24 = (bf16[256,2176]{1,0:T(8,128)(2,1)S(1)}, bf16[256,2176]{1,0:T(8,128)(2,1)}, u32[]{:S(2)}, u32[]{:S(2)}) collective-permute-start(bf16[256,2176]{1,0:T(8,128)(2,1)S(1)} %pad_maximum_fusion.3.refs_3_), channel_id=1, source_target_pairs={{0,4},{1,5},{2,6},{3,7},{4,0},{5,1},{6,2},{7,3},{8,12},{9,13},{10,... | collective-permute-start | bytes 3342344 | tf_op jit(solution)/shard_map/ppermute | solution.py:650
  268.1 41.9 %collective-permute-start.39 = (bf16[128,2048]{1,0:T(8,128)(2,1)S(1)}, bf16[128,2048]{1,0:T(8,128)(2,1)S(1)}, u32[]{:S(2)}, u32[]{:S(2)}) collective-permute-start(bf16[128,2048]{1,0:T(8,128)(2,1)S(1)} %bitcast.177), channel_id=1, source_target_pairs={{0,2},{1,3},{2,0},{3,1},{4,6},{5,7},{6,4},{7,5},{8,10},{9,11},{10,... | collective-permute-start | bytes 1572872 | tf_op jit(solution)/shard_map/ppermute | solution.py:650
  269.2 40.9 %collective-permute-start.38 = (bf16[128,2048]{1,0:T(8,128)(2,1)S(1)}, bf16[128,2048]{1,0:T(8,128)(2,1)S(1)}, u32[]{:S(2)}, u32[]{:S(2)}) collective-permute-start(bf16[128,2048]{1,0:T(8,128)(2,1)S(1)} %bitcast.175), channel_id=1, source_target_pairs={{0,4},{1,5},{2,6},{3,7},{4,0},{5,1},{6,2},{7,3},{8,12},{9,13},{10,... | collective-permute-start | bytes 1572872 | tf_op jit(solution)/shard_map/ppermute | solution.py:650
  270.5 39.8 %collective-permute-start.40 = (bf16[256,2176]{1,0:T(8,128)(2,1)S(1)}, bf16[256,2176]{1,0:T(8,128)(2,1)S(1)}, u32[]{:S(2)}, u32[]{:S(2)}) collective-permute-start(bf16[256,2176]{1,0:T(8,128)(2,1)S(1)} %pad_maximum_fusion.4.refs_3_), channel_id=1, source_target_pairs={{0,2},{1,3},{2,0},{3,1},{4,6},{5,7},{6,4},{7,5},{8,10},{9,11},{10,... | collective-permute-start | bytes 3342344 | tf_op jit(solution)/shard_map/ppermute | solution.py:650
  270.8 39.5 %collective-permute-start.41 = (bf16[256,2176]{1,0:T(8,128)(2,1)S(1)}, bf16[256,2176]{1,0:T(8,128)(2,1)S(1)}, u32[]{:S(2)}, u32[]{:S(2)}) collective-permute-start(bf16[256,2176]{1,0:T(8,128)(2,1)S(1)} %pad_maximum_fusion.5.refs_3_), channel_id=1, source_target_pairs={{0,4},{1,5},{2,6},{3,7},{4,0},{5,1},{6,2},{7,3},{8,12},{9,13},{10,... | collective-permute-start | bytes 3342344 | tf_op jit(solution)/shard_map/ppermute | solution.py:650
  310.3 42.2 %collective-permute-start.42 = (bf16[256,2048]{1,0:T(8,128)(2,1)}, bf16[256,2048]{1,0:T(8,128)(2,1)}, u32[]{:S(2)}, u32[]{:S(2)}) collective-permute-start(bf16[256,2048]{1,0:T(8,128)(2,1)} %get-tuple-element.368), channel_id=1, source_target_pairs={{0,24},{1,25},{2,26},{3,27},{4,28},{5,29},{6,30},{7,31},{8,0},{9,1... | collective-permute-start | bytes 3145736 | tf_op jit(solution)/shard_map/ppermute | solution.py:650
  311.4 42.8 %collective-permute-start.43 = (bf16[256,2176]{1,0:T(8,128)(2,1)}, bf16[256,2176]{1,0:T(8,128)(2,1)}, u32[]{:S(2)}, u32[]{:S(2)}) collective-permute-start(bf16[256,2176]{1,0:T(8,128)(2,1)} %get-tuple-element.379), channel_id=1, source_target_pairs={{0,24},{1,25},{2,26},{3,27},{4,28},{5,29},{6,30},{7,31},{8,0},{9,1... | collective-permute-start | bytes 3342344 | tf_op jit(solution)/shard_map/ppermute | solution.py:650
  312.0 43.9 %collective-permute-start.44 = (bf16[256,2048]{1,0:T(8,128)(2,1)S(1)}, bf16[256,2048]{1,0:T(8,128)(2,1)}, u32[]{:S(2)}, u32[]{:S(2)}) collective-permute-start(bf16[256,2048]{1,0:T(8,128)(2,1)S(1)} %pad_maximum_fusion.10.refs_1_), channel_id=1, source_target_pairs={{0,2},{1,3},{2,0},{3,1},{4,6},{5,7},{6,4},{7,5},{8,10},{9,11},{10,... | collective-permute-start | bytes 3145736 | tf_op jit(solution)/shard_map/ppermute | solution.py:650
  313.1 42.8 %collective-permute-start.45 = (bf16[256,2048]{1,0:T(8,128)(2,1)S(1)}, bf16[256,2048]{1,0:T(8,128)(2,1)S(1)}, u32[]{:S(2)}, u32[]{:S(2)}) collective-permute-start(bf16[256,2048]{1,0:T(8,128)(2,1)S(1)} %pad_maximum_fusion.11.refs_1_), channel_id=1, source_target_pairs={{0,4},{1,5},{2,6},{3,7},{4,0},{5,1},{6,2},{7,3},{8,12},{9,13},{10,... | collective-permute-start | bytes 3145736 | tf_op jit(solution)/shard_map/ppermute | solution.py:650
  355.9 40.6 %collective-permute-start.46 = (bf16[128,2048]{1,0:T(8,128)(2,1)S(1)}, bf16[128,2048]{1,0:T(8,128)(2,1)S(1)}, u32[]{:S(2)}, u32[]{:S(2)}) collective-permute-start(bf16[128,2048]{1,0:T(8,128)(2,1)S(1)} %slice.570), channel_id=1, source_target_pairs={{0,2},{1,3},{2,0},{3,1},{4,6},{5,7},{6,4},{7,5},{8,10},{9,11},{10,... | collective-permute-start | bytes 1572872 | tf_op jit(solution)/shard_map/ppermute | solution.py:650
  356.9 39.8 %collective-permute-start.48 = (bf16[128,2176]{1,0:T(8,128)(2,1)S(1)}, bf16[128,2176]{1,0:T(8,128)(2,1)S(1)}, u32[]{:S(2)}, u32[]{:S(2)}) collective-permute-start(bf16[128,2176]{1,0:T(8,128)(2,1)S(1)} %slice.569), channel_id=1, source_target_pairs={{0,2},{1,3},{2,0},{3,1},{4,6},{5,7},{6,4},{7,5},{8,10},{9,11},{10,... | collective-permute-start | bytes 1671176 | tf_op jit(solution)/shard_map/ppermute | solution.py:650
  357.5 40.1 %collective-permute-start.47 = (bf16[256,2176]{1,0:T(8,128)(2,1)}, bf16[256,2176]{1,0:T(8,128)(2,1)S(1)}, u32[]{:S(2)}, u32[]{:S(2)}) collective-permute-start(bf16[256,2176]{1,0:T(8,128)(2,1)} %get-tuple-element.391), channel_id=1, source_target_pairs={{0,24},{1,25},{2,26},{3,27},{4,28},{5,29},{6,30},{7,31},{8,0},{9,1... | collective-permute-start | bytes 3342344 | tf_op jit(solution)/shard_map/ppermute | solution.py:650
  398.3 44.9 %collective-permute-start.52 = (bf16[256,2048]{1,0:T(8,128)(2,1)}, bf16[256,2048]{1,0:T(8,128)(2,1)S(1)}, u32[]{:S(2)}, u32[]{:S(2)}) collective-permute-start(bf16[256,2048]{1,0:T(8,128)(2,1)} %get-tuple-element.425), channel_id=1, source_target_pairs={{0,24},{1,25},{2,26},{3,27},{4,28},{5,29},{6,30},{7,31},{8,0},{9,1... | collective-permute-start | bytes 3145736 | tf_op jit(solution)/shard_map/ppermute | solution.py:650
  401.0 43.3 %collective-permute-start.51 = (bf16[256,2176]{1,0:T(8,128)(2,1)}, bf16[256,2176]{1,0:T(8,128)(2,1)S(1)}, u32[]{:S(2)}, u32[]{:S(2)}) collective-permute-start(bf16[256,2176]{1,0:T(8,128)(2,1)} %get-tuple-element.424), channel_id=1, source_target_pairs={{0,2},{1,3},{2,0},{3,1},{4,6},{5,7},{6,4},{7,5},{8,10},{9,11},{10,... | collective-permute-start | bytes 3342344 | tf_op jit(solution)/shard_map/ppermute | solution.py:650
  401.9 40.4 %collective-permute-start.53 = (bf16[128,2176]{1,0:T(8,128)(2,1)S(1)}, bf16[128,2176]{1,0:T(8,128)(2,1)S(1)}, u32[]{:S(2)}, u32[]{:S(2)}) collective-permute-start(bf16[128,2176]{1,0:T(8,128)(2,1)S(1)} %slice.572), channel_id=1, source_target_pairs={{0,4},{1,5},{2,6},{3,7},{4,0},{5,1},{6,2},{7,3},{8,12},{9,13},{10,... | collective-permute-start | bytes 1671176 | tf_op jit(solution)/shard_map/ppermute | solution.py:650
  402.1 42.6 %collective-permute-start.50 = (bf16[64,2176]{1,0:T(8,128)(2,1)S(1)}, bf16[64,2176]{1,0:T(8,128)(2,1)S(1)}, u32[]{:S(2)}, u32[]{:S(2)}) collective-permute-start(bf16[64,2176]{1,0:T(8,128)(2,1)S(1)} %slice.574), channel_id=1, source_target_pairs={{0,4},{1,5},{2,6},{3,7},{4,0},{5,1},{6,2},{7,3},{8,12},{9,13},{10,... | collective-permute-start | bytes 835592 | tf_op jit(solution)/shard_map/ppermute | solution.py:650
  403.4 41.2 %collective-permute-start.49 = (bf16[64,2048]{1,0:T(8,128)(2,1)S(1)}, bf16[64,2048]{1,0:T(8,128)(2,1)S(1)}, u32[]{:S(2)}, u32[]{:S(2)}) collective-permute-start(bf16[64,2048]{1,0:T(8,128)(2,1)S(1)} %slice.575), channel_id=1, source_target_pairs={{0,4},{1,5},{2,6},{3,7},{4,0},{5,1},{6,2},{7,3},{8,12},{9,13},{10,... | collective-permute-start | bytes 786440 | tf_op jit(solution)/shard_map/ppermute | solution.py:650
  462.6 40.8 %collective-permute-start.62 = (bf16[1024,2048]{1,0:T(8,128)(2,1)}, bf16[1024,2048]{1,0:T(8,128)(2,1)S(1)}, u32[]{:S(2)}, u32[]{:S(2)}) collective-permute-start(bf16[1024,2048]{1,0:T(8,128)(2,1)} %fusion.6), channel_id=1, source_target_pairs={{0,1},{1,0},{2,3},{3,2},{4,5},{5,4},{6,7},{7,6},{8,9},{9,8},{10,11... | collective-permute-start | bytes 12582920 | tf_op jit(solution)/shard_map/ppermute | solution.py:650
  555.2 51.8 %all-to-all-start = ((bf16[8,264,256]{2,1,0:T(8,128)(2,1)}), bf16[8,264,256]{2,1,0:T(8,128)(2,1)S(1)}, u32[]{:S(2)}, u32[]{:S(2)}) async-start(bf16[8,264,256]{2,1,0:T(8,128)(2,1)} %maximum_bitcast_fusion), calls=%async_computation | async-start | bytes 2162688 | tf_op jit(solution)/shard_map/all_to_all | solution.py:1024
  567.8 37.0 %collective-permute-start.74 = (bf16[128,2048]{1,0:T(8,128)(2,1)}, bf16[128,2048]{1,0:T(8,128)(2,1)}, u32[]{:S(2)}, u32[]{:S(2)}) collective-permute-start(bf16[128,2048]{1,0:T(8,128)(2,1)} %slice.597), channel_id=1, source_target_pairs={{0,2},{1,3},{2,0},{3,1},{4,6},{5,7},{6,4},{7,5},{8,10},{9,11},{10,... | collective-permute-start | bytes 1572872 | tf_op jit(solution)/shard_map/ppermute | solution.py:650
  570.1 38.2 %collective-permute-start.75 = (bf16[1024,512]{1,0:T(8,128)(2,1)}, bf16[1024,512]{1,0:T(8,128)(2,1)}, u32[]{:S(2)}, u32[]{:S(2)}) collective-permute-start(bf16[1024,512]{1,0:T(8,128)(2,1)} %pad_maximum_fusion.13), channel_id=1, source_target_pairs={{0,4},{1,5},{2,6},{3,7},{4,0},{5,1},{6,2},{7,3},{8,12},{9,13},{10,... | collective-permute-start | bytes 3145736 | tf_op jit(solution)/shard_map/ppermute | solution.py:650
  681.8 35.9 %collective-permute-start.93 = (bf16[256,512]{1,0:T(8,128)(2,1)S(1)}, bf16[256,512]{1,0:T(8,128)(2,1)S(1)}, u32[]{:S(2)}, u32[]{:S(2)}) collective-permute-start(bf16[256,512]{1,0:T(8,128)(2,1)S(1)} %add_convert_fusion.35), channel_id=1, source_target_pairs={{0,8},{1,9},{2,10},{3,11},{4,12},{5,13},{6,14},{7,15},{8,16},{9,17... | collective-permute-start | bytes 786440 | tf_op jit(solution)/shard_map/ppermute | solution.py:650
  682.0 37.7 %collective-permute-start.92 = (bf16[256,1024]{1,0:T(8,128)(2,1)}, bf16[256,1024]{1,0:T(8,128)(2,1)S(1)}, u32[]{:S(2)}, u32[]{:S(2)}) collective-permute-start(bf16[256,1024]{1,0:T(8,128)(2,1)} %add_convert_fusion.18), channel_id=1, source_target_pairs={{0,8},{1,9},{2,10},{3,11},{4,12},{5,13},{6,14},{7,15},{8,16},{9,17... | collective-permute-start | bytes 1572872 | tf_op jit(solution)/shard_map/ppermute | solution.py:650
  (204 other events, 3089.8 us)

commit v5 on v4

--- a/solution.py
+++ b/solution.py
@@ -493,27 +493,48 @@
 
 
 def pick_pieces(order, sources):
-    n, lanes = sources[0].shape[0], sources[0].shape[2]
+    n, _, lanes = sources[0].shape
     heights = [v.shape[1] for v in sources]
-    shape = (n, sum(heights), lanes)
-
-    def kernel(_, *refs):
-        at = 0
-        for ref, high in zip(refs, heights):
-            refs[-1][0, at : at + high] = ref[0]
-            at += high
-
-    return pl.pallas_call(
-        kernel,
-        grid_spec=pltpu.PrefetchScalarGridSpec(
-            num_scalar_prefetch=1,
-            grid=(n,),
-            in_specs=[pl.BlockSpec((1, h, lanes), lambda p, order: (order[p], 0, 0)) for h in heights],
-            out_specs=pl.BlockSpec((1, *shape[1:]), lambda p, order: (p, 0, 0)),
-        ),
-        out_shape=jax.ShapeDtypeStruct(shape, sources[0].dtype),
-        cost_estimate=pl.CostEstimate(flops=0, bytes_accessed=2**21, transcendentals=0),
-    )(order, *sources)
+
+    def kernel(order_ref, *refs):
+        for p in range(n):
+            at = 0
+            for ref, high in zip(refs, heights):
+                refs[-1][p, at : at + high] = ref[order_ref[p]]
+                at += high
+
+    outs = [jax.ShapeDtypeStruct((n, sum(heights), lanes), BF16)]
+    return in_vmem(kernel, outs, [], 0, [order, *sources])[0]
+
+
+def place_pieces(places, pieces):
+    _, rows, lanes = pieces[0].shape
+    n = len(pieces)
+
+    def kernel(places_ref, *refs):
+        for k in range(n):
+            for flip in range(2):
+                refs[-1][places_ref[flip * n + k]] = refs[k][flip]
+
+    outs = [jax.ShapeDtypeStruct((2 * n, rows, lanes), BF16)]
+    return in_vmem(kernel, outs, [], 0, [places, *pieces])[0]
+
+
+def output_grad(places, d_attn, mixed, rows, peers):
+    width, value_cols = d_attn.shape[1], mixed.shape[1]
+    ring = peers // 2
+
+    def kernel(places_ref, d_ref, mixed_ref, own, other, total):
+        for lo in range(0, width, width // 4):
+            total[lo : lo + width // 4] = t_mm(d_ref[:, lo : lo + width // 4], mixed_ref[...]).astype(BF16)
+        for p in range(peers):
+            at = pl.ds(pl.multiple_of(places_ref[p] * rows, rows), rows)
+            to = p % ring * rows
+            (own if p < ring else other)[to : to + rows] = total[at, :]
+
+    outs = [jax.ShapeDtypeStruct((ring * rows, value_cols), BF16)] * 2
+    scratch = [pltpu.VMEM((width, value_cols), BF16)]
+    return in_vmem(kernel, outs, scratch, 2 * 10**9, [places, d_attn, mixed])
 
 
 def expert_grad(d, v, got, local, ff, seg):
@@ -651,7 +672,10 @@
 
     def step(sends, work=None, *args):
         nonlocal last
-        values, args = after(([v for v, _ in sends], args), last)
+        values = [v for v, _ in sends]
+        if last:
+            values, tied = after((values, args[:1]), last)
+            args = (*tied, *args[1:])
         got = [send(v, way) for v, (_, way) in zip(values, sends)]
         done = work(*args) if work else None
         last = [got, done]
@@ -661,9 +685,6 @@
     piece_e = plane_e + [e ^ 1 for e in plane_e]
     shard_order = [me_s, me_s ^ 2, me_s ^ 1, me_s ^ 3]
     places = jnp.stack([*piece_e, *shard_order]).astype(jnp.int32)
-    piece_of = jnp.stack(
-        [lax.rem(me_e // 2 + ring - e // 2, ring) + ring * (lax.rem(me_e, 2) ^ (e % 2)) for e in range(peers)]
-    ).astype(jnp.int32)
 
     orders = (("y", "x"), ("x", "y"))
     zones = [list(range(k, min(k + 2, ring))) for k in range(0, ring, 2)]
@@ -737,7 +758,7 @@
     grad_halves = zone_halves(grad_blocks)
     shared_ways = [jnp.stack([shared_keep[k], got[2][k]]) for k in range(ring)]
 
-    def places_in_group():
+    def places_in_group(segments):
         order = jnp.concatenate([s * own_rows + jnp.arange(own_rows, dtype=jnp.int32) for s in shard_order])
         segment = jnp.concatenate(
             [lax.dynamic_slice_in_dim(segments, s * own_rows, own_rows, 0) for s in shard_order], axis=0
@@ -769,7 +790,7 @@
             (main_own[1][:, :main_cols], "ring"), (main_own[1], "y"), (small_far, "y"), (token_near, "pair"),
             (own_side, "pair"),
         ],
-        places_in_group,
+        places_in_group, segments,
     )
     cos, sin = around[:2]
     main_own.append(got[0])
@@ -804,18 +825,15 @@
     mains = main_own + main_other
 
     gain_at = ROPE + experts
-    def attend(small_in, mains_in, *args):
-        return attn_forward(heads, peers, score_scale, gain_at, list(args), small_in, mains_in)
+    def attend(token_in, small_in, mains_in, places_in, *args):
+        return attn_forward(heads, peers, score_scale, gain_at, [places_in, token_in, *args], small_in, mains_in)
 
     got, outs = step(
         [(near, two) for near, (_, two) in zip(grad_nears, orders)] + [(shared_ways[k], k) for k in range(1, ring)],
-        attend, small_all, mains,
-        places, token_group, latent_x, latent_pair, *around,
+        attend, token_group, small_all, mains, places, latent_x, latent_pair, *around,
     )
     grad_tiles = {0: list(zip(grad_nears, got))}
-    shared_all = pick_pieces(
-        piece_of, [jnp.stack([pieces[flip] for flip in range(2) for pieces in (shared_ways[0], *got[2:])])]
-    )
+    shared_all = place_pieces(places[:peers], [shared_ways[0], *got[2:]])
     shared_all = shared_all.transpose(1, 0, 2).reshape(3, shared, width)
     shared_own = jnp.pad(shared_all, ((0, 0), (0, tail - shared), (0, 0)))
     saved, attn_weights = outs[2:10], outs[12:]
@@ -968,7 +986,7 @@
         dx_terms[turn].append(g)
     for_pair.append(part)
 
-    jobs = [("dx", last_call, 2)] + [(what, 1, 3) for what, home in (("dx", dx_home), ("out", out_home)) if 1 not in home]
+    jobs = [("dx", last_call, 2)] + ([("dx", 1, 3)] if 1 not in dx_home else [])
     moved, arrived = moves(jobs)
     keys = [(len(zones) - 1, 0, k) for k in zones[-1]]
     got, part = step(
@@ -1013,23 +1031,25 @@
         ],
         axis=0,
     ).transpose(1, 0, 2)
-    g_output = t_mm(d_attn_group, saved[5]).astype(BF16)
-    g_output = [lax.dynamic_slice_in_dim(g_output, e * rows_dev, rows_dev, 0) for e in piece_e]
-
-    def attend_back(*args):
-        return attn_backward(heads, peers, score_scale, gain_at, rows_dev, list(args))
+    output_own, output_other = output_grad(places, d_attn_group, saved[5], rows_dev, peers)
+
+    def attend_back(d_attn, *args):
+        return attn_backward(heads, peers, score_scale, gain_at, rows_dev, [places, d_attn, *args])
 
     keys = [(i, turn, k) for i in range(1, len(zones)) for turn in range(2) for k in zones[i] if 2 * i + turn < last_call]
-    moved, arrived = moves([("out", last_call, 2)])
+    jobs = [("out", last_call, 2)] + ([("out", 1, 3)] if 1 not in out_home else [])
+    moved, arrived = moves(jobs)
     shared_home = lax.all_to_all(shared_back, "expert", 0, 0, tiled=True).astype(F32)
     got, (g_mains, g_others, (near_keep, near_send, d_in_keep, d_in_send)) = step(
-        [(jnp.concatenate(g_output[ring:], axis=0), "y")] + moved + homeward(out_home, keys), attend_back,
-        places, d_attn_group, *attn_weights, gain_latent, cos, sin, *saved[:5], *saved[6:], normed_ffn,
+        [(output_other, "y")] + moved + homeward(out_home, keys), attend_back,
+        d_attn_group, *attn_weights, gain_latent, cos, sin, *saved[:5], *saved[6:], normed_ffn,
         jnp.pad(d_logits, ((0, 0), (ROPE, few - ROPE - experts))), token_group, grad_gain_ffn.reshape(1, width),
     )
-    output_parts = [add(g_output[k], got[0][k * rows_dev : (k + 1) * rows_dev]) for k in range(ring)]
-    arrived(got[1:2])
-    for (_, turn, _), g in zip(keys, got[2:]):
+    output_parts = [
+        add(output_own[k * rows_dev : (k + 1) * rows_dev], got[0][k * rows_dev : (k + 1) * rows_dev]) for k in range(ring)
+    ]
+    arrived(got[1:])
+    for (_, turn, _), g in zip(keys, got[1 + len(jobs) :]):
         out_terms[turn].append(g)
 
     def own_part(d, v, g):

time: 737 us -> 727 us (0.986)
    pallas_call x2 -> x0, Pallas kernels: 11.8 us -> none  [pick_pieces(): pl.pallas_call(kernel, grid_spec=pltpu.PrefetchScalarGridSpec(num_scalar_...]
    pallas_call x2 -> x5, Pallas kernels: 50.2 us -> 59.2 us  [in_vmem(): pl.pallas_call(kernel, in_specs=[pl.BlockSpec(memory_space=pltpu.SMEM)] +...]
    unnamed x287 -> x286, local copies, waits for them, and re-layouts: 24.8 us -> 20.4 us
    dot_general x6 -> x5, matrix products: 40.8 us -> 37.7 us  [dot(): return lax.dot_general(a, b, (dims, ((), ())), preferred_element_type=F32)]
  transfers between devices with their start and end apart: 97 -> 97, of which waited for: 30 -> 33; matrix products, arithmetic and copies ran while one was open for 19% -> 19% of each run, Pallas kernels for 38% -> 38%
where the time goes in v5:
time: 727 us; the launch traced here: 720 us
  Pallas kernels  276 us (38%)
  waiting for transfers between devices  184 us (25%)
  starting transfers between devices  104 us (14%)
  other arithmetic  58.3 us (8%)
  local copies, waits for them, and re-layouts  56.4 us (8%)
  matrix products  37.7 us (5%)
    ppermute x96, waiting for transfers between devices, send(): return lax.ppermute(values, BOTH, tables[way])  184 us
    pallas_call x4, Pallas kernels, ffn_tile(): pl.pallas_call(kernel, grid=(steps,), in_specs=in_specs, out_specs=out_sp...  155 us
    ppermute x96, starting transfers between devices, send(): return lax.ppermute(values, BOTH, tables[way])  100 us
    pallas_call x5, Pallas kernels, in_vmem(): pl.pallas_call(kernel, in_specs=[pl.BlockSpec(memory_space=pltpu.SMEM)] +...  59.2 us
    pallas_call x3, Pallas kernels, expert_grad(): pl.pallas_call(kernel, grid=(width // block,), in_specs=[pl.BlockSpec((ro...  42.7 us
    dot_general x5, matrix products, dot(): return lax.dot_general(a, b, (dims, ((), ())), preferred_element_type=F32)  37.7 us
    convert_element_type x30, other arithmetic, add(): return (a.astype(F32) + b.astype(F32)).astype(BF16)  22.3 us
    unnamed x286, local copies, waits for them, and re-layouts  20.4 us
  transfers between devices with their start and end apart: 97, of which 33 were waited for; matrix products, arithmetic and copies ran while one was open for 19% of the time, Pallas kernels for 38%

profile of v5, /device:TPU:1, one launch (start us, length us, event | category | flops | bytes accessed | tf_op | source)
XLA Modules:
  0.0 719.9 jit_solution(1100449789064520375)
XLA Ops:
  35.4 8.0 %shard_map.298 = (bf16[3,768,2048]{2,1,0:T(8,128)(2,1)}, bf16[3,1792,2048]{2,1,0:T(8,128)(2,1)}) custom-call(bf16[2,352,2048]{2,1,0:T(8,128)(2,1)S(1)} %bitcast.127, bf16[2,352,2048]{2,1,0:T(8,128)(2,1)S(1)} %bitcast.128, bf16[2,352,2048]{2,1,0:T(8,128)(2,1)S(1)} %copy-done.2), custom_call_target="tpu_custom_call" | custom-call | bytes 31457280 | tf_op jit(solution)/shard_map/pallas_call | solution.py:583
  43.4 13.2 %collective-permute-done.5 = bf16[256,256]{1,0:T(8,128)(2,1)S(1)} collective-permute-done((bf16[256,256]{1,0:T(8,128)(2,1)S(1)}, bf16[256,256]{1,0:T(8,128)(2,1)S(1)}, u32[]{:S(2)}, u32[]{:S(2)}) %collective-permute-start.5) | collective-permute-done | bytes 131104 | tf_op jit(solution)/shard_map/ppermute | solution.py:671
  71.6 15.7 %collective-permute-done.9.refs_16_ = bf16[256,1792]{1,0:T(8,128)(2,1)S(1)} collective-permute-done((bf16[256,1792]{1,0:T(8,128)(2,1)S(1)}, bf16[256,1792]{1,0:T(8,128)(2,1)S(1)}, u32[]{:S(2)}, u32[]{:S(2)}) %collective-permute-start.9) | collective-permute-done | bytes 917536 | tf_op jit(solution)/shard_map/ppermute | solution.py:671
  105.9 11.8 %collective-permute-done.13 = bf16[128,2176]{1,0:T(8,128)(2,1)S(1)} collective-permute-done((bf16[128,2176]{1,0:T(8,128)(2,1)S(1)}, bf16[128,2176]{1,0:T(8,128)(2,1)S(1)}, u32[]{:S(2)}, u32[]{:S(2)}) %collective-permute-start.13) | collective-permute-done | bytes 557088 | tf_op jit(solution)/shard_map/ppermute | solution.py:671
  122.4 15.2 %collective-permute-done.19 = bf16[128,2176]{1,0:T(8,128)(2,1)S(1)} collective-permute-done((bf16[128,2176]{1,0:T(8,128)(2,1)}, bf16[128,2176]{1,0:T(8,128)(2,1)S(1)}, u32[]{:S(2)}, u32[]{:S(2)}) %collective-permute-start.19) | collective-permute-done | bytes 557088 | tf_op jit(solution)/shard_map/ppermute | solution.py:671
  151.3 21.5 %shard_map.299 = (bf16[256,2048]{1,0:T(8,128)(2,1)}, bf16[256,2048]{1,0:T(8,128)(2,1)}, bf16[512,2048]{1,0:T(8,128)(2,1)}, bf16[512,768]{1,0:T(8,128)(2,1)}, bf1...) custom-call(s32[12]{0:T(128)} %stack.146.refs_0_.places_ref, ...), custom_call_target="tpu_custom_call" | custom-call | flops 6000000000 | bytes 25165824 | tf_op jit(solution)/shard_map/pallas_call | solution.py:290
  192.1 11.5 %shard_map.301.refs_6_.refs_7_.refs_8_ = bf16[3,1792,2048]{2,1,0:T(8,128)(2,1)} custom-call(bf16[3,768,2048]{2,1,0:T(8,128)(2,1)} %collective-permute-done.12.other_ref, bf16[3,256,2048]{2,1,0:T(8,128)(2,1)S(1)} %pad_maximum_fusion.shared_ref, bf16[3,1792,2048]{2,1,0:T(8,128)(2,1)} %get-tuple-element.243._), custom_call_target="tpu_custom_call", output_to_operand_aliasing={{}: (2, {})} | custom-call | bytes 23068672 | tf_op jit(solution)/shard_map/pallas_call | solution.py:608
  208.2 11.6 %collective-permute-done.29 = bf16[128,2048]{1,0:T(8,128)(2,1)S(1)} collective-permute-done((bf16[128,2048]{1,0:T(8,128)(2,1)S(1)}, bf16[128,2048]{1,0:T(8,128)(2,1)S(1)}, u32[]{:S(2)}, u32[]{:S(2)}) %collective-permute-start.29) | collective-permute-done | bytes 524320 | tf_op jit(solution)/shard_map/ppermute | solution.py:671
  238.2 10.5 %collective-permute-done.35 = bf16[128,2048]{1,0:T(8,128)(2,1)S(1)} collective-permute-done((bf16[128,2048]{1,0:T(8,128)(2,1)S(1)}, bf16[128,2048]{1,0:T(8,128)(2,1)S(1)}, u32[]{:S(2)}, u32[]{:S(2)}) %collective-permute-start.35) | collective-permute-done | bytes 524320 | tf_op jit(solution)/shard_map/ppermute | solution.py:671
  260.3 39.0 %shard_map.302 = (bf16[256,2176]{1,0:T(8,128)(2,1)}, bf16[256,2176]{1,0:T(8,128)(2,1)}, bf16[256,2048]{1,0:T(8,128)(2,1)}, bf16[256,2048]{1,0:T(8,128)(2,1)}, bf...) custom-call(s32[1]{0:T(128)} %bitcast.39.refs_0_, ...), custom_call_target="tpu_custom_call" | custom-call | flops 22548578304 | bytes 30408704 | tf_op jit(solution)/shard_map/pallas_call | solution.py:474
  302.8 38.5 %shard_map.303 = (bf16[256,2176]{1,0:T(8,128)(2,1)}, bf16[256,2176]{1,0:T(8,128)(2,1)}, bf16[256,2048]{1,0:T(8,128)(2,1)}, bf16[256,2048]{1,0:T(8,128)(2,1)}, bf...) custom-call(s32[1]{0:T(128)} %bitcast.39.refs_0_, ...), custom_call_target="tpu_custom_call", output_to_operand_aliasing={{4}: (9, {}), {5}: (10, {}), {6}: (11, {}), {7}: (12, {}), ... | custom-call | flops 22548578304 | bytes 30408704 | tf_op jit(solution)/shard_map/pallas_call | solution.py:474
  346.5 38.5 %shard_map.304 = (bf16[256,2176]{1,0:T(8,128)(2,1)}, bf16[256,2176]{1,0:T(8,128)(2,1)}, bf16[256,2048]{1,0:T(8,128)(2,1)}, bf16[256,2048]{1,0:T(8,128)(2,1)}, bf...) custom-call(s32[1]{0:T(128)} %bitcast.39.refs_0_, ...), custom_call_target="tpu_custom_call", output_to_operand_aliasing={{4}: (9, {}), {5}: (10, {}), {6}: (11, {}), {7}: (12, {}), ... | custom-call | flops 22548578304 | bytes 30408704 | tf_op jit(solution)/shard_map/pallas_call | solution.py:474
  393.1 38.7 %shard_map.305 = (bf16[256,2176]{1,0:T(8,128)(2,1)}, bf16[256,2176]{1,0:T(8,128)(2,1)}, bf16[256,2048]{1,0:T(8,128)(2,1)}, bf16[256,2048]{1,0:T(8,128)(2,1)}, bf...) custom-call(s32[1]{0:T(128)} %bitcast.39.refs_0_, ...), custom_call_target="tpu_custom_call", output_to_operand_aliasing={{4}: (9, {}), {5}: (10, {}), {6}: (11, {}), {7}: (12, {}), ... | custom-call | flops 22548578304 | bytes 30408704 | tf_op jit(solution)/shard_map/pallas_call | solution.py:474
  436.9 12.5 %fusion.6 = bf16[1024,2048]{1,0:T(8,128)(2,1)} fusion(bf16[2048,2048]{1,0:T(8,128)(2,1)S(1)} %bitcast.131, bf16[2048,1792]{1,0:T(8,128)(2,1)} %bitcast.141), kind=kOutput, calls=%fused_computation.6 | convolution fusion | flops 8592031744 | bytes 16777216 | tf_op jit(solution)/shard_map/dot_general | solution.py:52
  452.8 11.0 %collective-permute-start.61 = (bf16[1024,2048]{1,0:T(8,128)(2,1)}, bf16[1024,2048]{1,0:T(8,128)(2,1)S(1)}, u32[]{:S(2)}, u32[]{:S(2)}) collective-permute-start(bf16[1024,2048]{1,0:T(8,128)(2,1)} %fusion.6), channel_id=1, source_target_pairs={{0,1},{1,0},{2,3},{3,2},{4,5},{5,4},{6,7},{7,6},{8,9},{9,8},{10,11... | collective-permute-start | bytes 12582920 | tf_op jit(solution)/shard_map/ppermute | solution.py:671
  465.0 12.7 %fusion.9 = bf16[1024,2048]{1,0:T(8,128)(2,1)} fusion(bf16[2048,2048]{1,0:T(8,128)(2,1)S(1)} %bitcast.132, bf16[2048,1792]{1,0:T(8,128)(2,1)} %bitcast.143), kind=kOutput, calls=%fused_computation.7 | convolution fusion | flops 8592031744 | bytes 16777216 | tf_op jit(solution)/shard_map/dot_general | solution.py:52
  497.4 10.9 %fusion.12 = bf16[1024,2048]{1,0:T(8,128)(2,1)} fusion(bf16[2048,2048]{1,0:T(8,128)(2,1)S(1)} %bitcast.136, bf16[2048,1792]{1,0:T(8,128)(2,1)S(1)} %bitcast.140), kind=kOutput, calls=%fused_computation.8 | convolution fusion | flops 8592031744 | bytes 16777216 | tf_op jit(solution)/shard_map/dot_general | solution.py:52
  531.2 8.6 %collective-permute-done.67 = bf16[128,2048]{1,0:T(8,128)(2,1)S(1)} collective-permute-done((bf16[128,2048]{1,0:T(8,128)(2,1)S(1)}, bf16[128,2048]{1,0:T(8,128)(2,1)S(1)}, u32[]{:S(2)}, u32[]{:S(2)}) %collective-permute-start.67) | collective-permute-done | bytes 524320 | tf_op jit(solution)/shard_map/ppermute | solution.py:671
  564.6 28.7 %shard_map.307 = (bf16[256,1024]{1,0:T(8,128)(2,1)}, bf16[256,1024]{1,0:T(8,128)(2,1)}, bf16[256,1024]{1,0:T(8,128)(2,1)}, bf16[256,1024]{1,0:T(8,128)(2,1)}, bf...) custom-call(s32[12]{0:T(128)} %stack.146.refs_0_.places_ref, ...), custom_call_target="tpu_custom_call" | custom-call | flops 12000000000 | bytes 25165824 | tf_op jit(solution)/shard_map/pallas_call | solution.py:290
  602.8 14.3 %shard_map.308 = f32[2,352,2048]{2,1,0:T(8,128)} custom-call(bf16[2048,1792]{1,0:T(8,128)(2,1)} %bitcast.142, bf16[2048,2048]{1,0:T(8,128)(2,1)} %bitcast.129, bf16[1024,2048]{1,0:T(8,128)(2,1)} %copy-done.8), custom_call_target="tpu_custom_call" | custom-call | flops 6442450944 | bytes 20971520 | tf_op jit(solution)/shard_map/pallas_call | solution.py:554
  629.0 14.2 %shard_map.309 = f32[2,352,2048]{2,1,0:T(8,128)} custom-call(bf16[2048,1792]{1,0:T(8,128)(2,1)} %bitcast.144, bf16[2048,2048]{1,0:T(8,128)(2,1)} %bitcast.130, bf16[1024,2048]{1,0:T(8,128)(2,1)} %collective-permute-done.66.got_ref), custom_call_target="tpu_custom_call" | custom-call | flops 6442450944 | bytes 20971520 | tf_op jit(solution)/shard_map/pallas_call | solution.py:554
  655.4 14.2 %shard_map.310 = f32[2,352,2048]{2,1,0:T(8,128)} custom-call(bf16[2048,1792]{1,0:T(8,128)(2,1)} %bitcast.137, bf16[2048,2048]{1,0:T(8,128)(2,1)} %bitcast.133, bf16[1024,2048]{1,0:T(8,128)(2,1)} %collective-permute-done.68.got_ref), custom_call_target="tpu_custom_call" | custom-call | flops 6442450944 | bytes 20971520 | tf_op jit(solution)/shard_map/pallas_call | solution.py:554
  679.1 15.5 %collective-permute-done.89 = bf16[256,256]{1,0:T(8,128)(2,1)S(1)} collective-permute-done((bf16[256,256]{1,0:T(8,128)(2,1)S(1)}, bf16[256,256]{1,0:T(8,128)(2,1)S(1)}, u32[]{:S(2)}, u32[]{:S(2)}) %collective-permute-start.89) | collective-permute-done | bytes 131104 | tf_op jit(solution)/shard_map/ppermute | solution.py:671
  694.6 10.1 %collective-permute-done.90 = bf16[256,256]{1,0:T(8,128)(2,1)S(1)} collective-permute-done((bf16[256,256]{1,0:T(8,128)(2,1)S(1)}, bf16[256,256]{1,0:T(8,128)(2,1)S(1)}, u32[]{:S(2)}, u32[]{:S(2)}) %collective-permute-start.90) | collective-permute-done | bytes 131104 | tf_op jit(solution)/shard_map/ppermute | solution.py:671
  (662 shorter events, 290.1 us)
Async XLA Ops:
  139.3 41.8 %collective-permute-start.23 = (bf16[256,2176]{1,0:T(8,128)(2,1)}, bf16[256,2176]{1,0:T(8,128)(2,1)}, u32[]{:S(2)}, u32[]{:S(2)}) collective-permute-start(bf16[256,2176]{1,0:T(8,128)(2,1)} %pad_maximum_fusion.2.refs_3_), channel_id=1, source_target_pairs={{0,2},{1,3},{2,0},{3,1},{4,6},{5,7},{6,4},{7,5},{8,10},{9,11},{10,... | collective-permute-start | bytes 3342344 | tf_op jit(solution)/shard_map/ppermute | solution.py:671
  140.5 40.6 %collective-permute-start.24 = (bf16[256,2176]{1,0:T(8,128)(2,1)S(1)}, bf16[256,2176]{1,0:T(8,128)(2,1)}, u32[]{:S(2)}, u32[]{:S(2)}) collective-permute-start(bf16[256,2176]{1,0:T(8,128)(2,1)S(1)} %pad_maximum_fusion.3.refs_3_), channel_id=1, source_target_pairs={{0,4},{1,5},{2,6},{3,7},{4,0},{5,1},{6,2},{7,3},{8,12},{9,13},{10,... | collective-permute-start | bytes 3342344 | tf_op jit(solution)/shard_map/ppermute | solution.py:671
  257.4 41.9 %collective-permute-start.39 = (bf16[128,2048]{1,0:T(8,128)(2,1)S(1)}, bf16[128,2048]{1,0:T(8,128)(2,1)S(1)}, u32[]{:S(2)}, u32[]{:S(2)}) collective-permute-start(bf16[128,2048]{1,0:T(8,128)(2,1)S(1)} %bitcast.160), channel_id=1, source_target_pairs={{0,2},{1,3},{2,0},{3,1},{4,6},{5,7},{6,4},{7,5},{8,10},{9,11},{10,... | collective-permute-start | bytes 1572872 | tf_op jit(solution)/shard_map/ppermute | solution.py:671
  258.0 41.5 %collective-permute-start.38 = (bf16[128,2048]{1,0:T(8,128)(2,1)S(1)}, bf16[128,2048]{1,0:T(8,128)(2,1)S(1)}, u32[]{:S(2)}, u32[]{:S(2)}) collective-permute-start(bf16[128,2048]{1,0:T(8,128)(2,1)S(1)} %bitcast.158), channel_id=1, source_target_pairs={{0,4},{1,5},{2,6},{3,7},{4,0},{5,1},{6,2},{7,3},{8,12},{9,13},{10,... | collective-permute-start | bytes 1572872 | tf_op jit(solution)/shard_map/ppermute | solution.py:671
  258.2 41.4 %collective-permute-start.40 = (bf16[256,2176]{1,0:T(8,128)(2,1)S(1)}, bf16[256,2176]{1,0:T(8,128)(2,1)S(1)}, u32[]{:S(2)}, u32[]{:S(2)}) collective-permute-start(bf16[256,2176]{1,0:T(8,128)(2,1)S(1)} %pad_maximum_fusion.4.refs_3_), channel_id=1, source_target_pairs={{0,2},{1,3},{2,0},{3,1},{4,6},{5,7},{6,4},{7,5},{8,10},{9,11},{10,... | collective-permute-start | bytes 3342344 | tf_op jit(solution)/shard_map/ppermute | solution.py:671
  259.1 40.5 %collective-permute-start.41 = (bf16[256,2176]{1,0:T(8,128)(2,1)S(1)}, bf16[256,2176]{1,0:T(8,128)(2,1)S(1)}, u32[]{:S(2)}, u32[]{:S(2)}) collective-permute-start(bf16[256,2176]{1,0:T(8,128)(2,1)S(1)} %pad_maximum_fusion.5.refs_3_), channel_id=1, source_target_pairs={{0,4},{1,5},{2,6},{3,7},{4,0},{5,1},{6,2},{7,3},{8,12},{9,13},{10,... | collective-permute-start | bytes 3342344 | tf_op jit(solution)/shard_map/ppermute | solution.py:671
  299.6 41.7 %collective-permute-start.42 = (bf16[256,2048]{1,0:T(8,128)(2,1)}, bf16[256,2048]{1,0:T(8,128)(2,1)}, u32[]{:S(2)}, u32[]{:S(2)}) collective-permute-start(bf16[256,2048]{1,0:T(8,128)(2,1)} %get-tuple-element.268), channel_id=1, source_target_pairs={{0,24},{1,25},{2,26},{3,27},{4,28},{5,29},{6,30},{7,31},{8,0},{9,1... | collective-permute-start | bytes 3145736 | tf_op jit(solution)/shard_map/ppermute | solution.py:671
  299.7 43.5 %collective-permute-start.43 = (bf16[256,2176]{1,0:T(8,128)(2,1)}, bf16[256,2176]{1,0:T(8,128)(2,1)}, u32[]{:S(2)}, u32[]{:S(2)}) collective-permute-start(bf16[256,2176]{1,0:T(8,128)(2,1)} %get-tuple-element.272), channel_id=1, source_target_pairs={{0,24},{1,25},{2,26},{3,27},{4,28},{5,29},{6,30},{7,31},{8,0},{9,1... | collective-permute-start | bytes 3342344 | tf_op jit(solution)/shard_map/ppermute | solution.py:671
  300.7 44.1 %collective-permute-start.44 = (bf16[256,2048]{1,0:T(8,128)(2,1)S(1)}, bf16[256,2048]{1,0:T(8,128)(2,1)}, u32[]{:S(2)}, u32[]{:S(2)}) collective-permute-start(bf16[256,2048]{1,0:T(8,128)(2,1)S(1)} %pad_maximum_fusion.10.refs_1_), channel_id=1, source_target_pairs={{0,2},{1,3},{2,0},{3,1},{4,6},{5,7},{6,4},{7,5},{8,10},{9,11},{10,... | collective-permute-start | bytes 3145736 | tf_op jit(solution)/shard_map/ppermute | solution.py:671
  301.3 43.6 %collective-permute-start.45 = (bf16[256,2048]{1,0:T(8,128)(2,1)S(1)}, bf16[256,2048]{1,0:T(8,128)(2,1)S(1)}, u32[]{:S(2)}, u32[]{:S(2)}) collective-permute-start(bf16[256,2048]{1,0:T(8,128)(2,1)S(1)} %pad_maximum_fusion.11.refs_1_), channel_id=1, source_target_pairs={{0,4},{1,5},{2,6},{3,7},{4,0},{5,1},{6,2},{7,3},{8,12},{9,13},{10,... | collective-permute-start | bytes 3145736 | tf_op jit(solution)/shard_map/ppermute | solution.py:671
  344.9 40.2 %collective-permute-start.46 = (bf16[128,2048]{1,0:T(8,128)(2,1)S(1)}, bf16[128,2048]{1,0:T(8,128)(2,1)S(1)}, u32[]{:S(2)}, u32[]{:S(2)}) collective-permute-start(bf16[128,2048]{1,0:T(8,128)(2,1)S(1)} %slice.558), channel_id=1, source_target_pairs={{0,2},{1,3},{2,0},{3,1},{4,6},{5,7},{6,4},{7,5},{8,10},{9,11},{10,... | collective-permute-start | bytes 1572872 | tf_op jit(solution)/shard_map/ppermute | solution.py:671
  345.8 40.2 %collective-permute-start.48 = (bf16[128,2176]{1,0:T(8,128)(2,1)S(1)}, bf16[128,2176]{1,0:T(8,128)(2,1)S(1)}, u32[]{:S(2)}, u32[]{:S(2)}) collective-permute-start(bf16[128,2176]{1,0:T(8,128)(2,1)S(1)} %slice.557), channel_id=1, source_target_pairs={{0,2},{1,3},{2,0},{3,1},{4,6},{5,7},{6,4},{7,5},{8,10},{9,11},{10,... | collective-permute-start | bytes 1671176 | tf_op jit(solution)/shard_map/ppermute | solution.py:671
  346.4 40.5 %collective-permute-start.47 = (bf16[256,2176]{1,0:T(8,128)(2,1)S(1)}, bf16[256,2176]{1,0:T(8,128)(2,1)S(1)}, u32[]{:S(2)}, u32[]{:S(2)}) collective-permute-start(bf16[256,2176]{1,0:T(8,128)(2,1)S(1)} %copy-done.120), channel_id=1, source_target_pairs={{0,24},{1,25},{2,26},{3,27},{4,28},{5,29},{6,30},{7,31},{8,0},{9,1... | collective-permute-start | bytes 3342344 | tf_op jit(solution)/shard_map/ppermute | solution.py:671
  387.3 45.5 %collective-permute-start.52 = (bf16[256,2048]{1,0:T(8,128)(2,1)}, bf16[256,2048]{1,0:T(8,128)(2,1)S(1)}, u32[]{:S(2)}, u32[]{:S(2)}) collective-permute-start(bf16[256,2048]{1,0:T(8,128)(2,1)} %get-tuple-element.304), channel_id=1, source_target_pairs={{0,24},{1,25},{2,26},{3,27},{4,28},{5,29},{6,30},{7,31},{8,0},{9,1... | collective-permute-start | bytes 3145736 | tf_op jit(solution)/shard_map/ppermute | solution.py:671
  389.5 44.3 %collective-permute-start.51 = (bf16[256,2176]{1,0:T(8,128)(2,1)}, bf16[256,2176]{1,0:T(8,128)(2,1)S(1)}, u32[]{:S(2)}, u32[]{:S(2)}) collective-permute-start(bf16[256,2176]{1,0:T(8,128)(2,1)} %get-tuple-element.303), channel_id=1, source_target_pairs={{0,2},{1,3},{2,0},{3,1},{4,6},{5,7},{6,4},{7,5},{8,10},{9,11},{10,... | collective-permute-start | bytes 3342344 | tf_op jit(solution)/shard_map/ppermute | solution.py:671
  390.4 41.4 %collective-permute-start.53 = (bf16[128,2176]{1,0:T(8,128)(2,1)S(1)}, bf16[128,2176]{1,0:T(8,128)(2,1)S(1)}, u32[]{:S(2)}, u32[]{:S(2)}) collective-permute-start(bf16[128,2176]{1,0:T(8,128)(2,1)S(1)} %slice.560), channel_id=1, source_target_pairs={{0,4},{1,5},{2,6},{3,7},{4,0},{5,1},{6,2},{7,3},{8,12},{9,13},{10,... | collective-permute-start | bytes 1671176 | tf_op jit(solution)/shard_map/ppermute | solution.py:671
  391.6 42.5 %collective-permute-start.50 = (bf16[64,2176]{1,0:T(8,128)(2,1)S(1)}, bf16[64,2176]{1,0:T(8,128)(2,1)S(1)}, u32[]{:S(2)}, u32[]{:S(2)}) collective-permute-start(bf16[64,2176]{1,0:T(8,128)(2,1)S(1)} %slice.562), channel_id=1, source_target_pairs={{0,4},{1,5},{2,6},{3,7},{4,0},{5,1},{6,2},{7,3},{8,12},{9,13},{10,... | collective-permute-start | bytes 835592 | tf_op jit(solution)/shard_map/ppermute | solution.py:671
  391.8 42.3 %collective-permute-start.49 = (bf16[64,2048]{1,0:T(8,128)(2,1)S(1)}, bf16[64,2048]{1,0:T(8,128)(2,1)S(1)}, u32[]{:S(2)}, u32[]{:S(2)}) collective-permute-start(bf16[64,2048]{1,0:T(8,128)(2,1)S(1)} %slice.563), channel_id=1, source_target_pairs={{0,4},{1,5},{2,6},{3,7},{4,0},{5,1},{6,2},{7,3},{8,12},{9,13},{10,... | collective-permute-start | bytes 786440 | tf_op jit(solution)/shard_map/ppermute | solution.py:671
  452.8 39.0 %collective-permute-start.61 = (bf16[1024,2048]{1,0:T(8,128)(2,1)}, bf16[1024,2048]{1,0:T(8,128)(2,1)S(1)}, u32[]{:S(2)}, u32[]{:S(2)}) collective-permute-start(bf16[1024,2048]{1,0:T(8,128)(2,1)} %fusion.6), channel_id=1, source_target_pairs={{0,1},{1,0},{2,3},{3,2},{4,5},{5,4},{6,7},{7,6},{8,9},{9,8},{10,11... | collective-permute-start | bytes 12582920 | tf_op jit(solution)/shard_map/ppermute | solution.py:671
  547.3 49.9 %all-to-all-start = ((bf16[8,264,256]{2,1,0:T(8,128)(2,1)}), bf16[8,264,256]{2,1,0:T(8,128)(2,1)S(1)}, u32[]{:S(2)}, u32[]{:S(2)}) async-start(bf16[8,264,256]{2,1,0:T(8,128)(2,1)} %maximum_bitcast_fusion), calls=%async_computation | async-start | bytes 2162688 | tf_op jit(solution)/shard_map/all_to_all | solution.py:1042
  558.0 37.3 %collective-permute-start.74 = (bf16[128,2048]{1,0:T(8,128)(2,1)}, bf16[128,2048]{1,0:T(8,128)(2,1)S(1)}, u32[]{:S(2)}, u32[]{:S(2)}) collective-permute-start(bf16[128,2048]{1,0:T(8,128)(2,1)} %slice.583), channel_id=1, source_target_pairs={{0,2},{1,3},{2,0},{3,1},{4,6},{5,7},{6,4},{7,5},{8,10},{9,11},{10,... | collective-permute-start | bytes 1572872 | tf_op jit(solution)/shard_map/ppermute | solution.py:671
  558.7 40.0 %collective-permute-start.75 = (bf16[1024,512]{1,0:T(8,128)(2,1)}, bf16[1024,512]{1,0:T(8,128)(2,1)}, u32[]{:S(2)}, u32[]{:S(2)}) collective-permute-start(bf16[1024,512]{1,0:T(8,128)(2,1)} %get-tuple-element.342), channel_id=1, source_target_pairs={{0,4},{1,5},{2,6},{3,7},{4,0},{5,1},{6,2},{7,3},{8,12},{9,13},{10,... | collective-permute-start | bytes 3145736 | tf_op jit(solution)/shard_map/ppermute | solution.py:671
  672.2 35.9 %collective-permute-start.93 = (bf16[256,512]{1,0:T(8,128)(2,1)S(1)}, bf16[256,512]{1,0:T(8,128)(2,1)S(1)}, u32[]{:S(2)}, u32[]{:S(2)}) collective-permute-start(bf16[256,512]{1,0:T(8,128)(2,1)S(1)} %add_convert_fusion.35), channel_id=1, source_target_pairs={{0,8},{1,9},{2,10},{3,11},{4,12},{5,13},{6,14},{7,15},{8,16},{9,17... | collective-permute-start | bytes 786440 | tf_op jit(solution)/shard_map/ppermute | solution.py:671
  672.5 37.6 %collective-permute-start.92 = (bf16[256,1024]{1,0:T(8,128)(2,1)}, bf16[256,1024]{1,0:T(8,128)(2,1)S(1)}, u32[]{:S(2)}, u32[]{:S(2)}) collective-permute-start(bf16[256,1024]{1,0:T(8,128)(2,1)} %add_convert_fusion.18), channel_id=1, source_target_pairs={{0,8},{1,9},{2,10},{3,11},{4,12},{5,13},{6,14},{7,15},{8,16},{9,17... | collective-permute-start | bytes 1572872 | tf_op jit(solution)/shard_map/ppermute | solution.py:671
  (207 other events, 2996.8 us)

commit v6 on v5

--- a/solution.py
+++ b/solution.py
@@ -364,7 +364,7 @@
 def ffn_kernel(
     local, segs_side, steps, width, dx_mode, out_mode,
     first_ref, x0, x1, g0, g1, router, wg, wu, wd,
-    dx_keep, dx_send, out_keep, out_send, x_all, g_all, hs_all, dg_all, du_all,
+    dx_keep, dx_send, out_keep, out_send, hs_all, dg_all, du_all,
     acc_out, acc_dx, gates_s, dgates_s,
 ):
     j = pl.program_id(0)
@@ -386,8 +386,6 @@
         dgates_s[...] = jnp.zeros_like(dgates_s)
         acc_out[...] = jnp.zeros_like(acc_out)
         acc_dx[...] = jnp.zeros_like(acc_dx)
-        x_all[0] = x
-        g_all[0] = g_in
 
     gates = gates_s[...]
     wanted, columns = [], []
@@ -457,16 +455,14 @@
         in_specs += [pl.BlockSpec(memory_space=pl.ANY)] * len(kept)
         args += list(kept)
         aliases = {plain + i: 4 + i for i in range(len(kept))}
-    tile_rows = pl.BlockSpec((1, 2 * half, width), lambda j: (call, 0, 0))
     tile_hidden = pl.BlockSpec((1, 2 * half, block), lambda j: (call, 0, j))
     shape = jax.ShapeDtypeStruct
     out_shape = (
         [shape((half, width + LANES), BF16)] * 2
         + [shape((half, width), BF16)] * 2
-        + [shape((calls, 2 * half, width), BF16)] * 2
         + [shape((calls, 2 * half, hid), BF16)] * 3
     )
-    out_specs = [whole(half, width + LANES)] * 2 + [whole(half, width)] * 2 + [tile_rows] * 2 + [tile_hidden] * 3
+    out_specs = [whole(half, width + LANES)] * 2 + [whole(half, width)] * 2 + [tile_hidden] * 3
 
     def kernel(*refs):
         ffn_kernel(local, segs_side, steps, width, dx_mode, out_mode, *refs[:plain], *refs[len(args) :])
@@ -537,34 +533,55 @@
     return in_vmem(kernel, outs, scratch, 2 * 10**9, [places, d_attn, mixed])
 
 
-def expert_grad(d, v, got, local, ff, seg):
-    rows, width = v.shape
-    side = local * seg
+def weight_grad(d, first, cols, tiles, emit, out, got=None):
+    rows, width = d.shape[0], out.shape[-1]
     block = 2 * LANES
-
-    def kernel(d_ref, v_ref, got_ref, out, turned):
+    pieces, n = cols // block, len(tiles)
+    more = [] if got is None else [got]
+
+    def kernel(*refs):
+        turned = refs[-1]
+
         @pl.when(pl.program_id(0) == 0)
         def _():
-            turned[...] = d_ref[...].T
-
-        total = mm(turned[...], v_ref[...]) + got_ref[...].astype(F32)
-        for j in range(local):
-            out[j] = total[j * seg : j * seg + ff]
+            for c in range(pieces):
+                turned[c * block : (c + 1) * block] = refs[c][...].T
+
+        total = mm(turned[...], jnp.concatenate([ref[...] for ref in refs[pieces : pieces + n]], axis=0))
+        emit(refs[-2], total, refs[pieces + n] if more else None)
 
     return pl.pallas_call(
         kernel,
         grid=(width // block,),
         in_specs=[
-            pl.BlockSpec((rows, side), lambda i: (0, 0), pipeline_mode=pl.Buffered(1)),
-            pl.BlockSpec((rows, block), lambda i: (0, i)),
-            pl.BlockSpec((side, block), lambda i: (0, i)),
-        ],
-        out_specs=pl.BlockSpec((local, ff, block), lambda i: (0, 0, i)),
-        out_shape=jax.ShapeDtypeStruct((local, ff, width), F32),
-        scratch_shapes=[pltpu.VMEM((side, rows), BF16)],
+            pl.BlockSpec((rows, block), lambda i, c=c: (0, first // block + c), pipeline_mode=pl.Buffered(1))
+            for c in range(pieces)
+        ]
+        + [pl.BlockSpec((v.shape[0], block), lambda i: (0, i)) for v in tiles]
+        + [pl.BlockSpec((cols, block), lambda i: (0, i)) for _ in more],
+        out_specs=pl.BlockSpec((*out.shape[:-1], block), lambda i: (0,) * (len(out.shape) - 1) + (i,)),
+        out_shape=out,
+        scratch_shapes=[pltpu.VMEM((cols, rows), BF16)],
         compiler_params=pltpu.CompilerParams(vmem_limit_bytes=56 * 2**20, dimension_semantics=("arbitrary",)),
-        cost_estimate=pl.CostEstimate(flops=2 * rows * width * side, bytes_accessed=20 * 2**20, transcendentals=0),
-    )(d, v, got)
+        cost_estimate=pl.CostEstimate(flops=2 * rows * width * cols, bytes_accessed=20 * 2**20, transcendentals=0),
+    )(*[d] * pieces, *tiles, *more)
+
+
+def expert_grad(d, tiles, got, local, ff, seg, width):
+    def emit(ref, total, got_ref):
+        total = total + got_ref[...].astype(F32)
+        for j in range(local):
+            ref[j] = total[j * seg : j * seg + ff]
+
+    return weight_grad(d, 0, local * seg, tiles, emit, jax.ShapeDtypeStruct((local, ff, width), F32), got)
+
+
+def pair_grad(d, tiles, side, width):
+    def emit(ref, total, _):
+        ref[...] = total.astype(BF16)
+
+    cols = d.shape[1] - side
+    return weight_grad(d, side, cols, tiles, emit, jax.ShapeDtypeStruct((cols, width), BF16))
 
 
 def pack_experts(parts, seg, room):
@@ -966,10 +983,12 @@
             total = total + term.astype(F32)
         return total
 
-    def weight_part(d, v):
-        return t_mm(d.reshape(-1, d.shape[-1])[:, side:], v.reshape(-1, v.shape[-1])).astype(BF16)
-
-    x_all, g_all, hs_all, dg_all, du_all = kept
+    def weight_part(d, *tiles):
+        return pair_grad(d.reshape(-1, d.shape[-1]), tiles, side, width)
+
+    hs_all, dg_all, du_all = kept
+    x_all = [v for i in range(len(zones)) for pair in row_tiles[i] for v in pair]
+    g_all = [v for i in range(len(zones)) for pair in grad_tiles[i] for v in pair]
     dx_terms, out_terms = {0: [], 1: []}, {0: [], 1: []}
 
     def homeward(home, keys):
@@ -980,7 +999,7 @@
     jobs += [("out", 1, 2)] if 1 not in out_near or out_near[1].shape[0] == 4 * own_rows // 2 else []
     moved, arrived = moves(jobs)
     keys = [(i, turn, k) for i in late for turn in range(2) for k in zones[i]]
-    got, part = step(moved + homeward(dx_home, keys), weight_part, dg_all, x_all)
+    got, part = step(moved + homeward(dx_home, keys), weight_part, dg_all, *x_all)
     arrived(got)
     for (_, turn, _), g in zip(keys, got[len(jobs) :]):
         dx_terms[turn].append(g)
@@ -990,7 +1009,7 @@
     moved, arrived = moves(jobs)
     keys = [(len(zones) - 1, 0, k) for k in zones[-1]]
     got, part = step(
-        moved + homeward(dx_home, keys) + [(for_pair[0], "pair")], weight_part, du_all, x_all
+        moved + homeward(dx_home, keys) + [(for_pair[0], "pair")], weight_part, du_all, *x_all
     )
     arrived(got)
     dx_terms[0] += got[len(jobs) : -1]
@@ -1001,7 +1020,7 @@
     moved, arrived = moves(jobs)
     keys = [(len(zones) - 1, 1, k) for k in zones[-1]]
     got, part = step(
-        moved + homeward(dx_home, keys) + [(for_pair[1], "pair")], weight_part, hs_all, g_all
+        moved + homeward(dx_home, keys) + [(for_pair[1], "pair")], weight_part, hs_all, *g_all
     )
     arrived(got)
     dx_terms[1] += got[len(jobs) : -1]
@@ -1052,8 +1071,8 @@
     for (_, turn, _), g in zip(keys, got[1 + len(jobs) :]):
         out_terms[turn].append(g)
 
-    def own_part(d, v, g):
-        return expert_grad(d.reshape(-1, d.shape[-1]), v.reshape(-1, v.shape[-1]), g, local, ff, seg)
+    def own_part(d, g, *tiles):
+        return expert_grad(d.reshape(-1, d.shape[-1]), tiles, g, local, ff, seg, width)
 
     order = [*range(1, ring), 0]
 
@@ -1063,7 +1082,7 @@
     keys = [(len(zones) - 1, 1, k) for k in zones[-1]]
     got, grad_gate = step(
         [(g_others[0], "y"), (near_send, "pair"), (d_in_send, "pair"), *homeward(out_home, keys)],
-        own_part, dg_all, x_all, from_pair[0],
+        own_part, dg_all, from_pair[0], *x_all,
     )
     main_parts = two_parts(0, got[0])
     near = add(near_keep, got[1])
@@ -1076,7 +1095,7 @@
 
     got, grad_up = step(
         [(g_others[1], "y"), (few_away, "x"), (main_parts[0], "ring"), (output_parts[order[0]], "ring")],
-        own_part, du_all, x_all, from_pair[1],
+        own_part, du_all, from_pair[1], *x_all,
     )
     main_parts += two_parts(1, got[0])
     few_sum = add(few_keep, got[1])
@@ -1087,7 +1106,7 @@
     few_half = few_sum.shape[0] // 2
     got, grad_down = step(
         [(few_sum[few_half:], "y"), (d_away, "x"), (total, "ring"), (total_out, "ring")],
-        own_part, hs_all, g_all, from_pair[2],
+        own_part, hs_all, from_pair[2], *g_all,
     )
     few_sum = add(few_sum[:few_half], got[0])
     few_planes = [few_sum[k * rows_dev : (k + 1) * rows_dev] for k in range(ring)]

time: 727 us -> 731 us (level)
  Pallas kernels: 276 us -> 313 us
  matrix products: 37.7 us -> 1.59 us
  waiting for transfers between devices: 184 us -> 166 us
  starting transfers between devices: 104 us -> 115 us
    pallas_call x3 -> x6, Pallas kernels: 42.7 us -> 90.3 us  [weight_grad(): pl.pallas_call(kernel, grid=(width // block,), in_specs=[pl.BlockSpec((ro...]
    dot_general x5 -> x2, matrix products: 37.7 us -> 1.59 us  [dot(): return lax.dot_general(a, b, (dims, ((), ())), preferred_element_type=F32)]
    ppermute x96, waiting for transfers between devices: 184 us -> 166 us  [send(): return lax.ppermute(values, BOTH, tables[way])]
    pallas_call x4, Pallas kernels: 155 us -> 143 us  [ffn_tile(): pl.pallas_call(kernel, grid=(steps,), in_specs=in_specs, out_specs=out_sp...]
    ppermute x96, starting transfers between devices: 100 us -> 111 us  [send(): return lax.ppermute(values, BOTH, tables[way])]
    unnamed x286 -> x266, local copies, waits for them, and re-layouts: 20.4 us -> 21.4 us
  transfers between devices with their start and end apart: 97 -> 97, of which waited for: 33 -> 33; matrix products, arithmetic and copies ran while one was open for 19% -> 14% of each run, Pallas kernels for 38% -> 43%
where the time goes in v6:
time: 731 us; the launch traced here: 724 us
  Pallas kernels  313 us (43%)
  waiting for transfers between devices  166 us (23%)
  starting transfers between devices  115 us (16%)
  local copies, waits for them, and re-layouts  62.8 us (9%)
  other arithmetic  62 us (8%)
    ppermute x96, waiting for transfers between devices, send(): return lax.ppermute(values, BOTH, tables[way])  166 us
    pallas_call x4, Pallas kernels, ffn_tile(): pl.pallas_call(kernel, grid=(steps,), in_specs=in_specs, out_specs=out_sp...  143 us
    ppermute x96, starting transfers between devices, send(): return lax.ppermute(values, BOTH, tables[way])  111 us
    pallas_call x6, Pallas kernels, weight_grad(): pl.pallas_call(kernel, grid=(width // block,), in_specs=[pl.BlockSpec((ro...  90.3 us
    pallas_call x5, Pallas kernels, in_vmem(): pl.pallas_call(kernel, in_specs=[pl.BlockSpec(memory_space=pltpu.SMEM)] +...  59.5 us
    convert_element_type x30, other arithmetic, add(): return (a.astype(F32) + b.astype(F32)).astype(BF16)  24.5 us
    unnamed x266, local copies, waits for them, and re-layouts  21.4 us
  transfers between devices with their start and end apart: 97, of which 33 were waited for; matrix products, arithmetic and copies ran while one was open for 14% of the time, Pallas kernels for 43%

profile of v6, /device:TPU:1, one launch (start us, length us, event | category | flops | bytes accessed | tf_op | source)
XLA Modules:
  0.0 723.5 jit_solution(921836491543167699)
XLA Ops:
  34.4 8.1 %shard_map.298 = (bf16[3,768,2048]{2,1,0:T(8,128)(2,1)}, bf16[3,1792,2048]{2,1,0:T(8,128)(2,1)}) custom-call(bf16[2,352,2048]{2,1,0:T(8,128)(2,1)S(1)} %bitcast.122, bf16[2,352,2048]{2,1,0:T(8,128)(2,1)S(1)} %bitcast.123, bf16[2,352,2048]{2,1,0:T(8,128)(2,1)S(1)} %copy-done.2), custom_call_target="tpu_custom_call" | custom-call | bytes 31457280 | tf_op jit(solution)/shard_map/pallas_call | solution.py:600
  42.4 9.7 %collective-permute-done.6 = bf16[256,256]{1,0:T(8,128)(2,1)S(1)} collective-permute-done((bf16[256,256]{1,0:T(8,128)(2,1)S(1)}, bf16[256,256]{1,0:T(8,128)(2,1)S(1)}, u32[]{:S(2)}, u32[]{:S(2)}) %collective-permute-start.6) | collective-permute-done | bytes 131104 | tf_op jit(solution)/shard_map/ppermute | solution.py:688
  71.7 16.3 %collective-permute-done.9.refs_16_ = bf16[256,1792]{1,0:T(8,128)(2,1)S(1)} collective-permute-done((bf16[256,1792]{1,0:T(8,128)(2,1)S(1)}, bf16[256,1792]{1,0:T(8,128)(2,1)S(1)}, u32[]{:S(2)}, u32[]{:S(2)}) %collective-permute-start.9) | collective-permute-done | bytes 917536 | tf_op jit(solution)/shard_map/ppermute | solution.py:688
  106.2 11.8 %collective-permute-done.13 = bf16[128,2176]{1,0:T(8,128)(2,1)S(1)} collective-permute-done((bf16[128,2176]{1,0:T(8,128)(2,1)S(1)}, bf16[128,2176]{1,0:T(8,128)(2,1)S(1)}, u32[]{:S(2)}, u32[]{:S(2)}) %collective-permute-start.13) | collective-permute-done | bytes 557088 | tf_op jit(solution)/shard_map/ppermute | solution.py:688
  124.7 14.5 %collective-permute-done.19 = bf16[128,2176]{1,0:T(8,128)(2,1)S(1)} collective-permute-done((bf16[128,2176]{1,0:T(8,128)(2,1)}, bf16[128,2176]{1,0:T(8,128)(2,1)S(1)}, u32[]{:S(2)}, u32[]{:S(2)}) %collective-permute-start.19) | collective-permute-done | bytes 557088 | tf_op jit(solution)/shard_map/ppermute | solution.py:688
  153.0 21.4 %shard_map.299 = (bf16[256,2048]{1,0:T(8,128)(2,1)}, bf16[256,2048]{1,0:T(8,128)(2,1)}, bf16[512,2048]{1,0:T(8,128)(2,1)}, bf16[512,768]{1,0:T(8,128)(2,1)}, bf1...) custom-call(s32[12]{0:T(128)} %stack.146.refs_0_.places_ref, ...), custom_call_target="tpu_custom_call" | custom-call | flops 6000000000 | bytes 25165824 | tf_op jit(solution)/shard_map/pallas_call | solution.py:290
  195.0 11.5 %shard_map.301.refs_6_.refs_7_.refs_8_ = bf16[3,1792,2048]{2,1,0:T(8,128)(2,1)} custom-call(bf16[3,768,2048]{2,1,0:T(8,128)(2,1)} %collective-permute-done.12.other_ref, bf16[3,256,2048]{2,1,0:T(8,128)(2,1)S(1)} %pad_maximum_fusion.shared_ref, bf16[3,1792,2048]{2,1,0:T(8,128)(2,1)} %get-tuple-element.235._), custom_call_target="tpu_custom_call", output_to_operand_aliasing={{}: (2, {})} | custom-call | bytes 23068672 | tf_op jit(solution)/shard_map/pallas_call | solution.py:625
  210.8 12.4 %collective-permute-done.29 = bf16[128,2048]{1,0:T(8,128)(2,1)S(1)} collective-permute-done((bf16[128,2048]{1,0:T(8,128)(2,1)S(1)}, bf16[128,2048]{1,0:T(8,128)(2,1)S(1)}, u32[]{:S(2)}, u32[]{:S(2)}) %collective-permute-start.29) | collective-permute-done | bytes 524320 | tf_op jit(solution)/shard_map/ppermute | solution.py:688
  224.5 9.9 %collective-permute-done.33 = bf16[128,2048]{1,0:T(8,128)(2,1)S(1)} collective-permute-done((bf16[128,2048]{1,0:T(8,128)(2,1)S(1)}, bf16[128,2048]{1,0:T(8,128)(2,1)S(1)}, u32[]{:S(2)}, u32[]{:S(2)}) %collective-permute-start.33) | collective-permute-done | bytes 524320 | tf_op jit(solution)/shard_map/ppermute | solution.py:688
  241.9 10.7 %collective-permute-done.35 = bf16[128,2048]{1,0:T(8,128)(2,1)S(1)} collective-permute-done((bf16[128,2048]{1,0:T(8,128)(2,1)}, bf16[128,2048]{1,0:T(8,128)(2,1)S(1)}, u32[]{:S(2)}, u32[]{:S(2)}) %collective-permute-start.35) | collective-permute-done | bytes 524320 | tf_op jit(solution)/shard_map/ppermute | solution.py:688
  261.6 36.1 %shard_map.302 = (bf16[256,2176]{1,0:T(8,128)(2,1)}, bf16[256,2176]{1,0:T(8,128)(2,1)}, bf16[256,2048]{1,0:T(8,128)(2,1)}, bf16[256,2048]{1,0:T(8,128)(2,1)}, bf...) custom-call(s32[1]{0:T(128)} %bitcast.39.refs_0_, ...), custom_call_target="tpu_custom_call" | custom-call | flops 22548578304 | bytes 30408704 | tf_op jit(solution)/shard_map/pallas_call | solution.py:470
  303.0 35.7 %shard_map.303 = (bf16[256,2176]{1,0:T(8,128)(2,1)}, bf16[256,2176]{1,0:T(8,128)(2,1)}, bf16[256,2048]{1,0:T(8,128)(2,1)}, bf16[256,2048]{1,0:T(8,128)(2,1)}, bf...) custom-call(s32[1]{0:T(128)} %bitcast.39.refs_0_, ...), custom_call_target="tpu_custom_call", output_to_operand_aliasing={{4}: (9, {}), {5}: (10, {}), {6}: (11, {})} | custom-call | flops 22548578304 | bytes 30408704 | tf_op jit(solution)/shard_map/pallas_call | solution.py:470
  346.9 35.7 %shard_map.304 = (bf16[256,2176]{1,0:T(8,128)(2,1)}, bf16[256,2176]{1,0:T(8,128)(2,1)}, bf16[256,2048]{1,0:T(8,128)(2,1)}, bf16[256,2048]{1,0:T(8,128)(2,1)}, bf...) custom-call(s32[1]{0:T(128)} %bitcast.39.refs_0_, ...), custom_call_target="tpu_custom_call", output_to_operand_aliasing={{4}: (9, {}), {5}: (10, {}), {6}: (11, {})} | custom-call | flops 22548578304 | bytes 30408704 | tf_op jit(solution)/shard_map/pallas_call | solution.py:470
  389.6 35.8 %shard_map.305 = (bf16[256,2176]{1,0:T(8,128)(2,1)}, bf16[256,2176]{1,0:T(8,128)(2,1)}, bf16[256,2048]{1,0:T(8,128)(2,1)}, bf16[256,2048]{1,0:T(8,128)(2,1)}, bf...) custom-call(s32[1]{0:T(128)} %bitcast.39.refs_0_, ...), custom_call_target="tpu_custom_call", output_to_operand_aliasing={{4}: (9, {}), {5}: (10, {}), {6}: (11, {})} | custom-call | flops 22548578304 | bytes 30408704 | tf_op jit(solution)/shard_map/pallas_call | solution.py:470
  432.4 15.7 %shard_map.306 = bf16[1024,2048]{1,0:T(8,128)(2,1)} custom-call(bf16[2048,1792]{1,0:T(8,128)(2,1)} %bitcast.124, bf16[2048,1792]{1,0:T(8,128)(2,1)} %bitcast.125, bf16[2048,1792]{1,0:T(8,128)(2,1)} %bitcast.126, bf16[2048,1792]{1,0:T(8,128)(2,1)} %bitcast.127, bf16[256,2048]{1,0:T(8,128)(2,1)} %copy-done.11, ...), custom_call_target="tpu_custom_call" | custom-call | flops 8589934592 | bytes 20971520 | tf_op jit(solution)/shard_map/pallas_call | solution.py:553
  450.6 11.9 %collective-permute-start.61 = (bf16[1024,2048]{1,0:T(8,128)(2,1)}, bf16[1024,2048]{1,0:T(8,128)(2,1)S(1)}, u32[]{:S(2)}, u32[]{:S(2)}) collective-permute-start(bf16[1024,2048]{1,0:T(8,128)(2,1)} %shard_map.306), channel_id=1, source_target_pairs={{0,1},{1,0},{2,3},{3,2},{4,5},{5,4},{6,7},{7,6},{8,9},{9,8},{10,11... | collective-permute-start | bytes 12582920 | tf_op jit(solution)/shard_map/ppermute | solution.py:688
  467.5 15.6 %shard_map.307 = bf16[1024,2048]{1,0:T(8,128)(2,1)} custom-call(bf16[2048,1792]{1,0:T(8,128)(2,1)} %bitcast.131, bf16[2048,1792]{1,0:T(8,128)(2,1)} %bitcast.132, bf16[2048,1792]{1,0:T(8,128)(2,1)} %bitcast.133, bf16[2048,1792]{1,0:T(8,128)(2,1)} %bitcast.134, bf16[256,2048]{1,0:T(8,128)(2,1)} %copy-done.11, ...), custom_call_target="tpu_custom_call" | custom-call | flops 8589934592 | bytes 20971520 | tf_op jit(solution)/shard_map/pallas_call | solution.py:553
  494.2 15.5 %shard_map.308 = bf16[1024,2048]{1,0:T(8,128)(2,1)} custom-call(bf16[2048,1792]{1,0:T(8,128)(2,1)} %bitcast.138, bf16[2048,1792]{1,0:T(8,128)(2,1)} %bitcast.139, bf16[2048,1792]{1,0:T(8,128)(2,1)} %bitcast.140, bf16[2048,1792]{1,0:T(8,128)(2,1)} %bitcast.141, bf16[256,2176]{1,0:T(8,128)(2,1)} %pad_maximum_fusion.2.refs_3_.refs_4_, ...), custom_call_target="tpu_custom_call" | custom-call | flops 8589934592 | bytes 20971520 | tf_op jit(solution)/shard_map/pallas_call | solution.py:553
  563.4 29.0 %shard_map.310 = (bf16[256,1024]{1,0:T(8,128)(2,1)}, bf16[256,1024]{1,0:T(8,128)(2,1)}, bf16[256,1024]{1,0:T(8,128)(2,1)}, bf16[256,1024]{1,0:T(8,128)(2,1)}, bf...) custom-call(s32[12]{0:T(128)} %stack.146.refs_0_.places_ref, ...), custom_call_target="tpu_custom_call" | custom-call | flops 12000000000 | bytes 25165824 | tf_op jit(solution)/shard_map/pallas_call | solution.py:290
  602.7 14.5 %shard_map.311 = f32[2,352,2048]{2,1,0:T(8,128)} custom-call(bf16[2048,1792]{1,0:T(8,128)(2,1)} %bitcast.128, bf16[2048,1792]{1,0:T(8,128)(2,1)} %bitcast.129, bf16[2048,1792]{1,0:T(8,128)(2,1)} %bitcast.130, bf16[256,2048]{1,0:T(8,128)(2,1)} %copy-done.11, bf16[256,2048]{1,0:T(8,128)(2,1)} %collective-permute-done.36.refs_2_.refs_5_.refs_4_, ...), custom_call_target="tpu_custom_call" | custom-call | flops 6442450944 | bytes 20971520 | tf_op jit(solution)/shard_map/pallas_call | solution.py:553
  631.9 14.5 %shard_map.312 = f32[2,352,2048]{2,1,0:T(8,128)} custom-call(bf16[2048,1792]{1,0:T(8,128)(2,1)} %bitcast.135, bf16[2048,1792]{1,0:T(8,128)(2,1)} %bitcast.136, bf16[2048,1792]{1,0:T(8,128)(2,1)} %bitcast.137, bf16[256,2048]{1,0:T(8,128)(2,1)} %copy-done.11, bf16[256,2048]{1,0:T(8,128)(2,1)} %collective-permute-done.36.refs_2_.refs_5_.refs_4_, ...), custom_call_target="tpu_custom_call" | custom-call | flops 6442450944 | bytes 20971520 | tf_op jit(solution)/shard_map/pallas_call | solution.py:553
  658.1 14.4 %shard_map.313 = f32[2,352,2048]{2,1,0:T(8,128)} custom-call(bf16[2048,1792]{1,0:T(8,128)(2,1)} %bitcast.142, bf16[2048,1792]{1,0:T(8,128)(2,1)} %bitcast.143, bf16[2048,1792]{1,0:T(8,128)(2,1)} %bitcast.144, bf16[256,2176]{1,0:T(8,128)(2,1)} %pad_maximum_fusion.2.refs_3_.refs_4_, bf16[256,2176]{1,0:T(8,128)(2,1)} %collective-permute-done.23.refs_4_.refs_5_, ...), custom_call_target="tpu_custom_call" | custom-call | flops 6442450944 | bytes 20971520 | tf_op jit(solution)/shard_map/pallas_call | solution.py:553
  688.4 14.4 %collective-permute-done.93 = bf16[256,512]{1,0:T(8,128)(2,1)S(1)} collective-permute-done((bf16[256,512]{1,0:T(8,128)(2,1)S(1)}, bf16[256,512]{1,0:T(8,128)(2,1)S(1)}, u32[]{:S(2)}, u32[]{:S(2)}) %collective-permute-start.93) | collective-permute-done | bytes 262176 | tf_op jit(solution)/shard_map/ppermute | solution.py:688
  710.1 10.1 %collective-permute-start.95 = (bf16[2,256,128]{2,1,0:T(8,128)(2,1)S(1)}, bf16[2,256,128]{2,1,0:T(8,128)(2,1)S(1)}, u32[]{:S(2)}, u32[]{:S(2)}) collective-permute-start(bf16[2,256,128]{2,1,0:T(8,128)(2,1)S(1)} %pad_maximum_fusion.27), channel_id=1, source_target_pairs={{0,1},{1,0},{2,3},{3,2},{4,5},{5,4},{6,7},{7,6},{8,9},{9,8},{10,11... | collective-permute-start | bytes 393224 | tf_op jit(solution)/shard_map/ppermute | solution.py:688
  (640 shorter events, 295.1 us)
Async XLA Ops:
  25.2 33.5 %collective-permute-start.4 = (bf16[256,1792]{1,0:T(8,128)(2,1)}, bf16[256,1792]{1,0:T(8,128)(2,1)S(1)}, u32[]{:S(2)}, u32[]{:S(2)}) collective-permute-start(bf16[256,1792]{1,0:T(8,128)(2,1)} %concatenate.104.refs_11_), channel_id=1, source_target_pairs={{0,8},{1,9},{2,10},{3,11},{4,12},{5,13},{6,14},{7,15},{8,16},{9,17... | collective-permute-start | bytes 2752520 | tf_op jit(solution)/shard_map/ppermute | solution.py:688
  140.2 44.8 %collective-permute-start.23 = (bf16[256,2176]{1,0:T(8,128)(2,1)}, bf16[256,2176]{1,0:T(8,128)(2,1)}, u32[]{:S(2)}, u32[]{:S(2)}) collective-permute-start(bf16[256,2176]{1,0:T(8,128)(2,1)} %pad_maximum_fusion.2.refs_3_.refs_4_), channel_id=1, source_target_pairs={{0,2},{1,3},{2,0},{3,1},{4,6},{5,7},{6,4},{7,5},{8,10},{9,11},{10,... | collective-permute-start | bytes 3342344 | tf_op jit(solution)/shard_map/ppermute | solution.py:688
  141.4 43.6 %collective-permute-start.24 = (bf16[256,2176]{1,0:T(8,128)(2,1)S(1)}, bf16[256,2176]{1,0:T(8,128)(2,1)S(1)}, u32[]{:S(2)}, u32[]{:S(2)}) collective-permute-start(bf16[256,2176]{1,0:T(8,128)(2,1)S(1)} %pad_maximum_fusion.3.refs_3_.refs_6_.refs_5_), channel_id=1, source_target_pairs={{0,4},{1,5},{2,6},{3,7},{4,0},{5,1},{6,2},{7,3},{8,12},{9,13},{10,... | collective-permute-start | bytes 3342344 | tf_op jit(solution)/shard_map/ppermute | solution.py:688
  258.7 39.0 %collective-permute-start.38 = (bf16[128,2048]{1,0:T(8,128)(2,1)S(1)}, bf16[128,2048]{1,0:T(8,128)(2,1)S(1)}, u32[]{:S(2)}, u32[]{:S(2)}) collective-permute-start(bf16[128,2048]{1,0:T(8,128)(2,1)S(1)} %bitcast.158), channel_id=1, source_target_pairs={{0,4},{1,5},{2,6},{3,7},{4,0},{5,1},{6,2},{7,3},{8,12},{9,13},{10,... | collective-permute-start | bytes 1572872 | tf_op jit(solution)/shard_map/ppermute | solution.py:688
  259.9 38.9 %collective-permute-start.39 = (bf16[128,2048]{1,0:T(8,128)(2,1)}, bf16[128,2048]{1,0:T(8,128)(2,1)S(1)}, u32[]{:S(2)}, u32[]{:S(2)}) collective-permute-start(bf16[128,2048]{1,0:T(8,128)(2,1)} %bitcast.52), channel_id=1, source_target_pairs={{0,2},{1,3},{2,0},{3,1},{4,6},{5,7},{6,4},{7,5},{8,10},{9,11},{10,... | collective-permute-start | bytes 1572872 | tf_op jit(solution)/shard_map/ppermute | solution.py:688
  260.7 39.6 %collective-permute-start.40 = (bf16[256,2176]{1,0:T(8,128)(2,1)S(1)}, bf16[256,2176]{1,0:T(8,128)(2,1)S(1)}, u32[]{:S(2)}, u32[]{:S(2)}) collective-permute-start(bf16[256,2176]{1,0:T(8,128)(2,1)S(1)} %pad_maximum_fusion.4.refs_3_.refs_8_.refs_7_), channel_id=1, source_target_pairs={{0,2},{1,3},{2,0},{3,1},{4,6},{5,7},{6,4},{7,5},{8,10},{9,11},{10,... | collective-permute-start | bytes 3342344 | tf_op jit(solution)/shard_map/ppermute | solution.py:688
  261.4 39.0 %collective-permute-start.41 = (bf16[256,2176]{1,0:T(8,128)(2,1)S(1)}, bf16[256,2176]{1,0:T(8,128)(2,1)}, u32[]{:S(2)}, u32[]{:S(2)}) collective-permute-start(bf16[256,2176]{1,0:T(8,128)(2,1)S(1)} %pad_maximum_fusion.5.refs_3_.refs_10_.refs_9_), channel_id=1, source_target_pairs={{0,4},{1,5},{2,6},{3,7},{4,0},{5,1},{6,2},{7,3},{8,12},{9,13},{10,... | collective-permute-start | bytes 3342344 | tf_op jit(solution)/shard_map/ppermute | solution.py:688
  300.4 43.7 %collective-permute-start.43 = (bf16[256,2176]{1,0:T(8,128)(2,1)}, bf16[256,2176]{1,0:T(8,128)(2,1)S(1)}, u32[]{:S(2)}, u32[]{:S(2)}) collective-permute-start(bf16[256,2176]{1,0:T(8,128)(2,1)} %get-tuple-element.262), channel_id=1, source_target_pairs={{0,24},{1,25},{2,26},{3,27},{4,28},{5,29},{6,30},{7,31},{8,0},{9,1... | collective-permute-start | bytes 3342344 | tf_op jit(solution)/shard_map/ppermute | solution.py:688
  300.5 40.8 %collective-permute-start.42 = (bf16[256,2048]{1,0:T(8,128)(2,1)}, bf16[256,2048]{1,0:T(8,128)(2,1)}, u32[]{:S(2)}, u32[]{:S(2)}) collective-permute-start(bf16[256,2048]{1,0:T(8,128)(2,1)} %get-tuple-element.258), channel_id=1, source_target_pairs={{0,24},{1,25},{2,26},{3,27},{4,28},{5,29},{6,30},{7,31},{8,0},{9,1... | collective-permute-start | bytes 3145736 | tf_op jit(solution)/shard_map/ppermute | solution.py:688
  301.6 42.8 %collective-permute-start.44 = (bf16[256,2048]{1,0:T(8,128)(2,1)S(1)}, bf16[256,2048]{1,0:T(8,128)(2,1)S(1)}, u32[]{:S(2)}, u32[]{:S(2)}) collective-permute-start(bf16[256,2048]{1,0:T(8,128)(2,1)S(1)} %pad_maximum_fusion.10.refs_1_.refs_8_.refs_7_), channel_id=1, source_target_pairs={{0,2},{1,3},{2,0},{3,1},{4,6},{5,7},{6,4},{7,5},{8,10},{9,11},{10,... | collective-permute-start | bytes 3145736 | tf_op jit(solution)/shard_map/ppermute | solution.py:688
  302.2 42.2 %collective-permute-start.45 = (bf16[256,2048]{1,0:T(8,128)(2,1)S(1)}, bf16[256,2048]{1,0:T(8,128)(2,1)S(1)}, u32[]{:S(2)}, u32[]{:S(2)}) collective-permute-start(bf16[256,2048]{1,0:T(8,128)(2,1)S(1)} %pad_maximum_fusion.11.refs_1_.refs_10_.refs_9_), channel_id=1, source_target_pairs={{0,4},{1,5},{2,6},{3,7},{4,0},{5,1},{6,2},{7,3},{8,12},{9,13},{10,... | collective-permute-start | bytes 3145736 | tf_op jit(solution)/shard_map/ppermute | solution.py:688
  344.5 39.3 %collective-permute-start.47 = (bf16[256,2176]{1,0:T(8,128)(2,1)}, bf16[256,2176]{1,0:T(8,128)(2,1)S(1)}, u32[]{:S(2)}, u32[]{:S(2)}) collective-permute-start(bf16[256,2176]{1,0:T(8,128)(2,1)} %get-tuple-element.272), channel_id=1, source_target_pairs={{0,24},{1,25},{2,26},{3,27},{4,28},{5,29},{6,30},{7,31},{8,0},{9,1... | collective-permute-start | bytes 3342344 | tf_op jit(solution)/shard_map/ppermute | solution.py:688
  345.5 38.1 %collective-permute-start.48 = (bf16[128,2176]{1,0:T(8,128)(2,1)S(1)}, bf16[128,2176]{1,0:T(8,128)(2,1)S(1)}, u32[]{:S(2)}, u32[]{:S(2)}) collective-permute-start(bf16[128,2176]{1,0:T(8,128)(2,1)S(1)} %slice.545), channel_id=1, source_target_pairs={{0,2},{1,3},{2,0},{3,1},{4,6},{5,7},{6,4},{7,5},{8,10},{9,11},{10,... | collective-permute-start | bytes 1671176 | tf_op jit(solution)/shard_map/ppermute | solution.py:688
  346.3 36.4 %collective-permute-start.46 = (bf16[128,2048]{1,0:T(8,128)(2,1)}, bf16[128,2048]{1,0:T(8,128)(2,1)S(1)}, u32[]{:S(2)}, u32[]{:S(2)}) collective-permute-start(bf16[128,2048]{1,0:T(8,128)(2,1)} %slice.546), channel_id=1, source_target_pairs={{0,2},{1,3},{2,0},{3,1},{4,6},{5,7},{6,4},{7,5},{8,10},{9,11},{10,... | collective-permute-start | bytes 1572872 | tf_op jit(solution)/shard_map/ppermute | solution.py:688
  384.6 44.6 %collective-permute-start.51 = (bf16[256,2176]{1,0:T(8,128)(2,1)}, bf16[256,2176]{1,0:T(8,128)(2,1)S(1)}, u32[]{:S(2)}, u32[]{:S(2)}) collective-permute-start(bf16[256,2176]{1,0:T(8,128)(2,1)} %get-tuple-element.289), channel_id=1, source_target_pairs={{0,2},{1,3},{2,0},{3,1},{4,6},{5,7},{6,4},{7,5},{8,10},{9,11},{10,... | collective-permute-start | bytes 3342344 | tf_op jit(solution)/shard_map/ppermute | solution.py:688
  385.5 40.8 %collective-permute-start.52 = (bf16[256,2048]{1,0:T(8,128)(2,1)}, bf16[256,2048]{1,0:T(8,128)(2,1)}, u32[]{:S(2)}, u32[]{:S(2)}) collective-permute-start(bf16[256,2048]{1,0:T(8,128)(2,1)} %get-tuple-element.290), channel_id=1, source_target_pairs={{0,24},{1,25},{2,26},{3,27},{4,28},{5,29},{6,30},{7,31},{8,0},{9,1... | collective-permute-start | bytes 3145736 | tf_op jit(solution)/shard_map/ppermute | solution.py:688
  386.0 39.4 %collective-permute-start.53 = (bf16[128,2176]{1,0:T(8,128)(2,1)S(1)}, bf16[128,2176]{1,0:T(8,128)(2,1)S(1)}, u32[]{:S(2)}, u32[]{:S(2)}) collective-permute-start(bf16[128,2176]{1,0:T(8,128)(2,1)S(1)} %slice.548), channel_id=1, source_target_pairs={{0,4},{1,5},{2,6},{3,7},{4,0},{5,1},{6,2},{7,3},{8,12},{9,13},{10,... | collective-permute-start | bytes 1671176 | tf_op jit(solution)/shard_map/ppermute | solution.py:688
  388.1 41.4 %collective-permute-start.50 = (bf16[64,2176]{1,0:T(8,128)(2,1)S(1)}, bf16[64,2176]{1,0:T(8,128)(2,1)S(1)}, u32[]{:S(2)}, u32[]{:S(2)}) collective-permute-start(bf16[64,2176]{1,0:T(8,128)(2,1)S(1)} %slice.550), channel_id=1, source_target_pairs={{0,4},{1,5},{2,6},{3,7},{4,0},{5,1},{6,2},{7,3},{8,12},{9,13},{10,... | collective-permute-start | bytes 835592 | tf_op jit(solution)/shard_map/ppermute | solution.py:688
  388.2 41.3 %collective-permute-start.49 = (bf16[64,2048]{1,0:T(8,128)(2,1)}, bf16[64,2048]{1,0:T(8,128)(2,1)S(1)}, u32[]{:S(2)}, u32[]{:S(2)}) collective-permute-start(bf16[64,2048]{1,0:T(8,128)(2,1)} %slice.551), channel_id=1, source_target_pairs={{0,4},{1,5},{2,6},{3,7},{4,0},{5,1},{6,2},{7,3},{8,12},{9,13},{10,... | collective-permute-start | bytes 786440 | tf_op jit(solution)/shard_map/ppermute | solution.py:688
  450.6 35.5 %collective-permute-start.61 = (bf16[1024,2048]{1,0:T(8,128)(2,1)}, bf16[1024,2048]{1,0:T(8,128)(2,1)S(1)}, u32[]{:S(2)}, u32[]{:S(2)}) collective-permute-start(bf16[1024,2048]{1,0:T(8,128)(2,1)} %shard_map.306), channel_id=1, source_target_pairs={{0,1},{1,0},{2,3},{3,2},{4,5},{5,4},{6,7},{7,6},{8,9},{9,8},{10,11... | collective-permute-start | bytes 12582920 | tf_op jit(solution)/shard_map/ppermute | solution.py:688
  545.7 50.6 %all-to-all-start = ((bf16[8,264,256]{2,1,0:T(8,128)(2,1)}), bf16[8,264,256]{2,1,0:T(8,128)(2,1)S(1)}, u32[]{:S(2)}, u32[]{:S(2)}) async-start(bf16[8,264,256]{2,1,0:T(8,128)(2,1)} %maximum_bitcast_fusion), calls=%async_computation | async-start | bytes 2162688 | tf_op jit(solution)/shard_map/all_to_all | solution.py:1061
  557.0 37.1 %collective-permute-start.74 = (bf16[128,2048]{1,0:T(8,128)(2,1)}, bf16[128,2048]{1,0:T(8,128)(2,1)}, u32[]{:S(2)}, u32[]{:S(2)}) collective-permute-start(bf16[128,2048]{1,0:T(8,128)(2,1)} %slice.568), channel_id=1, source_target_pairs={{0,2},{1,3},{2,0},{3,1},{4,6},{5,7},{6,4},{7,5},{8,10},{9,11},{10,... | collective-permute-start | bytes 1572872 | tf_op jit(solution)/shard_map/ppermute | solution.py:688
  557.8 39.9 %collective-permute-start.75 = (bf16[1024,512]{1,0:T(8,128)(2,1)}, bf16[1024,512]{1,0:T(8,128)(2,1)}, u32[]{:S(2)}, u32[]{:S(2)}) collective-permute-start(bf16[1024,512]{1,0:T(8,128)(2,1)} %get-tuple-element.326), channel_id=1, source_target_pairs={{0,4},{1,5},{2,6},{3,7},{4,0},{5,1},{6,2},{7,3},{8,12},{9,13},{10,... | collective-permute-start | bytes 3145736 | tf_op jit(solution)/shard_map/ppermute | solution.py:688
  559.2 38.5 %collective-permute-start.73 = (bf16[64,2048]{1,0:T(8,128)(2,1)S(1)}, bf16[64,2048]{1,0:T(8,128)(2,1)}, u32[]{:S(2)}, u32[]{:S(2)}) collective-permute-start(bf16[64,2048]{1,0:T(8,128)(2,1)S(1)} %slice.570), channel_id=1, source_target_pairs={{0,2},{1,3},{2,0},{3,1},{4,6},{5,7},{6,4},{7,5},{8,10},{9,11},{10,... | collective-permute-start | bytes 786440 | tf_op jit(solution)/shard_map/ppermute | solution.py:688
  (197 other events, 2746.3 us)
